TPU v7x, 32 devices: a whole 2x2x4 slice. The times are simulated.
32 devices in a mesh: groups: 2 (over x), tp: 16 (over z, y, core).
Axes of the slice: x: 2, y: 2, z: 4, core: 2. Of those that a mesh axis runs over, the one named last changes fastest.
Arguments:
- queries: bfloat16 [512, 8192], P('groups', 'tp'), parts along dimension 0, may hold values from -200 to 200, as said below
- cache: bfloat16 [16, 16384, 256], P('tp', 'groups'), parts along dimension 1, may hold values from -8 to 8, as said below
- offset: int32 [2], P('groups'), parts along dimension 0, may hold values from 4096 to 7936
- out_weight: bfloat16 [8192, 16384], P('tp'), may hold values from -3 to 3
- residual: bfloat16 [512, 16384], P(('groups', 'tp')), parts along dimension 0, may hold values from -60 to 60
- term_exp: int32 [16, 512, 128], P('tp', 'groups'), parts along dimension 1, may hold values from -13 to -7
- code_exp: int32 [512, 128], P('groups'), parts along dimension 0, may hold values from -9 to -4
- gain: float32 [16384], replicated, may hold values from 0.1 to 1.9
Outputs:
- mixed: bfloat16 [512, 16384], P('groups'), parts along dimension 0
- stream: bfloat16 [512, 16384], P(('groups', 'tp')), parts along dimension 0
There are 2 independent parts, one for each index of `groups`. A program takes and returns all parts, laid end to end along the dimension named above; an argument that names none is the same for every part. Nothing has to cross between parts.
Inputs may be any that keep to these rules, and one draw needn't show every extreme that they name: `queries`: mostly values of about unit size, with possibly a few much larger entries. `cache`: copies for the devices of one key and value head are equal.
All inputs are finite; a program needn't handle non-finite values.
Results may differ from a plain program's by a relative error of at most 0.0095.
Values may be sent and summed in bfloat16 or wider, within the bound.
No kernel may reach another device: no remote copies, remote signals or barrier semaphores. Data moves between devices by JAX's collectives and lax.ppermute only.
A program may use at most 256 MiB of HBM per device.

v0:
```python
import jax
import jax.numpy as jnp
from jax import lax
from jax.sharding import PartitionSpec as P


def powers(exps):
    magnitude = jnp.abs(exps)
    result = jnp.ones(exps.shape, jnp.float32)
    for bit in range(6):
        chosen = magnitude // 2**bit % 2 == 1
        result = result * jnp.where(chosen, jnp.float32(2.0**2**bit), jnp.float32(1.0))
    return jnp.where(exps < 0, 1.0 / result, result)


def encode(values, exps):
    rows, cols = values.shape
    blocks = exps.shape[1]
    scale = powers(exps)[:, :, None]
    shaped = values.reshape(rows, blocks, cols // blocks) / scale
    return jnp.clip(shaped, -448.0, 448.0).astype(jnp.bfloat16).reshape(rows, cols)


def decode(codes, exps):
    rows, cols = codes.shape
    blocks = exps.shape[1]
    scale = powers(exps)[:, :, None]
    return (codes.astype(jnp.float32).reshape(rows, blocks, cols // blocks) * scale).reshape(
        rows, cols
    )


def restored(values, exps):
    codes = lax.optimization_barrier(encode(values, exps))
    return decode(codes, exps)


def attend(query_rows, key_values, start):
    rows = query_rows.shape[0]
    head = key_values.shape[1] // 2
    heads = query_rows.shape[1] // head
    stacked = query_rows.reshape(rows, heads, head).transpose(1, 0, 2)
    keys = key_values[:, :head]
    values = key_values[:, head:]
    query_pos = start + jnp.arange(rows)
    key_pos = jnp.arange(keys.shape[0])
    seen = key_pos[None, :] <= query_pos[:, None]

    def one_head(single):
        scores = lax.dot_general(
            single, keys, (((1,), (1,)), ((), ())), preferred_element_type=jnp.float32
        )
        scores = scores * head ** (-0.5)
        scores = jnp.where(seen, scores, jnp.float32(-1e30))
        top = jnp.max(scores, axis=1, keepdims=True)
        weights = jnp.exp(scores - top)
        probs = (weights / jnp.sum(weights, axis=1, keepdims=True)).astype(jnp.bfloat16)
        return jnp.dot(probs, values, preferred_element_type=jnp.float32).astype(jnp.bfloat16)

    mixed = lax.map(one_head, stacked)
    return mixed.transpose(1, 0, 2).reshape(rows, heads * head)


def per_device(queries, cache, offset, out_weight, residual, term_exp, code_exp, gain):
    attn = attend(queries, cache[0], offset[0])
    exps = term_exp[0]
    width = residual.shape[1]
    blocks = code_exp.shape[1]
    position = lax.axis_index("tp")
    parts = lax.axis_size("tp")
    cols = width // parts
    resid_cols = lax.all_to_all(residual, "tp", split_axis=1, concat_axis=0, tiled=True)
    partial_out = jnp.dot(attn, out_weight, preferred_element_type=jnp.float32)
    summed = lax.psum_scatter(
        restored(partial_out, exps).astype(jnp.bfloat16), "tp", scatter_dimension=1, tiled=True
    ).astype(jnp.float32)
    stream_cols = (summed + resid_cols.astype(jnp.float32)).astype(jnp.bfloat16)
    wide = stream_cols.astype(jnp.float32)
    squares = lax.psum(jnp.sum(wide * wide, axis=1), "tp")
    inverse = lax.rsqrt(squares / width + 1e-05)
    gain_cols = lax.dynamic_slice_in_dim(gain, position * cols, cols, 0)
    normed = wide * inverse[:, None] * gain_cols[None, :]
    exp_cols = lax.dynamic_slice_in_dim(code_exp, position * (blocks // parts), blocks // parts, 1)
    codes = encode(normed, exp_cols)
    gathered = lax.all_gather(codes, "tp", axis=1, tiled=True)
    stream = lax.all_to_all(stream_cols, "tp", split_axis=0, concat_axis=1, tiled=True)
    gathered = lax.optimization_barrier(gathered)
    mixed = decode(gathered, code_exp).astype(jnp.bfloat16)
    return (mixed, stream)


def solution(mesh):
    in_specs = (
        P("groups", "tp"),
        P("tp", "groups", None),
        P("groups"),
        P("tp", None),
        P(("groups", "tp"), None),
        P("tp", "groups", None),
        P("groups", None),
        P(),
    )
    out_specs = (P("groups", None), P(("groups", "tp"), None))
    return jax.shard_map(
        per_device, mesh=mesh, in_specs=in_specs, out_specs=out_specs, check_vma=False
    )
```

profile of v0, /device:TPU:0, one launch (start us, length us, event | category | flops | bytes accessed | tf_op | source)
XLA Modules:
  0.0 371.6 jit_solution(16705866179643566734)
XLA Ops:
  7.2 3.8 %fusion.80 = (bf16[8192,128]{1,0:T(8,128)(2,1)S(1)}, bf16[8192,128]{1,0:T(8,128)(2,1)}) fusion(bf16[8192,256]{1,0:T(8,128)(2,1)} %bitcast.89), kind=kLoop, calls=%fused_computation.195 | loop fusion | bytes 8388608 | tf_op jit(solution)/shard_map/slice | solution.py:44
  11.9 29.4 %while.11 = (s32[]{:T(128)}, bf16[4,256,128]{1,2,0:T(8,128)(2,1)S(1)}, bf16[4,256,128]{1,2,0:T(8,128)(2,1)S(1)}, bf16[8192,128]{1,0:T(8,128)(2,1)}, bf16[8192,12...) while((s32[]{:T(128)}, bf16[4,256,128]{1,2,0:T(8,128)(2,1)S(1)}, ...), condition=%wide.region_3.4_spmd.clone, body=%wide.region_0.3_spmd.clone.sunk | while | flops 1092648448 | bytes 29759572 | solution.py:60
  11.9 3.9 %fusion.92 = (f32[256]{0:T(256)S(1)}, f32[256,8192]{1,0:T(8,128)S(1)}) fusion(bf16[8192,128]{1,0:T(8,128)(2,1)} %get-tuple-element.144, bf16[4,256,128]{1,2,0:T(8,128)(2,1)S(1)} %get-tuple-element.143, s32[]{:T(128)} %get-tuple-element.134, s32[256]{0:T(256)S(1)} %get-tuple-element.146), kind=kOutput, calls=%fused_computation.194.clone.1 | convolution fusion | flops 545259264 | bytes 10553348 | tf_op jit(solution)/shard_map/while/body/eval_jaxpr/dot_general | solution.py:50
  19.3 3.9 %fusion.92 = (f32[256]{0:T(256)S(1)}, f32[256,8192]{1,0:T(8,128)S(1)}) fusion(bf16[8192,128]{1,0:T(8,128)(2,1)} %get-tuple-element.144, bf16[4,256,128]{1,2,0:T(8,128)(2,1)S(1)} %get-tuple-element.143, s32[]{:T(128)} %get-tuple-element.134, s32[256]{0:T(256)S(1)} %get-tuple-element.146), kind=kOutput, calls=%fused_computation.194.clone.1 | convolution fusion | flops 545259264 | bytes 10553348 | tf_op jit(solution)/shard_map/while/body/eval_jaxpr/dot_general | solution.py:50
  26.6 3.9 %fusion.92 = (f32[256]{0:T(256)S(1)}, f32[256,8192]{1,0:T(8,128)S(1)}) fusion(bf16[8192,128]{1,0:T(8,128)(2,1)} %get-tuple-element.144, bf16[4,256,128]{1,2,0:T(8,128)(2,1)S(1)} %get-tuple-element.143, s32[]{:T(128)} %get-tuple-element.134, s32[256]{0:T(256)S(1)} %get-tuple-element.146), kind=kOutput, calls=%fused_computation.194.clone.1 | convolution fusion | flops 545259264 | bytes 10553348 | tf_op jit(solution)/shard_map/while/body/eval_jaxpr/dot_general | solution.py:50
  31.8 1.9 fusion.94
  33.9 3.9 %fusion.92 = (f32[256]{0:T(256)S(1)}, f32[256,8192]{1,0:T(8,128)S(1)}) fusion(bf16[8192,128]{1,0:T(8,128)(2,1)} %get-tuple-element.144, bf16[4,256,128]{1,2,0:T(8,128)(2,1)S(1)} %get-tuple-element.143, s32[]{:T(128)} %get-tuple-element.134, s32[256]{0:T(256)S(1)} %get-tuple-element.146), kind=kOutput, calls=%fused_computation.194.clone.1 | convolution fusion | flops 545259264 | bytes 10553348 | tf_op jit(solution)/shard_map/while/body/eval_jaxpr/dot_general | solution.py:50
  42.0 22.4 %copy.47 = bf16[16384,512]{1,0:T(8,128)(2,1)} copy(bf16[16384,512]{0,1:T(8,128)(2,1)} %bitcast.86) | data formatting | bytes 33554432 | tf_op jit(solution)/shard_map/dot_general | solution.py:73
  64.5 10.1 %clamp_convert_fusion = bf16[256,128,128]{0,2,1:T(8,128)(2,1)} fusion(bf16[256,512,1]{0,1,2:T(8,128)(2,1)S(1)} %bitcast.95, bf16[128,128,512]{2,1,0:T(8,128)(2,1)} %bitcast.87, f32[256,128]{0,1:T(8,128)S(1)} %copy.40), kind=kOutput, calls=%fused_computation.17 | convolution fusion | flops 4307550208 | bytes 25559040 | tf_op jit(solution)/shard_map/dot_general | solution.py:73
  74.6 12.0 %copy.41 = bf16[256,16384]{1,0:T(8,128)(2,1)} copy(bf16[256,16384]{0,1:T(8,128)(2,1)} %bitcast.88) | data formatting | bytes 16777216 | tf_op jit(solution)/shard_map/optimization_barrier | solution.py:34
  86.6 7.0 %div.220 = f32[256,128,128]{0,2,1:T(8,128)} broadcast(f32[256,128]{0,1:T(8,128)S(1)} %copy.40), dimensions={0,1} | broadcast | bytes 16908288 | tf_op jit(solution)/shard_map/div | solution.py:20
  93.6 17.4 %copy.42 = f32[256,16384]{1,0:T(8,128)} copy(f32[256,16384]{0,1:T(8,128)} %bitcast.85) | data formatting | bytes 33554432 | tf_op jit(solution)/shard_map/div | solution.py:20
  111.0 12.2 %multiply_convert_fusion = bf16[256,16384]{1,0:T(8,128)(2,1)} fusion(f32[256,16384]{1,0:T(8,128)} %copy.42, bf16[256,16384]{1,0:T(8,128)(2,1)} %copy.41), kind=kLoop, calls=%fused_computation.16 | loop fusion | flops 12582912 | bytes 33554432 | tf_op jit(solution)/shard_map/convert_element_type | solution.py:75
  125.1 7.4 %all-to-all-start = ((bf16[16,16,1024]{2,0,1:T(8,128)(2,1)}), bf16[16,16,1024]{2,0,1:T(8,128)(2,1)S(1)}, u32[]{:S(2)}, u32[]{:S(2)}) async-start(bf16[16,16,1024]{2,0,1:T(8,128)(2,1)} %bitcast.74), calls=%async_computation.1 | async-start | bytes 1048576 | tf_op jit(solution)/shard_map/all_to_all | solution.py:72
  134.0 13.0 %all-to-all-done = bf16[16,16,1024]{2,0,1:T(8,128)(2,1)S(1)} async-done(((bf16[16,16,1024]{2,0,1:T(8,128)(2,1)}), bf16[16,16,1024]{2,0,1:T(8,128)(2,1)S(1)}, u32[]{:S(2)}, u32[]{:S(2)}) %all-to-all-start) | async-done | bytes 524320 | tf_op jit(solution)/shard_map/all_to_all | solution.py:72
  147.0 84.0 %reduce-scatter.2.cloned.1.call-done = bf16[256,1024]{1,0:T(8,128)(2,1)} async-done(((bf16[256,16384]{1,0:T(8,128)(2,1)}), bf16[256,1024]{1,0:T(8,128)(2,1)}) %reduce-scatter.2.cloned.1.call-update) | async-done | bytes 524304 | tf_op jit(solution)/shard_map/reduce_scatter | solution.py:74
  230.9 2.0 fusion.11
  232.9 32.2 %psum.7 = f32[256]{0:T(256)S(1)} all-reduce(f32[256]{0:T(256)S(1)} %get-tuple-element.80), channel_id=1, replica_groups=mesh['groups'=2,'tp'=16] {'tp'}, use_global_device_ids=true, to_apply=%region_6.7 | all-reduce | flops 256 | bytes 2048 | tf_op jit(solution)/shard_map/psum | solution.py:79
  265.5 2.1 fusion.16
  267.7 3.6 all-to-all-start.1
  271.9 20.7 %all-to-all-done.1 = bf16[16,16,1024]{2,1,0:T(8,128)(2,1)S(1)} async-done(((bf16[16,16,1024]{2,1,0:T(8,128)(2,1)}), bf16[16,16,1024]{2,1,0:T(8,128)(2,1)S(1)}, u32[]{:S(2)}, u32[]{:S(2)}) %all-to-all-start.1) | async-done | bytes 524320 | tf_op jit(solution)/shard_map/all_to_all | solution.py:86
  293.4 55.5 %all-gather.2.cloned.1.call-done = bf16[256,16384]{1,0:T(8,128)(2,1)} async-done(((bf16[256,1024]{1,0:T(8,128)(2,1)}), bf16[256,16384]{1,0:T(8,128)(2,1)}) %all-gather.2.cloned.1.call-update) | async-done | bytes 8388624 | tf_op jit(solution)/shard_map/all_gather | solution.py:85
  348.9 4.6 %mul.139 = f32[256,128,128]{2,1,0:T(8,128)S(1)} broadcast(f32[256,128]{1,0:T(8,128)S(1)} %divide_select_fusion), dimensions={0,1} | broadcast | bytes 16908288 | tf_op jit(solution)/shard_map/mul | solution.py:28
  353.5 11.2 %fusion.10 = bf16[256,16384]{1,0:T(8,128)(2,1)} fusion(f32[32,8,128,128]{3,2,1,0:T(8,128)S(1)} %bitcast.84, bf16[256,16384]{1,0:T(8,128)(2,1)S(1)} %copy-done), kind=kLoop, calls=%fused_computation.15 | loop fusion | flops 12582912 | bytes 33554432 | tf_op jit(solution)/shard_map/convert_element_type | solution.py:88
  (41 shorter events, 17.8 us)
Async XLA Ops:
  7.2 3.9 %copy-start.3 = (bf16[256,512]{1,0:T(8,128)(2,1)S(1)}, bf16[256,512]{1,0:T(8,128)(2,1)}, u32[]{:S(2)}) copy-start(bf16[256,512]{1,0:T(8,128)(2,1)} %param.10) | copy-start | bytes 786436
  7.2 223.7 %reduce-scatter.2.cloned.1.call-start = ((), (), s32[]{:S(2)}) async-start(), calls=%async_computation.3 | async-start | bytes 8912896 | tf_op jit(solution)/shard_map/reduce_scatter | solution.py:74
  11.9 29.4 %copy-start.4 = (s32[1,256,128]{2,1,0:T(8,128)S(1)}, s32[1,256,128]{2,1,0:T(8,128)}, u32[]{:S(2)}) copy-start(s32[1,256,128]{2,1,0:T(8,128)} %param.15) | copy-start | bytes 393220
  123.2 1.0 copy-start.1
  123.2 10.0 %copy-start.2 = (s32[256,128]{1,0:T(8,128)S(1)}, s32[256,128]{1,0:T(8,128)}, u32[]{:S(2)}) copy-start(s32[256,128]{1,0:T(8,128)} %param.16) | copy-start | bytes 393220
  125.1 21.9 %all-to-all-start = ((bf16[16,16,1024]{2,0,1:T(8,128)(2,1)}), bf16[16,16,1024]{2,0,1:T(8,128)(2,1)S(1)}, u32[]{:S(2)}, u32[]{:S(2)}) async-start(bf16[16,16,1024]{2,0,1:T(8,128)(2,1)} %bitcast.74), calls=%async_computation.1 | async-start | bytes 1048576 | tf_op jit(solution)/shard_map/all_to_all | solution.py:72
  132.5 216.4 %all-gather.2.cloned.1.call-start = ((), (), s32[]{:S(2)}) async-start(), calls=%async_computation.4 | async-start | bytes 8912896 | tf_op jit(solution)/shard_map/all_gather | solution.py:85
  267.7 24.9 %all-to-all-start.1 = ((bf16[16,16,1024]{2,1,0:T(8,128)(2,1)}), bf16[16,16,1024]{2,1,0:T(8,128)(2,1)S(1)}, u32[]{:S(2)}, u32[]{:S(2)}) async-start(bf16[16,16,1024]{2,1,0:T(8,128)(2,1)} %bitcast.15), calls=%async_computation.2 | async-start | bytes 1048576 | tf_op jit(solution)/shard_map/all_to_all | solution.py:86
  348.9 4.6 %copy-start = (bf16[256,16384]{1,0:T(8,128)(2,1)S(1)}, bf16[256,16384]{1,0:T(8,128)(2,1)}, u32[]{:S(2)}) copy-start(bf16[256,16384]{1,0:T(8,128)(2,1)} %all-gather.2.cloned.1.call-done) | copy-start | bytes 25165828
Sparse Core Ops, SparseCore 0:
  123.4 107.5 reduce-scatter.1
  267.8 81.0 all-gather.1
where the time goes:
time: 373 us; the launch traced here: 372 us
  waiting for transfers between devices  173 us (46%)
  local copies, waits for them, and re-layouts  71.7 us (19%)
  other arithmetic  35.1 us (9%)
  matrix products  33.5 us (9%)
  blocking collectives  32.2 us (9%)
  between operations  14.8 us (4%)
  starting transfers between devices  11.1 us (3%)
    reduce_scatter x1, waiting for transfers between devices, per_device(): lax.psum_scatter(restored(partial_out, exps).astype(jnp.bfloat16), 'tp',...  84 us
    all_gather x1, waiting for transfers between devices, per_device(): gathered = lax.all_gather(codes, 'tp', axis=1, tiled=True)  55.5 us
    psum x1, blocking collectives, per_device(): squares = lax.psum(jnp.sum(wide * wide, axis=1), 'tp')  32.2 us
    div x3, local copies, waits for them, and re-layouts, encode(): shaped = values.reshape(rows, blocks, cols // blocks) / scale  24.8 us
    dot_general x1, local copies, waits for them, and re-layouts, per_device(): partial_out = jnp.dot(attn, out_weight, preferred_element_type=jnp.float32)  22.4 us
    all_to_all x1, waiting for transfers between devices, per_device(): lax.all_to_all(stream_cols, 'tp', split_axis=0, concat_axis=1, tiled=True)  20.7 us
    dot_general x4, matrix products, one_head(): lax.dot_general(single, keys, (((1,), (1,)), ((), ())), preferred_element...  15.6 us
    all_to_all x1, waiting for transfers between devices, per_device(): lax.all_to_all(residual, 'tp', split_axis=1, concat_axis=0, tiled=True)  13 us
  transfers between devices with their start and end apart: 4, of which 4 were waited for; matrix products, arithmetic and copies ran while one was open for 1% of the time, Pallas kernels for 0%

commit v1 on v0

v1 whole, which is shorter than its diff:
```python
import jax
import jax.numpy as jnp
from jax import lax
from jax.sharding import PartitionSpec as P

CHUNKS = 4


def powers(exps):
    magnitude = jnp.abs(exps)
    result = jnp.ones(exps.shape, jnp.float32)
    for bit in range(6):
        chosen = magnitude // 2**bit % 2 == 1
        result = result * jnp.where(chosen, jnp.float32(2.0**2**bit), jnp.float32(1.0))
    return jnp.where(exps < 0, 1.0 / result, result)


def attend(query_rows, key_values, start):
    rows = query_rows.shape[0]
    head = key_values.shape[1] // 2
    heads = query_rows.shape[1] // head
    stacked = query_rows.reshape(rows, heads, head).transpose(1, 0, 2)
    keys = key_values[:, :head]
    values = key_values[:, head:]
    query_pos = start + jnp.arange(rows)
    key_pos = jnp.arange(keys.shape[0])
    seen = key_pos[None, :] <= query_pos[:, None]

    def one_head(single):
        scores = lax.dot_general(
            single, keys, (((1,), (1,)), ((), ())), preferred_element_type=jnp.float32
        )
        scores = scores * head ** (-0.5)
        scores = jnp.where(seen, scores, jnp.float32(-1e30))
        top = jnp.max(scores, axis=1, keepdims=True)
        weights = jnp.exp(scores - top)
        probs = (weights / jnp.sum(weights, axis=1, keepdims=True)).astype(jnp.bfloat16)
        return jnp.dot(probs, values, preferred_element_type=jnp.float32).astype(jnp.bfloat16)

    mixed = lax.map(one_head, stacked)
    return mixed.transpose(1, 0, 2).reshape(rows, heads * head)


def to_relative(x, order, me):
    n = len(order)
    rows = x.shape[0]
    block = rows // 2**n
    shaped = x.reshape((2,) * n + (block,) + x.shape[1:])
    perm = tuple(n - 1 - b for b in order) + tuple(range(n, shaped.ndim))
    shaped = shaped.transpose(perm)
    for axis, b in enumerate(order):
        shaped = jnp.where((me >> b) & 1 == 1, jnp.flip(shaped, axis), shaped)
    return shaped.reshape(x.shape)


def from_relative(x, order, me):
    n = len(order)
    rows = x.shape[0]
    block = rows // 2**n
    shaped = x.reshape((2,) * n + (block,) + x.shape[1:])
    for axis, b in enumerate(order):
        shaped = jnp.where((me >> b) & 1 == 1, jnp.flip(shaped, axis), shaped)
    inverse = [0] * n
    for axis, b in enumerate(order):
        inverse[n - 1 - b] = axis
    shaped = shaped.transpose(tuple(inverse) + tuple(range(n, shaped.ndim)))
    return shaped.reshape(x.shape)


def per_device(queries, cache, offset, out_weight, residual, term_exp, code_exp, gain):
    me = lax.axis_index("tp")
    parts = lax.axis_size("tp")
    bits = parts.bit_length() - 1
    block = residual.shape[0]
    width = residual.shape[1]
    blocks = code_exp.shape[1]
    group = width // blocks
    cols = width // CHUNKS
    bcols = blocks // CHUNKS

    def flip(x, b):
        return lax.ppermute(x, "tp", [(i, i ^ (1 << b)) for i in range(parts)])

    order_a = list(range(bits))
    order_b = [0, 2, 1] + list(range(3, bits))
    orders = [order_b] + [order_a] * (CHUNKS - 1)

    attn = attend(queries, cache[0], offset[0])
    limit = powers(term_exp[0]) * 448.0
    attn_of = {}
    limit_of = {}
    for name, order in (("a", order_a), ("b", order_b)):
        attn_of[name] = to_relative(attn, order, me)
        limit_of[name] = to_relative(limit, order, me)

    sums = []
    for j in range(CHUNKS):
        order = orders[j]
        name = "b" if order is order_b else "a"
        part = jnp.dot(
            attn_of[name], out_weight[:, j * cols : (j + 1) * cols], preferred_element_type=jnp.float32
        )
        rows = part.shape[0]
        lim = limit_of[name][:, j * bcols : (j + 1) * bcols, None]
        part = jnp.clip(part.reshape(rows, bcols, group), -lim, lim).reshape(rows, cols)
        part = part.astype(jnp.bfloat16)
        for step, b in enumerate(order):
            half = part.shape[0] // 2
            came = flip(part[half:], b)
            part = part[:half].astype(jnp.float32) + came.astype(jnp.float32)
            if step < bits - 1:
                part = part.astype(jnp.bfloat16)
        sums.append(part)
    summed = jnp.concatenate(sums, axis=1)
    stream = (summed + residual.astype(jnp.float32)).astype(jnp.bfloat16)
    wide = stream.astype(jnp.float32)
    inverse = lax.rsqrt(jnp.mean(wide * wide, axis=1, keepdims=True) + 1e-05)
    exps = lax.dynamic_slice_in_dim(code_exp, me * block, block, 0)
    cap = (powers(exps) * 448.0)[:, :, None]
    normed = (wide * inverse * gain[None, :]).reshape(block, blocks, group)
    mixed = jnp.clip(normed, -cap, cap).reshape(block, width).astype(jnp.bfloat16)

    outs = []
    for j in range(CHUNKS):
        order = orders[j]
        held = mixed[:, j * cols : (j + 1) * cols]
        for b in reversed(order):
            held = jnp.concatenate([held, flip(held, b)], axis=0)
        outs.append(from_relative(held, order, me))
    return (jnp.concatenate(outs, axis=1), stream)


def solution(mesh):
    in_specs = (
        P("groups", "tp"),
        P("tp", "groups", None),
        P("groups"),
        P("tp", None),
        P(("groups", "tp"), None),
        P("tp", "groups", None),
        P("groups", None),
        P(),
    )
    out_specs = (P("groups", None), P(("groups", "tp"), None))
    return jax.shard_map(
        per_device, mesh=mesh, in_specs=in_specs, out_specs=out_specs, check_vma=False
    )
```

time: 373 us -> 271 us (0.73)
  waiting for transfers between devices: 173 us -> 98.8 us
  blocking collectives: 32.2 us -> 0 us
  starting transfers between devices: 11.1 us -> 29.7 us
  between operations: 14.8 us -> 2.36 us
  local copies, waits for them, and re-layouts: 71.7 us -> 66.7 us
    ppermute x0 -> x32, waiting for transfers between devices: none -> 98.8 us  [flip(): return lax.ppermute(x, 'tp', [(i, i ^ 1 << b) for i in range(parts)])]
    reduce_scatter x1 -> x0, waiting for transfers between devices: 84 us -> none  [per_device(): lax.psum_scatter(restored(partial_out, exps).astype(jnp.bfloat16), 'tp',...]
    all_gather x1 -> x0, waiting for transfers between devices: 55.5 us -> none  [per_device(): gathered = lax.all_gather(codes, 'tp', axis=1, tiled=True)]
    all_to_all x2 -> x0, waiting for transfers between devices: 33.7 us -> none  [the longest x1 20.7 us: per_device(): lax.all_to_all(stream_cols, 'tp', split_axis=0, concat_axis=1, tiled=True)]
    psum x1 -> x0, blocking collectives: 32.2 us -> none  [per_device(): squares = lax.psum(jnp.sum(wide * wide, axis=1), 'tp')]
    ppermute x0 -> x32, starting transfers between devices: none -> 29.7 us  [flip(): return lax.ppermute(x, 'tp', [(i, i ^ 1 << b) for i in range(parts)])]
    div x3 -> x0, local copies, waits for them, and re-layouts: 24.8 us -> none  [encode(): shaped = values.reshape(rows, blocks, cols // blocks) / scale]
    dot_general x1 -> x5, local copies, waits for them, and re-layouts: 22.4 us -> 38.2 us  [per_device(): jnp.dot(attn_of[name], out_weight[:, j * cols:(j + 1) * cols], preferred_...]
  transfers between devices with their start and end apart: 4 -> 32, of which waited for: 4 -> 18; matrix products, arithmetic and copies ran while one was open for 1% -> 25% of each run, Pallas kernels for 0% -> 0%
where the time goes in v1:
time: 271 us; the launch traced here: 270 us
  waiting for transfers between devices  98.8 us (36%)
  local copies, waits for them, and re-layouts  66.7 us (25%)
  matrix products  37.2 us (14%)
  other arithmetic  35 us (13%)
  starting transfers between devices  29.7 us (11%)
    ppermute x32, waiting for transfers between devices, flip(): return lax.ppermute(x, 'tp', [(i, i ^ 1 << b) for i in range(parts)])  98.8 us
    dot_general x5, local copies, waits for them, and re-layouts, per_device(): jnp.dot(attn_of[name], out_weight[:, j * cols:(j + 1) * cols], preferred_...  38.2 us
    ppermute x32, starting transfers between devices, flip(): return lax.ppermute(x, 'tp', [(i, i ^ 1 << b) for i in range(parts)])  29.7 us
    dot_general x4, matrix products, one_head(): lax.dot_general(single, keys, (((1,), (1,)), ((), ())), preferred_element...  15.5 us
    dot_general x4, matrix products, per_device(): jnp.dot(attn_of[name], out_weight[:, j * cols:(j + 1) * cols], preferred_...  13.9 us
    slice x20, local copies, waits for them, and re-layouts, per_device(): came = flip(part[half:], b)  10.9 us
    convert_element_type x4, local copies, waits for them, and re-layouts, per_device(): part = part[:half].astype(jnp.float32) + came.astype(jnp.float32)  8.92 us
    dot_general x4, matrix products, one_head(): jnp.dot(probs, values, preferred_element_type=jnp.float32)  7.74 us
  transfers between devices with their start and end apart: 32, of which 18 were waited for; matrix products, arithmetic and copies ran while one was open for 25% of the time, Pallas kernels for 0%

profile of v1, /device:TPU:0, one launch (start us, length us, event | category | flops | bytes accessed | tf_op | source)
XLA Modules:
  0.0 269.7 jit_solution(13671674310511733367)
XLA Ops:
  3.6 3.8 %fusion.67 = (bf16[8192,128]{1,0:T(8,128)(2,1)S(1)}, bf16[8192,128]{1,0:T(8,128)(2,1)}) fusion(bf16[8192,256]{1,0:T(8,128)(2,1)} %bitcast.108), kind=kLoop, calls=%fused_computation.237 | loop fusion | bytes 8388608 | tf_op jit(solution)/shard_map/slice | solution.py:24
  8.1 28.8 %while.11 = (s32[]{:T(128)}, bf16[4,256,128]{2,1,0:T(8,128)(2,1)S(1)}, bf16[4,256,128]{1,2,0:T(8,128)(2,1)S(1)}, bf16[8192,128]{1,0:T(8,128)(2,1)}, bf16[8192,12...) while((s32[]{:T(128)}, bf16[4,256,128]{2,1,0:T(8,128)(2,1)S(1)}, ...), condition=%wide.region_3.4_spmd.clone, body=%wide.region_0.3_spmd.clone.sunk | while | flops 1092648448 | bytes 29497436 | solution.py:40
  8.1 3.9 %fusion.93 = (f32[256]{0:T(256)S(1)}, f32[256,8192]{1,0:T(8,128)S(1)}) fusion(bf16[8192,128]{1,0:T(8,128)(2,1)} %get-tuple-element.175, bf16[4,256,128]{1,2,0:T(8,128)(2,1)S(1)} %get-tuple-element.174, s32[]{:T(128)S(6)} %copy.144, s32[256]{0:T(256)S(1)} %get-tuple-element.177), kind=kOutput, calls=%fused_computation.236.clone.1 | convolution fusion | flops 545259264 | bytes 10553348 | tf_op jit(solution)/shard_map/while/body/eval_jaxpr/dot_general | solution.py:30
  15.3 3.9 %fusion.93 = (f32[256]{0:T(256)S(1)}, f32[256,8192]{1,0:T(8,128)S(1)}) fusion(bf16[8192,128]{1,0:T(8,128)(2,1)} %get-tuple-element.175, bf16[4,256,128]{1,2,0:T(8,128)(2,1)S(1)} %get-tuple-element.174, s32[]{:T(128)S(6)} %copy.144, s32[256]{0:T(256)S(1)} %get-tuple-element.177), kind=kOutput, calls=%fused_computation.236.clone.1 | convolution fusion | flops 545259264 | bytes 10553348 | tf_op jit(solution)/shard_map/while/body/eval_jaxpr/dot_general | solution.py:30
  22.5 3.9 %fusion.93 = (f32[256]{0:T(256)S(1)}, f32[256,8192]{1,0:T(8,128)S(1)}) fusion(bf16[8192,128]{1,0:T(8,128)(2,1)} %get-tuple-element.175, bf16[4,256,128]{1,2,0:T(8,128)(2,1)S(1)} %get-tuple-element.174, s32[]{:T(128)S(6)} %copy.144, s32[256]{0:T(256)S(1)} %get-tuple-element.177), kind=kOutput, calls=%fused_computation.236.clone.1 | convolution fusion | flops 545259264 | bytes 10553348 | tf_op jit(solution)/shard_map/while/body/eval_jaxpr/dot_general | solution.py:30
  29.7 3.9 %fusion.93 = (f32[256]{0:T(256)S(1)}, f32[256,8192]{1,0:T(8,128)S(1)}) fusion(bf16[8192,128]{1,0:T(8,128)(2,1)} %get-tuple-element.175, bf16[4,256,128]{1,2,0:T(8,128)(2,1)S(1)} %get-tuple-element.174, s32[]{:T(128)S(6)} %copy.144, s32[256]{0:T(256)S(1)} %get-tuple-element.177), kind=kOutput, calls=%fused_computation.236.clone.1 | convolution fusion | flops 545259264 | bytes 10553348 | tf_op jit(solution)/shard_map/while/body/eval_jaxpr/dot_general | solution.py:30
  37.4 12.4 %slice_bitcast_fusion.3 = (bf16[4096,512]{0,1:T(8,128)(2,1)}, bf16[4096,512]{0,1:T(8,128)(2,1)}, bf16[4096,512]{0,1:T(8,128)(2,1)}, bf16[4096,512]{0,1:T(8,128)(2,1)}) fusion(bf16[512,16384]{1,0:T(8,128)(2,1)} %param.13), kind=kLoop, calls=%fused_computation.22 | loop fusion | bytes 33554432 | tf_op jit(solution)/shard_map/dot_general | solution.py:100
  49.8 6.4 %copy.122 = bf16[4096,512]{1,0:T(8,128)(2,1)} copy(bf16[4096,512]{0,1:T(8,128)(2,1)} %get-tuple-element.88) | data formatting | bytes 8388608 | tf_op jit(solution)/shard_map/dot_general | solution.py:100
  63.2 6.4 %copy.118 = bf16[4096,512]{1,0:T(8,128)(2,1)} copy(bf16[4096,512]{0,1:T(8,128)(2,1)} %get-tuple-element.89) | data formatting | bytes 8388608 | tf_op jit(solution)/shard_map/dot_general | solution.py:100
  76.2 6.5 %copy.114 = bf16[4096,512]{1,0:T(8,128)(2,1)} copy(bf16[4096,512]{0,1:T(8,128)(2,1)} %get-tuple-element.87) | data formatting | bytes 8388608 | tf_op jit(solution)/shard_map/dot_general | solution.py:100
  82.7 3.5 %minimum_convert_fusion.2 = bf16[256,32,128]{0,2,1:T(8,128)(2,1)S(1)} fusion(bf16[256,512,1]{1,0,2:T(8,128)(2,1)S(1)} %bitcast.133, bf16[32,128,512]{2,1,0:T(8,128)(2,1)} %bitcast.111, bf16[256,32]{0,1:T(8,128)(2,1)S(1)} %neg.22, f32[256,32]{0,1:T(8,128)S(1)} %copy.131), kind=kOutput, calls=%fused_computation.19 | convolution fusion | flops 1078984704 | bytes 6602752 | tf_op jit(solution)/shard_map/dot_general | solution.py:100
  90.5 6.4 %copy.108 = bf16[4096,512]{1,0:T(8,128)(2,1)} copy(bf16[4096,512]{0,1:T(8,128)(2,1)} %get-tuple-element.86) | data formatting | bytes 8388608 | tf_op jit(solution)/shard_map/dot_general | solution.py:100
  132.3 4.4 %collective-permute-done.13 = bf16[64,4096]{1,0:T(8,128)(2,1)S(1)} collective-permute-done((bf16[64,4096]{1,0:T(8,128)(2,1)S(1)}, bf16[64,4096]{1,0:T(8,128)(2,1)S(1)}, u32[]{:S(2)}, u32[]{:S(2)}) %collective-permute-start.13) | collective-permute-done | bytes 524320 | tf_op jit(solution)/shard_map/ppermute | solution.py:82
  138.9 9.0 %collective-permute-done.9 = bf16[64,4096]{1,0:T(8,128)(2,1)S(1)} collective-permute-done((bf16[64,4096]{1,0:T(8,128)(2,1)S(1)}, bf16[64,4096]{1,0:T(8,128)(2,1)S(1)}, u32[]{:S(2)}, u32[]{:S(2)}) %collective-permute-start.9) | collective-permute-done | bytes 524320 | tf_op jit(solution)/shard_map/ppermute | solution.py:82
  150.2 8.8 %collective-permute-done.5 = bf16[64,4096]{1,0:T(8,128)(2,1)S(1)} collective-permute-done((bf16[64,4096]{1,0:T(8,128)(2,1)S(1)}, bf16[64,4096]{1,0:T(8,128)(2,1)S(1)}, u32[]{:S(2)}, u32[]{:S(2)}) %collective-permute-start.5) | collective-permute-done | bytes 524320 | tf_op jit(solution)/shard_map/ppermute | solution.py:82
  166.0 4.9 %collective-permute-done.6 = bf16[32,4096]{1,0:T(8,128)(2,1)S(1)} collective-permute-done((bf16[32,4096]{1,0:T(8,128)(2,1)S(1)}, bf16[32,4096]{1,0:T(8,128)(2,1)S(1)}, u32[]{:S(2)}, u32[]{:S(2)}) %collective-permute-start.6) | collective-permute-done | bytes 262176 | tf_op jit(solution)/shard_map/ppermute | solution.py:82
  174.1 6.7 %collective-permute-done.15 = bf16[16,4096]{1,0:T(8,128)(2,1)S(1)} collective-permute-done((bf16[16,4096]{1,0:T(8,128)(2,1)S(1)}, bf16[16,4096]{1,0:T(8,128)(2,1)S(1)}, u32[]{:S(2)}, u32[]{:S(2)}) %collective-permute-start.15) | collective-permute-done | bytes 131104 | tf_op jit(solution)/shard_map/ppermute | solution.py:82
  196.2 10.6 %collective-permute-done.28 = bf16[16,4096]{1,0:T(8,128)(2,1)S(1)} collective-permute-done((bf16[16,4096]{1,0:T(8,128)(2,1)S(1)}, bf16[16,4096]{1,0:T(8,128)(2,1)S(1)}, u32[]{:S(2)}, u32[]{:S(2)}) %collective-permute-start.28) | collective-permute-done | bytes 131104 | tf_op jit(solution)/shard_map/ppermute | solution.py:82
  214.8 5.1 %collective-permute-done.29 = bf16[32,4096]{1,0:T(8,128)(2,1)S(1)} collective-permute-done((bf16[32,4096]{1,0:T(8,128)(2,1)S(1)}, bf16[32,4096]{1,0:T(8,128)(2,1)S(1)}, u32[]{:S(2)}, u32[]{:S(2)}) %collective-permute-start.29) | collective-permute-done | bytes 262176 | tf_op jit(solution)/shard_map/ppermute | solution.py:82
  220.4 5.2 %collective-permute-done.25 = bf16[32,4096]{1,0:T(8,128)(2,1)S(1)} collective-permute-done((bf16[32,4096]{1,0:T(8,128)(2,1)S(1)}, bf16[32,4096]{1,0:T(8,128)(2,1)S(1)}, u32[]{:S(2)}, u32[]{:S(2)}) %collective-permute-start.25) | collective-permute-done | bytes 262176 | tf_op jit(solution)/shard_map/ppermute | solution.py:82
  226.0 5.1 %collective-permute-done.21 = bf16[32,4096]{1,0:T(8,128)(2,1)S(1)} collective-permute-done((bf16[32,4096]{1,0:T(8,128)(2,1)S(1)}, bf16[32,4096]{1,0:T(8,128)(2,1)S(1)}, u32[]{:S(2)}, u32[]{:S(2)}) %collective-permute-start.21) | collective-permute-done | bytes 262176 | tf_op jit(solution)/shard_map/ppermute | solution.py:82
  235.0 11.1 %collective-permute-done.26 = bf16[64,4096]{1,0:T(8,128)(2,1)S(1)} collective-permute-done((bf16[64,4096]{1,0:T(8,128)(2,1)S(1)}, bf16[64,4096]{1,0:T(8,128)(2,1)S(1)}, u32[]{:S(2)}, u32[]{:S(2)}) %collective-permute-start.26) | collective-permute-done | bytes 524320 | tf_op jit(solution)/shard_map/ppermute | solution.py:82
  246.3 10.0 %collective-permute-done.22 = bf16[64,4096]{1,0:T(8,128)(2,1)S(1)} collective-permute-done((bf16[64,4096]{1,0:T(8,128)(2,1)S(1)}, bf16[64,4096]{1,0:T(8,128)(2,1)S(1)}, u32[]{:S(2)}, u32[]{:S(2)}) %collective-permute-start.22) | collective-permute-done | bytes 524320 | tf_op jit(solution)/shard_map/ppermute | solution.py:82
  266.0 3.6 %pad_maximum_fusion = bf16[256,16384]{1,0:T(8,128)(2,1)} fusion(bf16[256,4096]{1,0:T(8,128)(2,1)S(1)} %bitcast.104, bf16[256,4096]{1,0:T(8,128)(2,1)S(1)} %bitcast.105, bf16[256,4096]{1,0:T(8,128)(2,1)S(1)} %bitcast.106, bf16[256,4096]{1,0:T(8,128)(2,1)S(1)} %bitcast.107), kind=kLoop, calls=%fused_computation.14 | loop fusion | flops 33554432 | bytes 16777216 | tf_op jit(solution)/shard_map/concatenate | solution.py:130
  (218 shorter events, 121.7 us)
Async XLA Ops:
  62.7 56.3 %collective-permute-start.12 = (bf16[128,4096]{1,0:T(8,128)(2,1)}, bf16[128,4096]{1,0:T(8,128)(2,1)}, u32[]{:S(2)}, u32[]{:S(2)}) collective-permute-start(bf16[128,4096]{1,0:T(8,128)(2,1)} %copy.123), channel_id=1, source_target_pairs={{0,1},{1,0},{2,3},{3,2},{4,5},{5,4},{6,7},{7,6},{8,9},{9,8},{10,11... | collective-permute-start | bytes 3145736 | tf_op jit(solution)/shard_map/ppermute | solution.py:82
  76.1 47.8 %collective-permute-start.8 = (bf16[128,4096]{1,0:T(8,128)(2,1)}, bf16[128,4096]{1,0:T(8,128)(2,1)}, u32[]{:S(2)}, u32[]{:S(2)}) collective-permute-start(bf16[128,4096]{1,0:T(8,128)(2,1)} %copy.119), channel_id=1, source_target_pairs={{0,1},{1,0},{2,3},{3,2},{4,5},{5,4},{6,7},{7,6},{8,9},{9,8},{10,11... | collective-permute-start | bytes 3145736 | tf_op jit(solution)/shard_map/ppermute | solution.py:82
  89.1 36.7 %collective-permute-start.4 = (bf16[128,4096]{1,0:T(8,128)(2,1)}, bf16[128,4096]{1,0:T(8,128)(2,1)}, u32[]{:S(2)}, u32[]{:S(2)}) collective-permute-start(bf16[128,4096]{1,0:T(8,128)(2,1)} %copy.115), channel_id=1, source_target_pairs={{0,1},{1,0},{2,3},{3,2},{4,5},{5,4},{6,7},{7,6},{8,9},{9,8},{10,11... | collective-permute-start | bytes 3145736 | tf_op jit(solution)/shard_map/ppermute | solution.py:82
  103.5 25.7 %collective-permute-start = (bf16[128,4096]{1,0:T(8,128)(2,1)}, bf16[128,4096]{1,0:T(8,128)(2,1)}, u32[]{:S(2)}, u32[]{:S(2)}) collective-permute-start(bf16[128,4096]{1,0:T(8,128)(2,1)} %copy.109), channel_id=1, source_target_pairs={{0,1},{1,0},{2,3},{3,2},{4,5},{5,4},{6,7},{7,6},{8,9},{9,8},{10,11... | collective-permute-start | bytes 3145736 | tf_op jit(solution)/shard_map/ppermute | solution.py:82
  125.5 22.5 %collective-permute-start.9 = (bf16[64,4096]{1,0:T(8,128)(2,1)S(1)}, bf16[64,4096]{1,0:T(8,128)(2,1)S(1)}, u32[]{:S(2)}, u32[]{:S(2)}) collective-permute-start(bf16[64,4096]{1,0:T(8,128)(2,1)S(1)} %slice.228), channel_id=1, source_target_pairs={{0,2},{1,3},{2,0},{3,1},{4,6},{5,7},{6,4},{7,5},{8,10},{9,11},{10,... | collective-permute-start | bytes 1572872 | tf_op jit(solution)/shard_map/ppermute | solution.py:82
  127.4 31.6 %collective-permute-start.5 = (bf16[64,4096]{1,0:T(8,128)(2,1)S(1)}, bf16[64,4096]{1,0:T(8,128)(2,1)S(1)}, u32[]{:S(2)}, u32[]{:S(2)}) collective-permute-start(bf16[64,4096]{1,0:T(8,128)(2,1)S(1)} %slice.219), channel_id=1, source_target_pairs={{0,2},{1,3},{2,0},{3,1},{4,6},{5,7},{6,4},{7,5},{8,10},{9,11},{10,... | collective-permute-start | bytes 1572872 | tf_op jit(solution)/shard_map/ppermute | solution.py:82
  130.7 30.4 %collective-permute-start.1 = (bf16[64,4096]{1,0:T(8,128)(2,1)S(1)}, bf16[64,4096]{1,0:T(8,128)(2,1)S(1)}, u32[]{:S(2)}, u32[]{:S(2)}) collective-permute-start(bf16[64,4096]{1,0:T(8,128)(2,1)S(1)} %slice.210), channel_id=1, source_target_pairs={{0,4},{1,5},{2,6},{3,7},{4,0},{5,1},{6,2},{7,3},{8,12},{9,13},{10,... | collective-permute-start | bytes 1572872 | tf_op jit(solution)/shard_map/ppermute | solution.py:82
  136.9 25.9 %collective-permute-start.14 = (bf16[32,4096]{1,0:T(8,128)(2,1)S(1)}, bf16[32,4096]{1,0:T(8,128)(2,1)S(1)}, u32[]{:S(2)}, u32[]{:S(2)}) collective-permute-start(bf16[32,4096]{1,0:T(8,128)(2,1)S(1)} %slice.239), channel_id=1, source_target_pairs={{0,4},{1,5},{2,6},{3,7},{4,0},{5,1},{6,2},{7,3},{8,12},{9,13},{10,... | collective-permute-start | bytes 786440 | tf_op jit(solution)/shard_map/ppermute | solution.py:82
  148.1 17.4 %collective-permute-start.10 = (bf16[32,4096]{1,0:T(8,128)(2,1)S(1)}, bf16[32,4096]{1,0:T(8,128)(2,1)S(1)}, u32[]{:S(2)}, u32[]{:S(2)}) collective-permute-start(bf16[32,4096]{1,0:T(8,128)(2,1)S(1)} %slice.230), channel_id=1, source_target_pairs={{0,4},{1,5},{2,6},{3,7},{4,0},{5,1},{6,2},{7,3},{8,12},{9,13},{10,... | collective-permute-start | bytes 786440 | tf_op jit(solution)/shard_map/ppermute | solution.py:82
  162.9 18.0 %collective-permute-start.15 = (bf16[16,4096]{1,0:T(8,128)(2,1)S(1)}, bf16[16,4096]{1,0:T(8,128)(2,1)S(1)}, u32[]{:S(2)}, u32[]{:S(2)}) collective-permute-start(bf16[16,4096]{1,0:T(8,128)(2,1)S(1)} %slice.241), channel_id=1, source_target_pairs={{0,8},{1,9},{2,10},{3,11},{4,12},{5,13},{6,14},{7,15},{8,0},{9,1},... | collective-permute-start | bytes 393224 | tf_op jit(solution)/shard_map/ppermute | solution.py:82
  165.6 18.0 %collective-permute-start.11 = (bf16[16,4096]{1,0:T(8,128)(2,1)S(1)}, bf16[16,4096]{1,0:T(8,128)(2,1)S(1)}, u32[]{:S(2)}, u32[]{:S(2)}) collective-permute-start(bf16[16,4096]{1,0:T(8,128)(2,1)S(1)} %slice.232), channel_id=1, source_target_pairs={{0,8},{1,9},{2,10},{3,11},{4,12},{5,13},{6,14},{7,15},{8,0},{9,1},... | collective-permute-start | bytes 393224 | tf_op jit(solution)/shard_map/ppermute | solution.py:82
  171.0 15.5 %collective-permute-start.7 = (bf16[16,4096]{1,0:T(8,128)(2,1)S(1)}, bf16[16,4096]{1,0:T(8,128)(2,1)S(1)}, u32[]{:S(2)}, u32[]{:S(2)}) collective-permute-start(bf16[16,4096]{1,0:T(8,128)(2,1)S(1)} %slice.223), channel_id=1, source_target_pairs={{0,8},{1,9},{2,10},{3,11},{4,12},{5,13},{6,14},{7,15},{8,0},{9,1},... | collective-permute-start | bytes 393224 | tf_op jit(solution)/shard_map/ppermute | solution.py:82
  172.0 16.4 %collective-permute-start.3 = (bf16[16,4096]{1,0:T(8,128)(2,1)S(1)}, bf16[16,4096]{1,0:T(8,128)(2,1)S(1)}, u32[]{:S(2)}, u32[]{:S(2)}) collective-permute-start(bf16[16,4096]{1,0:T(8,128)(2,1)S(1)} %slice.214), channel_id=1, source_target_pairs={{0,8},{1,9},{2,10},{3,11},{4,12},{5,13},{6,14},{7,15},{8,0},{9,1},... | collective-permute-start | bytes 393224 | tf_op jit(solution)/shard_map/ppermute | solution.py:82
  190.2 16.5 %collective-permute-start.28 = (bf16[16,4096]{1,0:T(8,128)(2,1)S(1)}, bf16[16,4096]{1,0:T(8,128)(2,1)S(1)}, u32[]{:S(2)}, u32[]{:S(2)}) collective-permute-start(bf16[16,4096]{1,0:T(8,128)(2,1)S(1)} %get-tuple-element.105), channel_id=1, source_target_pairs={{0,8},{1,9},{2,10},{3,11},{4,12},{5,13},{6,14},{7,15},{8,0},{9,1},... | collective-permute-start | bytes 393224 | tf_op jit(solution)/shard_map/ppermute | solution.py:82
  190.3 19.4 %collective-permute-start.24 = (bf16[16,4096]{1,0:T(8,128)(2,1)S(1)}, bf16[16,4096]{1,0:T(8,128)(2,1)S(1)}, u32[]{:S(2)}, u32[]{:S(2)}) collective-permute-start(bf16[16,4096]{1,0:T(8,128)(2,1)S(1)} %get-tuple-element.106), channel_id=1, source_target_pairs={{0,8},{1,9},{2,10},{3,11},{4,12},{5,13},{6,14},{7,15},{8,0},{9,1},... | collective-permute-start | bytes 393224 | tf_op jit(solution)/shard_map/ppermute | solution.py:82
  193.2 19.3 %collective-permute-start.20 = (bf16[16,4096]{1,0:T(8,128)(2,1)S(1)}, bf16[16,4096]{1,0:T(8,128)(2,1)S(1)}, u32[]{:S(2)}, u32[]{:S(2)}) collective-permute-start(bf16[16,4096]{1,0:T(8,128)(2,1)S(1)} %get-tuple-element.107), channel_id=1, source_target_pairs={{0,8},{1,9},{2,10},{3,11},{4,12},{5,13},{6,14},{7,15},{8,0},{9,1},... | collective-permute-start | bytes 393224 | tf_op jit(solution)/shard_map/ppermute | solution.py:82
  193.3 21.0 %collective-permute-start.16 = (bf16[16,4096]{1,0:T(8,128)(2,1)S(1)}, bf16[16,4096]{1,0:T(8,128)(2,1)S(1)}, u32[]{:S(2)}, u32[]{:S(2)}) collective-permute-start(bf16[16,4096]{1,0:T(8,128)(2,1)S(1)} %get-tuple-element.100), channel_id=1, source_target_pairs={{0,8},{1,9},{2,10},{3,11},{4,12},{5,13},{6,14},{7,15},{8,0},{9,1},... | collective-permute-start | bytes 393224 | tf_op jit(solution)/shard_map/ppermute | solution.py:82
  209.7 15.9 %collective-permute-start.25 = (bf16[32,4096]{1,0:T(8,128)(2,1)S(1)}, bf16[32,4096]{1,0:T(8,128)(2,1)S(1)}, u32[]{:S(2)}, u32[]{:S(2)}) collective-permute-start(bf16[32,4096]{1,0:T(8,128)(2,1)S(1)} %pad_maximum_fusion.11), channel_id=1, source_target_pairs={{0,4},{1,5},{2,6},{3,7},{4,0},{5,1},{6,2},{7,3},{8,12},{9,13},{10,... | collective-permute-start | bytes 786440 | tf_op jit(solution)/shard_map/ppermute | solution.py:82
  212.5 18.6 %collective-permute-start.21 = (bf16[32,4096]{1,0:T(8,128)(2,1)S(1)}, bf16[32,4096]{1,0:T(8,128)(2,1)S(1)}, u32[]{:S(2)}, u32[]{:S(2)}) collective-permute-start(bf16[32,4096]{1,0:T(8,128)(2,1)S(1)} %pad_maximum_fusion.10), channel_id=1, source_target_pairs={{0,4},{1,5},{2,6},{3,7},{4,0},{5,1},{6,2},{7,3},{8,12},{9,13},{10,... | collective-permute-start | bytes 786440 | tf_op jit(solution)/shard_map/ppermute | solution.py:82
  214.4 17.2 %collective-permute-start.17 = (bf16[32,4096]{1,0:T(8,128)(2,1)S(1)}, bf16[32,4096]{1,0:T(8,128)(2,1)S(1)}, u32[]{:S(2)}, u32[]{:S(2)}) collective-permute-start(bf16[32,4096]{1,0:T(8,128)(2,1)S(1)} %pad_maximum_fusion.9), channel_id=1, source_target_pairs={{0,2},{1,3},{2,0},{3,1},{4,6},{5,7},{6,4},{7,5},{8,10},{9,11},{10,... | collective-permute-start | bytes 786440 | tf_op jit(solution)/shard_map/ppermute | solution.py:82
  225.6 20.5 %collective-permute-start.26 = (bf16[64,4096]{1,0:T(8,128)(2,1)S(1)}, bf16[64,4096]{1,0:T(8,128)(2,1)S(1)}, u32[]{:S(2)}, u32[]{:S(2)}) collective-permute-start(bf16[64,4096]{1,0:T(8,128)(2,1)S(1)} %pad_maximum_fusion.7), channel_id=1, source_target_pairs={{0,2},{1,3},{2,0},{3,1},{4,6},{5,7},{6,4},{7,5},{8,10},{9,11},{10,... | collective-permute-start | bytes 1572872 | tf_op jit(solution)/shard_map/ppermute | solution.py:82
  231.1 25.1 %collective-permute-start.22 = (bf16[64,4096]{1,0:T(8,128)(2,1)S(1)}, bf16[64,4096]{1,0:T(8,128)(2,1)S(1)}, u32[]{:S(2)}, u32[]{:S(2)}) collective-permute-start(bf16[64,4096]{1,0:T(8,128)(2,1)S(1)} %pad_maximum_fusion.6), channel_id=1, source_target_pairs={{0,2},{1,3},{2,0},{3,1},{4,6},{5,7},{6,4},{7,5},{8,10},{9,11},{10,... | collective-permute-start | bytes 1572872 | tf_op jit(solution)/shard_map/ppermute | solution.py:82
  231.6 24.9 %collective-permute-start.18 = (bf16[64,4096]{1,0:T(8,128)(2,1)S(1)}, bf16[64,4096]{1,0:T(8,128)(2,1)S(1)}, u32[]{:S(2)}, u32[]{:S(2)}) collective-permute-start(bf16[64,4096]{1,0:T(8,128)(2,1)S(1)} %pad_maximum_fusion.5), channel_id=1, source_target_pairs={{0,4},{1,5},{2,6},{3,7},{4,0},{5,1},{6,2},{7,3},{8,12},{9,13},{10,... | collective-permute-start | bytes 1572872 | tf_op jit(solution)/shard_map/ppermute | solution.py:82
  234.9 22.3 %collective-permute-start.31 = (bf16[128,4096]{1,0:T(8,128)(2,1)S(1)}, bf16[128,4096]{1,0:T(8,128)(2,1)S(1)}, u32[]{:S(2)}, u32[]{:S(2)}) collective-permute-start(bf16[128,4096]{1,0:T(8,128)(2,1)S(1)} %pad_maximum_fusion.4), channel_id=1, source_target_pairs={{0,1},{1,0},{2,3},{3,2},{4,5},{5,4},{6,7},{7,6},{8,9},{9,8},{10,11... | collective-permute-start | bytes 3145736 | tf_op jit(solution)/shard_map/ppermute | solution.py:82
  (17 other events, 135.5 us)

commit v2 on v1

v2 whole, which is shorter than its diff:
```python
import functools

import jax
import jax.numpy as jnp
from jax import lax
from jax.experimental import pallas as pl
from jax.experimental.pallas import tpu as pltpu
from jax.sharding import PartitionSpec as P

CHUNKS = 4
KEY_BLOCK = 2048
TILE = 1024
CODE_TOP = 448.0
LOG2E = 1.4426950408889634


def powers(exps):
    magnitude = jnp.abs(exps)
    result = jnp.ones(exps.shape, jnp.float32)
    for bit in range(6):
        chosen = (magnitude >> bit) & 1 == 1
        result = result * jnp.where(chosen, jnp.float32(2.0**2**bit), jnp.float32(1.0))
    return jnp.where(exps < 0, 1.0 / result, result)


def attention_kernel(
    start_ref, place_ref, q_ref, kv_ref, exp_ref, *refs, key_block, heads, head, n_orders
):
    attn_refs = refs[:n_orders]
    limit_refs = refs[n_orders : 2 * n_orders]
    top_ref, acc_ref = refs[2 * n_orders :]
    step = pl.program_id(0)
    start = start_ref[0]
    rows = q_ref.shape[0]
    n_blocks = place_ref.shape[1]
    block = rows // n_blocks
    coef = head**-0.5 * LOG2E

    @pl.when(step == 0)
    def _():
        top_ref[...] = jnp.full_like(top_ref, -1e30)
        acc_ref[...] = jnp.zeros_like(acc_ref)
        limit = powers(exp_ref[0]) * CODE_TOP
        for i in range(n_blocks):
            for o in range(n_orders):
                to = pl.ds(pl.multiple_of(place_ref[o, i] * block, block), block)
                limit_refs[o][to, :] = limit[i * block : (i + 1) * block]

    def attend(masked):
        keys = kv_ref[0, :, :head]
        ones = jnp.ones((key_block, head), jnp.bfloat16)
        values = jnp.concatenate([kv_ref[0, :, head:], ones], axis=1)
        if masked:
            row = lax.broadcasted_iota(jnp.int32, (rows, key_block), 0)
            col = lax.broadcasted_iota(jnp.int32, (rows, key_block), 1)
            seen = col - row <= start - step * key_block
        for h in range(heads):
            scores = lax.dot_general(
                q_ref[:, h * head : (h + 1) * head],
                keys,
                (((1,), (1,)), ((), ())),
                preferred_element_type=jnp.float32,
            )
            if masked:
                scores = jnp.where(seen, scores, jnp.float32(-1e30))
            before = top_ref[h]
            top = jnp.maximum(before, jnp.max(scores, axis=1, keepdims=True))
            weights = jnp.exp2((scores - top[:, :1]) * coef).astype(jnp.bfloat16)
            fade = jnp.exp2((before - top) * coef)
            got = jnp.dot(weights, values, preferred_element_type=jnp.float32)
            acc_ref[h] = acc_ref[h] * jnp.concatenate([fade, fade], axis=1) + got
            top_ref[h] = top

    first = step * key_block
    past = first + key_block - 1 > start

    @pl.when(jnp.logical_and(past, first <= start + rows - 1))
    def _():
        attend(True)

    @pl.when(jnp.logical_not(past))
    def _():
        attend(False)

    @pl.when(step == pl.num_programs(0) - 1)
    def _():
        for h in range(heads):
            acc = acc_ref[h]
            out = (acc[:, :head] / acc[:, head:]).astype(jnp.bfloat16)
            for i in range(n_blocks):
                for o in range(n_orders):
                    to = pl.ds(pl.multiple_of(place_ref[o, i] * block, block), block)
                    attn_refs[o][to, h * head : (h + 1) * head] = out[i * block : (i + 1) * block]


def attention(start, places, queries, cache, term_exp):
    rows, span = queries.shape
    context, head = cache.shape[1], cache.shape[2] // 2
    heads = span // head
    n_orders = places.shape[0]
    blocks = term_exp.shape[2]
    key_block = min(KEY_BLOCK, context)

    def cache_block(step, start_ref, place_ref):
        return (0, jnp.minimum(step, (start_ref[0] + rows - 1) // key_block), 0)

    def whole(*shape):
        return pl.BlockSpec(shape, lambda step, start_ref, place_ref: (0,) * len(shape))

    return pl.pallas_call(
        functools.partial(
            attention_kernel, key_block=key_block, heads=heads, head=head, n_orders=n_orders
        ),
        grid_spec=pltpu.PrefetchScalarGridSpec(
            num_scalar_prefetch=2,
            grid=(context // key_block,),
            in_specs=[
                whole(rows, span),
                pl.BlockSpec((1, key_block, 2 * head), cache_block),
                whole(1, rows, blocks),
            ],
            out_specs=[whole(rows, span)] * n_orders + [whole(rows, blocks)] * n_orders,
            scratch_shapes=[
                pltpu.VMEM((heads, rows, head), jnp.float32),
                pltpu.VMEM((heads, rows, 2 * head), jnp.float32),
            ],
        ),
        out_shape=[jax.ShapeDtypeStruct((rows, span), jnp.bfloat16)] * n_orders
        + [jax.ShapeDtypeStruct((rows, blocks), jnp.float32)] * n_orders,
        compiler_params=pltpu.CompilerParams(vmem_limit_bytes=48 << 20),
        name="attention",
    )(start, places, queries, cache, term_exp)


def project_kernel(attn_ref, weight_ref, limit_ref, keep_ref, send_ref, *, first, group):
    step = pl.program_id(0)
    half = keep_ref.shape[0]
    lanes = limit_ref.shape[1]
    per = weight_ref.shape[1] // group
    shift = lax.rem(lanes - (first + step * per), lanes)
    limit = pltpu.roll(limit_ref[...], shift, 1)
    got = jnp.dot(attn_ref[...], weight_ref[...], preferred_element_type=jnp.float32)
    for b in range(per):
        cut = slice(b * group, (b + 1) * group)
        bound = jnp.broadcast_to(limit[:, b : b + 1], (2 * half, group))
        part = jnp.minimum(jnp.maximum(got[:, cut], -bound), bound).astype(jnp.bfloat16)
        keep_ref[:, cut] = part[:half]
        send_ref[:, cut] = part[half:]


def project(attn, out_weight, limit, first_col, cols):
    rows, span = attn.shape
    group = out_weight.shape[1] // limit.shape[1]
    half = rows // 2
    base = first_col // TILE
    return pl.pallas_call(
        functools.partial(project_kernel, first=first_col // group, group=group),
        grid=(cols // TILE,),
        in_specs=[
            pl.BlockSpec((rows, span), lambda i: (0, 0)),
            pl.BlockSpec((span, TILE), lambda i: (0, base + i)),
            pl.BlockSpec(limit.shape, lambda i: (0, 0)),
        ],
        out_specs=[pl.BlockSpec((half, TILE), lambda i: (0, i))] * 2,
        out_shape=[jax.ShapeDtypeStruct((half, cols), jnp.bfloat16)] * 2,
        compiler_params=pltpu.CompilerParams(vmem_limit_bytes=32 << 20),
        cost_estimate=pl.CostEstimate(
            flops=2 * rows * span * cols,
            bytes_accessed=2 * (span * cols + rows * span + rows * cols),
            transcendentals=0,
        ),
        name="project",
    )(attn, out_weight, limit)


def from_relative(x, order, me):
    n = len(order)
    rows = x.shape[0]
    block = rows // 2**n
    shaped = x.reshape((2,) * n + (block,) + x.shape[1:])
    for axis, b in enumerate(order):
        shaped = jnp.where((me >> b) & 1 == 1, jnp.flip(shaped, axis), shaped)
    inverse = [0] * n
    for axis, b in enumerate(order):
        inverse[n - 1 - b] = axis
    shaped = shaped.transpose(tuple(inverse) + tuple(range(n, shaped.ndim)))
    return shaped.reshape(x.shape)


def per_device(queries, cache, offset, out_weight, residual, term_exp, code_exp, gain):
    me = lax.axis_index("tp")
    parts = lax.axis_size("tp")
    bits = parts.bit_length() - 1
    block, width = residual.shape
    blocks = code_exp.shape[1]
    group = width // blocks
    cols = width // CHUNKS

    def flip(x, b):
        return lax.ppermute(x, "tp", [(i, i ^ (1 << b)) for i in range(parts)])

    order_a = list(range(bits))
    order_b = [0, 2, 1] + list(range(3, bits))
    kinds = [order_a, order_b]
    uses = [1] + [0] * (CHUNKS - 1)

    apart = jnp.arange(parts, dtype=jnp.int32) ^ me
    places = jnp.stack(
        [sum(((apart >> b) & 1) << (bits - 1 - k) for k, b in enumerate(order)) for order in kinds]
    )
    got = attention(offset, places, queries, cache, term_exp)
    attns, limits = got[: len(kinds)], got[len(kinds) :]

    sums = []
    for j in range(CHUNKS):
        kind = uses[j]
        keep, send = project(attns[kind], out_weight, limits[kind], j * cols, cols)
        for step, b in enumerate(kinds[kind]):
            came = flip(send, b)
            if step < bits - 1:
                half = keep.shape[0] // 2
                send = (keep[half:].astype(jnp.float32) + came[half:].astype(jnp.float32)).astype(jnp.bfloat16)
                keep = (keep[:half].astype(jnp.float32) + came[:half].astype(jnp.float32)).astype(jnp.bfloat16)
            else:
                keep = keep.astype(jnp.float32) + came.astype(jnp.float32)
        sums.append(keep)
    summed = jnp.concatenate(sums, axis=1)
    stream = (summed + residual.astype(jnp.float32)).astype(jnp.bfloat16)
    wide = stream.astype(jnp.float32)
    inverse = lax.rsqrt(jnp.mean(wide * wide, axis=1, keepdims=True) + 1e-05)
    exps = lax.dynamic_slice_in_dim(code_exp, me * block, block, 0)
    cap = (powers(exps) * CODE_TOP)[:, :, None]
    normed = (wide * inverse * gain[None, :]).reshape(block, blocks, group)
    mixed = jnp.clip(normed, -cap, cap).reshape(block, width).astype(jnp.bfloat16)

    outs = []
    for j in range(CHUNKS):
        order = kinds[uses[j]]
        held = mixed[:, j * cols : (j + 1) * cols]
        for b in reversed(order):
            held = jnp.concatenate([held, flip(held, b)], axis=0)
        outs.append(from_relative(held, order, me))
    return (jnp.concatenate(outs, axis=1), stream)


def solution(mesh):
    in_specs = (
        P("groups", "tp"),
        P("tp", "groups", None),
        P("groups"),
        P("tp", None),
        P(("groups", "tp"), None),
        P("tp", "groups", None),
        P("groups", None),
        P(),
    )
    out_specs = (P("groups", None), P(("groups", "tp"), None))
    return jax.shard_map(
        per_device, mesh=mesh, in_specs=in_specs, out_specs=out_specs, check_vma=False
    )
```

time: 271 us -> 199 us (0.73)
  local copies, waits for them, and re-layouts: 66.7 us -> 13.7 us
  matrix products: 37.2 us -> 0 us
  Pallas kernels: 0 us -> 24.3 us
  other arithmetic: 35 us -> 20 us
  waiting for transfers between devices: 98.8 us -> 103 us
    dot_general x5 -> x0, local copies, waits for them, and re-layouts: 38.2 us -> none  [per_device(): jnp.dot(attn_of[name], out_weight[:, j * cols:(j + 1) * cols], preferred_...]
    dot_general x12 -> x0, matrix products: 37.2 us -> none  [the longest x4 15.5 us: one_head(): lax.dot_general(single, keys, (((1,), (1,)), ((), ())), preferred_element...]
    pallas_call x0 -> x5, Pallas kernels: none -> 24.3 us  [the longest x4 12.6 us: project(): pl.pallas_call(functools.partial(project_kernel, first=first_col // group...]
    slice x22 -> x0, local copies, waits for them, and re-layouts: 14.9 us -> none  [the longest x20 10.9 us: per_device(): came = flip(part[half:], b)]
    convert_element_type x4 -> x0, local copies, waits for them, and re-layouts: 8.92 us -> none  [per_device(): part = part[:half].astype(jnp.float32) + came.astype(jnp.float32)]
    unnamed x35 -> x34, local copies, waits for them, and re-layouts: 2.58 us -> 11.4 us
    convert_element_type x16 -> x12, other arithmetic: 12.2 us -> 6.73 us  [the longest x8 6.6 us: per_device(): (keep[:half].astype(jnp.float32) + came[:half].astype(jnp.float32)).astyp...]
    reduce_sum x4 -> x0, other arithmetic: 5.43 us -> none  [one_head(): jnp.sum(weights, axis=1, keepdims=True)]
  transfers between devices with their start and end apart: 32 -> 32, of which waited for: 18 -> 19; matrix products, arithmetic and copies ran while one was open for 25% -> 8% of each run, Pallas kernels for 0% -> 5%
where the time goes in v2:
time: 199 us; the launch traced here: 195 us
  waiting for transfers between devices  103 us (52%)
  starting transfers between devices  32.1 us (16%)
  Pallas kernels  24.3 us (12%)
  other arithmetic  20 us (10%)
  local copies, waits for them, and re-layouts  13.7 us (7%)
    ppermute x32, waiting for transfers between devices, flip(): return lax.ppermute(x, 'tp', [(i, i ^ 1 << b) for i in range(parts)])  103 us
    ppermute x32, starting transfers between devices, flip(): return lax.ppermute(x, 'tp', [(i, i ^ 1 << b) for i in range(parts)])  32.1 us
    pallas_call x4, Pallas kernels, project(): pl.pallas_call(functools.partial(project_kernel, first=first_col // group...  12.6 us
    pallas_call x1, Pallas kernels, attention(): pl.pallas_call(functools.partial(attention_kernel, key_block=key_block, h...  11.7 us
    unnamed x34, local copies, waits for them, and re-layouts  11.4 us
    convert_element_type x8, other arithmetic, per_device(): (keep[:half].astype(jnp.float32) + came[:half].astype(jnp.float32)).astyp...  6.6 us
    select_n x12, other arithmetic, from_relative(): shaped = jnp.where(me >> b & 1 == 1, jnp.flip(shaped, axis), shaped)  5.53 us
  transfers between devices with their start and end apart: 32, of which 19 were waited for; matrix products, arithmetic and copies ran while one was open for 8% of the time, Pallas kernels for 5%

profile of v2, /device:TPU:0, one launch (start us, length us, event | category | flops | bytes accessed | tf_op | source)
XLA Modules:
  0.0 195.1 jit_solution(12203165414194446404)
XLA Ops:
  5.4 11.7 %attention.1 = (bf16[256,512]{1,0:T(8,128)(2,1)S(1)}, bf16[256,512]{1,0:T(8,128)(2,1)S(1)}, f32[256,128]{1,0:T(8,128)S(1)}, f32[256,128]{1,0:T(8,128)S(1)}) custom-call(s32[1]{0:T(128)S(6)} %copy.34.start_ref, s32[2,16]{1,0:T(2,128)S(1)} %pad_add_fusion.place_ref, bf16[256,512]{1,0:T(8,128)(2,1)S(1)} %copy-done.3, bf16[1,8192,256]{2,1,0:T(8,128)(2,1)S(1)} %copy-done.1, ...), custom_call_target="tpu_custom_call" | custom-call | tf_op jit(solution)/shard_map/attention/pallas_call | solution.py:110
  17.1 5.8 %copy-done = bf16[512,16384]{1,0:T(8,128)(2,1)S(1)} copy-done((bf16[512,16384]{1,0:T(8,128)(2,1)S(1)}, bf16[512,16384]{1,0:T(8,128)(2,1)}, u32[]{:S(2)}) %copy-start) | copy-done | bytes 16777240
  22.8 3.1 %project.4 = (bf16[128,4096]{1,0:T(8,128)(2,1)S(1)}, bf16[128,4096]{1,0:T(8,128)(2,1)}) custom-call(bf16[256,512]{1,0:T(8,128)(2,1)S(1)} %get-tuple-element.14.attn_ref, bf16[512,16384]{1,0:T(8,128)(2,1)S(1)} %copy-done, f32[256,128]{1,0:T(8,128)S(1)} %get-tuple-element.15.limit_ref), custom_call_target="tpu_custom_call" | custom-call | flops 1073741824 | bytes 6553600 | tf_op jit(solution)/shard_map/project/pallas_call | solution.py:156
  26.4 3.1 %project.7 = (bf16[128,4096]{1,0:T(8,128)(2,1)S(1)}, bf16[128,4096]{1,0:T(8,128)(2,1)}) custom-call(bf16[256,512]{1,0:T(8,128)(2,1)S(1)} %get-tuple-element.18.attn_ref, bf16[512,16384]{1,0:T(8,128)(2,1)S(1)} %copy-done, f32[256,128]{1,0:T(8,128)S(1)} %get-tuple-element.19.limit_ref), custom_call_target="tpu_custom_call" | custom-call | flops 1073741824 | bytes 6553600 | tf_op jit(solution)/shard_map/project/pallas_call | solution.py:156
  29.6 3.2 %project.6 = (bf16[128,4096]{1,0:T(8,128)(2,1)S(1)}, bf16[128,4096]{1,0:T(8,128)(2,1)}) custom-call(bf16[256,512]{1,0:T(8,128)(2,1)S(1)} %get-tuple-element.18.attn_ref, bf16[512,16384]{1,0:T(8,128)(2,1)S(1)} %copy-done, f32[256,128]{1,0:T(8,128)S(1)} %get-tuple-element.19.limit_ref), custom_call_target="tpu_custom_call" | custom-call | flops 1073741824 | bytes 6553600 | tf_op jit(solution)/shard_map/project/pallas_call | solution.py:156
  33.2 3.1 %project.5 = (bf16[128,4096]{1,0:T(8,128)(2,1)S(1)}, bf16[128,4096]{1,0:T(8,128)(2,1)}) custom-call(bf16[256,512]{1,0:T(8,128)(2,1)S(1)} %get-tuple-element.18.attn_ref, bf16[512,16384]{1,0:T(8,128)(2,1)S(1)} %copy-done, f32[256,128]{1,0:T(8,128)S(1)} %get-tuple-element.19.limit_ref), custom_call_target="tpu_custom_call" | custom-call | flops 1073741824 | bytes 6553600 | tf_op jit(solution)/shard_map/project/pallas_call | solution.py:156
  38.9 3.1 %collective-permute-start.1 = (bf16[64,4096]{1,0:T(8,128)(2,1)S(1)}, bf16[64,4096]{1,0:T(8,128)(2,1)S(1)}, u32[]{:S(2)}, u32[]{:S(2)}) collective-permute-start(bf16[64,4096]{1,0:T(8,128)(2,1)S(1)} %get-tuple-element.31), channel_id=1, source_target_pairs={{0,4},{1,5},{2,6},{3,7},{4,0},{5,1},{6,2},{7,3},{8,12},{9,13},{10,... | collective-permute-start | bytes 1572872 | tf_op jit(solution)/shard_map/ppermute | solution.py:200
  50.1 4.0 %collective-permute-done.1 = bf16[64,4096]{1,0:T(8,128)(2,1)S(1)} collective-permute-done((bf16[64,4096]{1,0:T(8,128)(2,1)S(1)}, bf16[64,4096]{1,0:T(8,128)(2,1)S(1)}, u32[]{:S(2)}, u32[]{:S(2)}) %collective-permute-start.1) | collective-permute-done | bytes 524320 | tf_op jit(solution)/shard_map/ppermute | solution.py:200
  58.6 11.0 %collective-permute-done.9 = bf16[64,4096]{1,0:T(8,128)(2,1)S(1)} collective-permute-done((bf16[64,4096]{1,0:T(8,128)(2,1)S(1)}, bf16[64,4096]{1,0:T(8,128)(2,1)S(1)}, u32[]{:S(2)}, u32[]{:S(2)}) %collective-permute-start.9) | collective-permute-done | bytes 524320 | tf_op jit(solution)/shard_map/ppermute | solution.py:200
  69.8 11.0 %collective-permute-done.5 = bf16[64,4096]{1,0:T(8,128)(2,1)S(1)} collective-permute-done((bf16[64,4096]{1,0:T(8,128)(2,1)S(1)}, bf16[64,4096]{1,0:T(8,128)(2,1)S(1)}, u32[]{:S(2)}, u32[]{:S(2)}) %collective-permute-start.5) | collective-permute-done | bytes 524320 | tf_op jit(solution)/shard_map/ppermute | solution.py:200
  81.0 4.1 %collective-permute-done.2 = bf16[32,4096]{1,0:T(8,128)(2,1)S(1)} collective-permute-done((bf16[32,4096]{1,0:T(8,128)(2,1)S(1)}, bf16[32,4096]{1,0:T(8,128)(2,1)S(1)}, u32[]{:S(2)}, u32[]{:S(2)}) %collective-permute-start.2) | collective-permute-done | bytes 262176 | tf_op jit(solution)/shard_map/ppermute | solution.py:200
  85.2 2.7 %collective-permute-start.3 = (bf16[16,4096]{1,0:T(8,128)(2,1)S(1)}, bf16[16,4096]{1,0:T(8,128)(2,1)S(1)}, u32[]{:S(2)}, u32[]{:S(2)}) collective-permute-start(bf16[16,4096]{1,0:T(8,128)(2,1)S(1)} %add_convert_fusion.22), channel_id=1, source_target_pairs={{0,8},{1,9},{2,10},{3,11},{4,12},{5,13},{6,14},{7,15},{8,0},{9,1},... | collective-permute-start | bytes 393224 | tf_op jit(solution)/shard_map/ppermute | solution.py:200
  88.3 2.7 %collective-permute-start.11 = (bf16[16,4096]{1,0:T(8,128)(2,1)S(1)}, bf16[16,4096]{1,0:T(8,128)(2,1)S(1)}, u32[]{:S(2)}, u32[]{:S(2)}) collective-permute-start(bf16[16,4096]{1,0:T(8,128)(2,1)S(1)} %add_convert_fusion.18), channel_id=1, source_target_pairs={{0,8},{1,9},{2,10},{3,11},{4,12},{5,13},{6,14},{7,15},{8,0},{9,1},... | collective-permute-start | bytes 393224 | tf_op jit(solution)/shard_map/ppermute | solution.py:200
  91.9 10.9 %collective-permute-done.3 = bf16[16,4096]{1,0:T(8,128)(2,1)S(1)} collective-permute-done((bf16[16,4096]{1,0:T(8,128)(2,1)S(1)}, bf16[16,4096]{1,0:T(8,128)(2,1)S(1)}, u32[]{:S(2)}, u32[]{:S(2)}) %collective-permute-start.3) | collective-permute-done | bytes 131104 | tf_op jit(solution)/shard_map/ppermute | solution.py:200
  102.8 2.8 %collective-permute-done.15 = bf16[16,4096]{1,0:T(8,128)(2,1)S(1)} collective-permute-done((bf16[16,4096]{1,0:T(8,128)(2,1)S(1)}, bf16[16,4096]{1,0:T(8,128)(2,1)S(1)}, u32[]{:S(2)}, u32[]{:S(2)}) %collective-permute-start.15) | collective-permute-done | bytes 131104 | tf_op jit(solution)/shard_map/ppermute | solution.py:200
  105.7 2.7 %collective-permute-done.11 = bf16[16,4096]{1,0:T(8,128)(2,1)S(1)} collective-permute-done((bf16[16,4096]{1,0:T(8,128)(2,1)S(1)}, bf16[16,4096]{1,0:T(8,128)(2,1)S(1)}, u32[]{:S(2)}, u32[]{:S(2)}) %collective-permute-start.11) | collective-permute-done | bytes 131104 | tf_op jit(solution)/shard_map/ppermute | solution.py:200
  112.6 2.9 %collective-permute-start.28 = (bf16[16,4096]{1,0:T(8,128)(2,1)S(1)}, bf16[16,4096]{1,0:T(8,128)(2,1)S(1)}, u32[]{:S(2)}, u32[]{:S(2)}) collective-permute-start(bf16[16,4096]{1,0:T(8,128)(2,1)S(1)} %get-tuple-element.51), channel_id=1, source_target_pairs={{0,8},{1,9},{2,10},{3,11},{4,12},{5,13},{6,14},{7,15},{8,0},{9,1},... | collective-permute-start | bytes 393224 | tf_op jit(solution)/shard_map/ppermute | solution.py:200
  115.5 2.9 %collective-permute-start.20 = (bf16[16,4096]{1,0:T(8,128)(2,1)S(1)}, bf16[16,4096]{1,0:T(8,128)(2,1)S(1)}, u32[]{:S(2)}, u32[]{:S(2)}) collective-permute-start(bf16[16,4096]{1,0:T(8,128)(2,1)S(1)} %get-tuple-element.53), channel_id=1, source_target_pairs={{0,8},{1,9},{2,10},{3,11},{4,12},{5,13},{6,14},{7,15},{8,0},{9,1},... | collective-permute-start | bytes 393224 | tf_op jit(solution)/shard_map/ppermute | solution.py:200
  118.4 10.9 %collective-permute-done.16 = bf16[16,4096]{1,0:T(8,128)(2,1)S(1)} collective-permute-done((bf16[16,4096]{1,0:T(8,128)(2,1)S(1)}, bf16[16,4096]{1,0:T(8,128)(2,1)S(1)}, u32[]{:S(2)}, u32[]{:S(2)}) %collective-permute-start.16) | collective-permute-done | bytes 131104 | tf_op jit(solution)/shard_map/ppermute | solution.py:200
  132.2 2.8 %collective-permute-done.24 = bf16[16,4096]{1,0:T(8,128)(2,1)S(1)} collective-permute-done((bf16[16,4096]{1,0:T(8,128)(2,1)S(1)}, bf16[16,4096]{1,0:T(8,128)(2,1)S(1)}, u32[]{:S(2)}, u32[]{:S(2)}) %collective-permute-start.24) | collective-permute-done | bytes 131104 | tf_op jit(solution)/shard_map/ppermute | solution.py:200
  144.6 4.0 %collective-permute-done.25 = bf16[32,4096]{1,0:T(8,128)(2,1)S(1)} collective-permute-done((bf16[32,4096]{1,0:T(8,128)(2,1)S(1)}, bf16[32,4096]{1,0:T(8,128)(2,1)S(1)}, u32[]{:S(2)}, u32[]{:S(2)}) %collective-permute-start.25) | collective-permute-done | bytes 262176 | tf_op jit(solution)/shard_map/ppermute | solution.py:200
  150.2 4.0 %collective-permute-done.21 = bf16[32,4096]{1,0:T(8,128)(2,1)S(1)} collective-permute-done((bf16[32,4096]{1,0:T(8,128)(2,1)S(1)}, bf16[32,4096]{1,0:T(8,128)(2,1)S(1)}, u32[]{:S(2)}, u32[]{:S(2)}) %collective-permute-start.21) | collective-permute-done | bytes 262176 | tf_op jit(solution)/shard_map/ppermute | solution.py:200
  156.0 23.4 %collective-permute-done.22 = bf16[64,4096]{1,0:T(8,128)(2,1)S(1)} collective-permute-done((bf16[64,4096]{1,0:T(8,128)(2,1)S(1)}, bf16[64,4096]{1,0:T(8,128)(2,1)S(1)}, u32[]{:S(2)}, u32[]{:S(2)}) %collective-permute-start.22) | collective-permute-done | bytes 524320 | tf_op jit(solution)/shard_map/ppermute | solution.py:200
  191.5 3.6 %pad_maximum_fusion = bf16[256,16384]{1,0:T(8,128)(2,1)} fusion(bf16[256,4096]{1,0:T(8,128)(2,1)S(1)} %bitcast.24, bf16[256,4096]{1,0:T(8,128)(2,1)S(1)} %bitcast.23, bf16[256,4096]{1,0:T(8,128)(2,1)S(1)} %bitcast.22, bf16[256,4096]{1,0:T(8,128)(2,1)S(1)} %bitcast.25), kind=kLoop, calls=%fused_computation | loop fusion | flops 33554432 | bytes 16777216 | tf_op jit(solution)/shard_map/concatenate | solution.py:243
  (141 shorter events, 53.8 us)
Async XLA Ops:
  26.0 11.2 %collective-permute-start = (bf16[128,4096]{1,0:T(8,128)(2,1)}, bf16[128,4096]{1,0:T(8,128)(2,1)}, u32[]{:S(2)}, u32[]{:S(2)}) collective-permute-start(bf16[128,4096]{1,0:T(8,128)(2,1)} %get-tuple-element.17), channel_id=1, source_target_pairs={{0,1},{1,0},{2,3},{3,2},{4,5},{5,4},{6,7},{7,6},{8,9},{9,8},{10,11... | collective-permute-start | bytes 3145736 | tf_op jit(solution)/shard_map/ppermute | solution.py:200
  29.5 12.5 %collective-permute-start.12 = (bf16[128,4096]{1,0:T(8,128)(2,1)}, bf16[128,4096]{1,0:T(8,128)(2,1)}, u32[]{:S(2)}, u32[]{:S(2)}) collective-permute-start(bf16[128,4096]{1,0:T(8,128)(2,1)} %get-tuple-element.25), channel_id=1, source_target_pairs={{0,1},{1,0},{2,3},{3,2},{4,5},{5,4},{6,7},{7,6},{8,9},{9,8},{10,11... | collective-permute-start | bytes 3145736 | tf_op jit(solution)/shard_map/ppermute | solution.py:200
  32.8 12.3 %collective-permute-start.8 = (bf16[128,4096]{1,0:T(8,128)(2,1)}, bf16[128,4096]{1,0:T(8,128)(2,1)}, u32[]{:S(2)}, u32[]{:S(2)}) collective-permute-start(bf16[128,4096]{1,0:T(8,128)(2,1)} %get-tuple-element.23), channel_id=1, source_target_pairs={{0,1},{1,0},{2,3},{3,2},{4,5},{5,4},{6,7},{7,6},{8,9},{9,8},{10,11... | collective-permute-start | bytes 3145736 | tf_op jit(solution)/shard_map/ppermute | solution.py:200
  38.9 15.2 %collective-permute-start.1 = (bf16[64,4096]{1,0:T(8,128)(2,1)S(1)}, bf16[64,4096]{1,0:T(8,128)(2,1)S(1)}, u32[]{:S(2)}, u32[]{:S(2)}) collective-permute-start(bf16[64,4096]{1,0:T(8,128)(2,1)S(1)} %get-tuple-element.31), channel_id=1, source_target_pairs={{0,4},{1,5},{2,6},{3,7},{4,0},{5,1},{6,2},{7,3},{8,12},{9,13},{10,... | collective-permute-start | bytes 1572872 | tf_op jit(solution)/shard_map/ppermute | solution.py:200
  43.5 14.9 %collective-permute-start.13 = (bf16[64,4096]{1,0:T(8,128)(2,1)S(1)}, bf16[64,4096]{1,0:T(8,128)(2,1)S(1)}, u32[]{:S(2)}, u32[]{:S(2)}) collective-permute-start(bf16[64,4096]{1,0:T(8,128)(2,1)S(1)} %get-tuple-element.37), channel_id=1, source_target_pairs={{0,2},{1,3},{2,0},{3,1},{4,6},{5,7},{6,4},{7,5},{8,10},{9,11},{10,... | collective-permute-start | bytes 1572872 | tf_op jit(solution)/shard_map/ppermute | solution.py:200
  46.5 23.1 %collective-permute-start.9 = (bf16[64,4096]{1,0:T(8,128)(2,1)S(1)}, bf16[64,4096]{1,0:T(8,128)(2,1)S(1)}, u32[]{:S(2)}, u32[]{:S(2)}) collective-permute-start(bf16[64,4096]{1,0:T(8,128)(2,1)S(1)} %get-tuple-element.35), channel_id=1, source_target_pairs={{0,2},{1,3},{2,0},{3,1},{4,6},{5,7},{6,4},{7,5},{8,10},{9,11},{10,... | collective-permute-start | bytes 1572872 | tf_op jit(solution)/shard_map/ppermute | solution.py:200
  48.5 32.3 %collective-permute-start.5 = (bf16[64,4096]{1,0:T(8,128)(2,1)S(1)}, bf16[64,4096]{1,0:T(8,128)(2,1)S(1)}, u32[]{:S(2)}, u32[]{:S(2)}) collective-permute-start(bf16[64,4096]{1,0:T(8,128)(2,1)S(1)} %get-tuple-element.33), channel_id=1, source_target_pairs={{0,2},{1,3},{2,0},{3,1},{4,6},{5,7},{6,4},{7,5},{8,10},{9,11},{10,... | collective-permute-start | bytes 1572872 | tf_op jit(solution)/shard_map/ppermute | solution.py:200
  54.2 30.9 %collective-permute-start.2 = (bf16[32,4096]{1,0:T(8,128)(2,1)S(1)}, bf16[32,4096]{1,0:T(8,128)(2,1)S(1)}, u32[]{:S(2)}, u32[]{:S(2)}) collective-permute-start(bf16[32,4096]{1,0:T(8,128)(2,1)S(1)} %get-tuple-element.39), channel_id=1, source_target_pairs={{0,2},{1,3},{2,0},{3,1},{4,6},{5,7},{6,4},{7,5},{8,10},{9,11},{10,... | collective-permute-start | bytes 786440 | tf_op jit(solution)/shard_map/ppermute | solution.py:200
  58.5 29.4 %collective-permute-start.14 = (bf16[32,4096]{1,0:T(8,128)(2,1)S(1)}, bf16[32,4096]{1,0:T(8,128)(2,1)S(1)}, u32[]{:S(2)}, u32[]{:S(2)}) collective-permute-start(bf16[32,4096]{1,0:T(8,128)(2,1)S(1)} %get-tuple-element.45), channel_id=1, source_target_pairs={{0,4},{1,5},{2,6},{3,7},{4,0},{5,1},{6,2},{7,3},{8,12},{9,13},{10,... | collective-permute-start | bytes 786440 | tf_op jit(solution)/shard_map/ppermute | solution.py:200
  69.7 18.6 %collective-permute-start.10 = (bf16[32,4096]{1,0:T(8,128)(2,1)S(1)}, bf16[32,4096]{1,0:T(8,128)(2,1)S(1)}, u32[]{:S(2)}, u32[]{:S(2)}) collective-permute-start(bf16[32,4096]{1,0:T(8,128)(2,1)S(1)} %get-tuple-element.43), channel_id=1, source_target_pairs={{0,4},{1,5},{2,6},{3,7},{4,0},{5,1},{6,2},{7,3},{8,12},{9,13},{10,... | collective-permute-start | bytes 786440 | tf_op jit(solution)/shard_map/ppermute | solution.py:200
  85.2 17.6 %collective-permute-start.3 = (bf16[16,4096]{1,0:T(8,128)(2,1)S(1)}, bf16[16,4096]{1,0:T(8,128)(2,1)S(1)}, u32[]{:S(2)}, u32[]{:S(2)}) collective-permute-start(bf16[16,4096]{1,0:T(8,128)(2,1)S(1)} %add_convert_fusion.22), channel_id=1, source_target_pairs={{0,8},{1,9},{2,10},{3,11},{4,12},{5,13},{6,14},{7,15},{8,0},{9,1},... | collective-permute-start | bytes 393224 | tf_op jit(solution)/shard_map/ppermute | solution.py:200
  87.9 17.7 %collective-permute-start.15 = (bf16[16,4096]{1,0:T(8,128)(2,1)S(1)}, bf16[16,4096]{1,0:T(8,128)(2,1)S(1)}, u32[]{:S(2)}, u32[]{:S(2)}) collective-permute-start(bf16[16,4096]{1,0:T(8,128)(2,1)S(1)} %add_convert_fusion.16), channel_id=1, source_target_pairs={{0,8},{1,9},{2,10},{3,11},{4,12},{5,13},{6,14},{7,15},{8,0},{9,1},... | collective-permute-start | bytes 393224 | tf_op jit(solution)/shard_map/ppermute | solution.py:200
  88.3 20.1 %collective-permute-start.11 = (bf16[16,4096]{1,0:T(8,128)(2,1)S(1)}, bf16[16,4096]{1,0:T(8,128)(2,1)S(1)}, u32[]{:S(2)}, u32[]{:S(2)}) collective-permute-start(bf16[16,4096]{1,0:T(8,128)(2,1)S(1)} %add_convert_fusion.18), channel_id=1, source_target_pairs={{0,8},{1,9},{2,10},{3,11},{4,12},{5,13},{6,14},{7,15},{8,0},{9,1},... | collective-permute-start | bytes 393224 | tf_op jit(solution)/shard_map/ppermute | solution.py:200
  91.0 19.0 %collective-permute-start.7 = (bf16[16,4096]{1,0:T(8,128)(2,1)S(1)}, bf16[16,4096]{1,0:T(8,128)(2,1)S(1)}, u32[]{:S(2)}, u32[]{:S(2)}) collective-permute-start(bf16[16,4096]{1,0:T(8,128)(2,1)S(1)} %add_convert_fusion.20), channel_id=1, source_target_pairs={{0,8},{1,9},{2,10},{3,11},{4,12},{5,13},{6,14},{7,15},{8,0},{9,1},... | collective-permute-start | bytes 393224 | tf_op jit(solution)/shard_map/ppermute | solution.py:200
  112.5 16.7 %collective-permute-start.16 = (bf16[16,4096]{1,0:T(8,128)(2,1)S(1)}, bf16[16,4096]{1,0:T(8,128)(2,1)S(1)}, u32[]{:S(2)}, u32[]{:S(2)}) collective-permute-start(bf16[16,4096]{1,0:T(8,128)(2,1)S(1)} %get-tuple-element.46), channel_id=1, source_target_pairs={{0,8},{1,9},{2,10},{3,11},{4,12},{5,13},{6,14},{7,15},{8,0},{9,1},... | collective-permute-start | bytes 393224 | tf_op jit(solution)/shard_map/ppermute | solution.py:200
  112.6 19.5 %collective-permute-start.28 = (bf16[16,4096]{1,0:T(8,128)(2,1)S(1)}, bf16[16,4096]{1,0:T(8,128)(2,1)S(1)}, u32[]{:S(2)}, u32[]{:S(2)}) collective-permute-start(bf16[16,4096]{1,0:T(8,128)(2,1)S(1)} %get-tuple-element.51), channel_id=1, source_target_pairs={{0,8},{1,9},{2,10},{3,11},{4,12},{5,13},{6,14},{7,15},{8,0},{9,1},... | collective-permute-start | bytes 393224 | tf_op jit(solution)/shard_map/ppermute | solution.py:200
  115.5 19.5 %collective-permute-start.24 = (bf16[16,4096]{1,0:T(8,128)(2,1)S(1)}, bf16[16,4096]{1,0:T(8,128)(2,1)S(1)}, u32[]{:S(2)}, u32[]{:S(2)}) collective-permute-start(bf16[16,4096]{1,0:T(8,128)(2,1)S(1)} %get-tuple-element.52), channel_id=1, source_target_pairs={{0,8},{1,9},{2,10},{3,11},{4,12},{5,13},{6,14},{7,15},{8,0},{9,1},... | collective-permute-start | bytes 393224 | tf_op jit(solution)/shard_map/ppermute | solution.py:200
  115.5 21.8 %collective-permute-start.20 = (bf16[16,4096]{1,0:T(8,128)(2,1)S(1)}, bf16[16,4096]{1,0:T(8,128)(2,1)S(1)}, u32[]{:S(2)}, u32[]{:S(2)}) collective-permute-start(bf16[16,4096]{1,0:T(8,128)(2,1)S(1)} %get-tuple-element.53), channel_id=1, source_target_pairs={{0,8},{1,9},{2,10},{3,11},{4,12},{5,13},{6,14},{7,15},{8,0},{9,1},... | collective-permute-start | bytes 393224 | tf_op jit(solution)/shard_map/ppermute | solution.py:200
  135.0 13.6 %collective-permute-start.25 = (bf16[32,4096]{1,0:T(8,128)(2,1)S(1)}, bf16[32,4096]{1,0:T(8,128)(2,1)S(1)}, u32[]{:S(2)}, u32[]{:S(2)}) collective-permute-start(bf16[32,4096]{1,0:T(8,128)(2,1)S(1)} %pad_maximum_fusion.11), channel_id=1, source_target_pairs={{0,4},{1,5},{2,6},{3,7},{4,0},{5,1},{6,2},{7,3},{8,12},{9,13},{10,... | collective-permute-start | bytes 786440 | tf_op jit(solution)/shard_map/ppermute | solution.py:200
  137.4 16.8 %collective-permute-start.21 = (bf16[32,4096]{1,0:T(8,128)(2,1)S(1)}, bf16[32,4096]{1,0:T(8,128)(2,1)S(1)}, u32[]{:S(2)}, u32[]{:S(2)}) collective-permute-start(bf16[32,4096]{1,0:T(8,128)(2,1)S(1)} %pad_maximum_fusion.10), channel_id=1, source_target_pairs={{0,4},{1,5},{2,6},{3,7},{4,0},{5,1},{6,2},{7,3},{8,12},{9,13},{10,... | collective-permute-start | bytes 786440 | tf_op jit(solution)/shard_map/ppermute | solution.py:200
  138.9 41.4 %collective-permute-start.18 = (bf16[64,4096]{1,0:T(8,128)(2,1)S(1)}, bf16[64,4096]{1,0:T(8,128)(2,1)S(1)}, u32[]{:S(2)}, u32[]{:S(2)}) collective-permute-start(bf16[64,4096]{1,0:T(8,128)(2,1)S(1)} %pad_maximum_fusion.5), channel_id=1, source_target_pairs={{0,4},{1,5},{2,6},{3,7},{4,0},{5,1},{6,2},{7,3},{8,12},{9,13},{10,... | collective-permute-start | bytes 1572872 | tf_op jit(solution)/shard_map/ppermute | solution.py:200
  143.0 37.1 %collective-permute-start.30 = (bf16[64,4096]{1,0:T(8,128)(2,1)S(1)}, bf16[64,4096]{1,0:T(8,128)(2,1)S(1)}, u32[]{:S(2)}, u32[]{:S(2)}) collective-permute-start(bf16[64,4096]{1,0:T(8,128)(2,1)S(1)} %pad_maximum_fusion.8), channel_id=1, source_target_pairs={{0,2},{1,3},{2,0},{3,1},{4,6},{5,7},{6,4},{7,5},{8,10},{9,11},{10,... | collective-permute-start | bytes 1572872 | tf_op jit(solution)/shard_map/ppermute | solution.py:200
  148.7 30.8 %collective-permute-start.26 = (bf16[64,4096]{1,0:T(8,128)(2,1)S(1)}, bf16[64,4096]{1,0:T(8,128)(2,1)S(1)}, u32[]{:S(2)}, u32[]{:S(2)}) collective-permute-start(bf16[64,4096]{1,0:T(8,128)(2,1)S(1)} %pad_maximum_fusion.7), channel_id=1, source_target_pairs={{0,2},{1,3},{2,0},{3,1},{4,6},{5,7},{6,4},{7,5},{8,10},{9,11},{10,... | collective-permute-start | bytes 1572872 | tf_op jit(solution)/shard_map/ppermute | solution.py:200
  154.3 25.1 %collective-permute-start.22 = (bf16[64,4096]{1,0:T(8,128)(2,1)S(1)}, bf16[64,4096]{1,0:T(8,128)(2,1)S(1)}, u32[]{:S(2)}, u32[]{:S(2)}) collective-permute-start(bf16[64,4096]{1,0:T(8,128)(2,1)S(1)} %pad_maximum_fusion.6), channel_id=1, source_target_pairs={{0,2},{1,3},{2,0},{3,1},{4,6},{5,7},{6,4},{7,5},{8,10},{9,11},{10,... | collective-permute-start | bytes 1572872 | tf_op jit(solution)/shard_map/ppermute | solution.py:200
  (19 other events, 169.9 us)

commit v3 on v2

v3 whole, which is shorter than its diff:
```python
import functools

import jax
import jax.numpy as jnp
from jax import lax
from jax.experimental import pallas as pl
from jax.experimental.pallas import tpu as pltpu
from jax.sharding import PartitionSpec as P

CHUNKS = 4
KEY_BLOCK = 2048
TILE = 1024
PUT_COST = 4
CODE_TOP = 448.0
LOG2E = 1.4426950408889634


def powers(exps):
    magnitude = jnp.abs(exps)
    result = jnp.ones(exps.shape, jnp.float32)
    for bit in range(6):
        chosen = (magnitude >> bit) & 1 == 1
        result = result * jnp.where(chosen, jnp.float32(2.0**2**bit), jnp.float32(1.0))
    return jnp.where(exps < 0, 1.0 / result, result)


def partial_kernel(
    start_ref, q_ref, kv_ref, exp_ref, weight_ref, *refs, key_block, heads, head, kinds, orders
):
    n_chunks = len(kinds)
    outs = [(refs[2 * j], refs[2 * j + 1]) for j in range(n_chunks)]
    top_ref, acc_ref, limit_ref, attn_ref, held_ref, stage_ref, in_sems, out_sems = refs[2 * n_chunks :]
    step = pl.program_id(0)
    start = start_ref[0]
    rows = q_ref.shape[0]
    n_orders, n_blocks = len(orders), 2 ** len(orders[0])
    me = lax.axis_index("tp")
    block = rows // n_blocks
    coef = head**-0.5 * LOG2E
    n_tiles, _, tile = held_ref.shape
    lanes = limit_ref.shape[2]
    group = weight_ref.shape[1] // lanes
    per = tile // group
    half = rows // 2

    def weight_copy(t):
        return pltpu.make_async_copy(
            weight_ref.at[:, pl.ds(pl.multiple_of(t * tile, tile), tile)], held_ref.at[t], in_sems.at[t]
        )

    @pl.when(step == 0)
    def _():
        for t in range(n_tiles):
            weight_copy(t).start()
        top_ref[...] = jnp.full_like(top_ref, -1e30)
        acc_ref[...] = jnp.zeros_like(acc_ref)
        limit = powers(exp_ref[0]) * CODE_TOP
        for i in range(n_blocks):
            for o in range(n_orders):
                to = pl.ds(pl.multiple_of(place_of(i ^ me, orders[o]) * block, block), block)
                limit_ref[o, to, :] = limit[i * block : (i + 1) * block]

    def attend(masked):
        keys = kv_ref[0, :, :head]
        ones = jnp.ones((key_block, head), jnp.bfloat16)
        values = jnp.concatenate([kv_ref[0, :, head:], ones], axis=1)
        if masked:
            row = lax.broadcasted_iota(jnp.int32, (rows, key_block), 0)
            col = lax.broadcasted_iota(jnp.int32, (rows, key_block), 1)
            seen = col - row <= start - step * key_block
        for h in range(heads):
            scores = lax.dot_general(
                q_ref[:, h * head : (h + 1) * head],
                keys,
                (((1,), (1,)), ((), ())),
                preferred_element_type=jnp.float32,
            )
            if masked:
                scores = jnp.where(seen, scores, jnp.float32(-1e30))
            before = top_ref[h]
            top = jnp.maximum(before, jnp.max(scores, axis=1, keepdims=True))
            weights = jnp.exp2((scores - top[:, :1]) * coef).astype(jnp.bfloat16)
            fade = jnp.exp2((before - top) * coef)
            got = jnp.dot(weights, values, preferred_element_type=jnp.float32)
            acc_ref[h] = acc_ref[h] * jnp.concatenate([fade, fade], axis=1) + got
            top_ref[h] = top

    first = step * key_block
    past = first + key_block - 1 > start

    @pl.when(jnp.logical_and(past, first <= start + rows - 1))
    def _():
        attend(True)

    @pl.when(jnp.logical_not(past))
    def _():
        attend(False)

    @pl.when(step == pl.num_programs(0) - 1)
    def _():
        for h in range(heads):
            acc = acc_ref[h]
            out = (acc[:, :head] / acc[:, head:]).astype(jnp.bfloat16)
            for i in range(n_blocks):
                for o in range(n_orders):
                    to = pl.ds(pl.multiple_of(place_of(i ^ me, orders[o]) * block, block), block)
                    attn_ref[o, to, h * head : (h + 1) * head] = out[i * block : (i + 1) * block]

        per_chunk = n_tiles // n_chunks
        slots = stage_ref.shape[0]
        waiting = {}
        for t in range(n_tiles):
            j, within = t // per_chunk, t % per_chunk
            slot = t % slots
            weight_copy(t).wait()
            for copy in waiting.pop(slot, ()):
                copy.wait()
            limit = limit_ref[kinds[j]]
            got = jnp.dot(attn_ref[kinds[j]], held_ref[t], preferred_element_type=jnp.float32)
            for b in range(per):
                cut = slice(b * group, (b + 1) * group)
                bound = jnp.broadcast_to(limit[:, t * per + b : t * per + b + 1], (rows, group))
                part = jnp.minimum(jnp.maximum(got[:, cut], -bound), bound)
                stage_ref[slot, :, cut] = part.astype(jnp.bfloat16)
            copies = []
            for side in range(2):
                copies.append(
                    pltpu.make_async_copy(
                        stage_ref.at[slot, pl.ds(side * half, half), :],
                        outs[j][side].at[:, pl.ds(within * tile, tile)],
                        out_sems.at[slot, side],
                    )
                )
                copies[-1].start()
            waiting[slot] = copies
        for copies in waiting.values():
            for copy in copies:
                copy.wait()


def partials(start, queries, cache, term_exp, out_weight, kinds, orders):
    rows, span = queries.shape
    context, head = cache.shape[1], cache.shape[2] // 2
    heads = span // head
    n_orders = len(orders)
    blocks = term_exp.shape[2]
    width = out_weight.shape[1]
    n_tiles = width // TILE
    key_block = min(KEY_BLOCK, context)
    half, cols = rows // 2, width // len(kinds)

    def cache_block(step, start_ref):
        return (0, jnp.minimum(step, (start_ref[0] + rows - 1) // key_block), 0)

    def whole(*shape):
        return pl.BlockSpec(shape, lambda step, start_ref: (0,) * len(shape))

    anywhere = pl.BlockSpec(memory_space=pl.ANY)
    got = pl.pallas_call(
        functools.partial(partial_kernel, key_block=key_block, heads=heads, head=head, kinds=kinds, orders=orders),
        grid_spec=pltpu.PrefetchScalarGridSpec(
            num_scalar_prefetch=1,
            grid=(context // key_block,),
            in_specs=[
                whole(rows, span),
                pl.BlockSpec((1, key_block, 2 * head), cache_block),
                whole(1, rows, blocks),
                anywhere,
            ],
            out_specs=[anywhere] * (2 * len(kinds)),
            scratch_shapes=[
                pltpu.VMEM((heads, rows, head), jnp.float32),
                pltpu.VMEM((heads, rows, 2 * head), jnp.float32),
                pltpu.VMEM((n_orders, rows, blocks), jnp.float32),
                pltpu.VMEM((n_orders, rows, span), jnp.bfloat16),
                pltpu.VMEM((n_tiles, span, TILE), jnp.bfloat16),
                pltpu.VMEM((4, rows, TILE), jnp.bfloat16),
                pltpu.SemaphoreType.DMA((n_tiles,)),
                pltpu.SemaphoreType.DMA((4, 2)),
            ],
        ),
        out_shape=[jax.ShapeDtypeStruct((half, cols), jnp.bfloat16)] * (2 * len(kinds)),
        compiler_params=pltpu.CompilerParams(vmem_limit_bytes=58 << 20),
        name="partials",
    )(start, queries, cache, term_exp, out_weight)
    return [(got[2 * j], got[2 * j + 1]) for j in range(len(kinds))]


def place_of(index, order):
    top = len(order) - 1
    return sum(((index >> b) & 1) << (top - k) for k, b in enumerate(order))


def device_of(place, order):
    top = len(order) - 1
    return sum(((place >> (top - k)) & 1) << b for k, b in enumerate(order))


def put_kernel(source_ref, *refs, first, order, base):
    out_ref, stage_ref, in_sems, out_sems = refs[-4:]
    me = lax.axis_index("tp")
    half, cols = source_ref.shape
    block = 2 * half >> len(order)
    reads, writes = [], []
    for i in range(half // block):
        here = pl.ds(i * block, block)
        to = pl.multiple_of((me ^ device_of(base + i, order)) * block, block)
        reads.append(pltpu.make_async_copy(source_ref.at[here, :], stage_ref.at[here, :], in_sems.at[i]))
        writes.append(
            pltpu.make_async_copy(
                stage_ref.at[here, :], out_ref.at[pl.ds(to, block), pl.ds(first, cols)], out_sems.at[i]
            )
        )
    for read in reads:
        read.start()
    for read, write in zip(reads, writes):
        read.wait()
        write.start()
    for write in writes:
        write.wait()


def put(source, out, first, width, order, base):
    half, cols = source.shape
    n = 2 ** len(order) // 2
    anywhere = pl.BlockSpec(memory_space=pl.ANY)
    given = (source,) + (() if out is None else (out,))
    return pl.pallas_call(
        functools.partial(put_kernel, first=first, order=order, base=base),
        in_specs=[anywhere] * len(given),
        out_specs=anywhere,
        scratch_shapes=[
            pltpu.VMEM((half, cols), source.dtype),
            pltpu.SemaphoreType.DMA((n,)),
            pltpu.SemaphoreType.DMA((n,)),
        ],
        out_shape=jax.ShapeDtypeStruct((2 * half, width), source.dtype),
        input_output_aliases={} if out is None else {1: 0},
        cost_estimate=pl.CostEstimate(flops=0, bytes_accessed=PUT_COST * half * cols, transcendentals=0),
        name="put",
    )(*given)


def scatter_plan(bits):
    last = bits - 1
    far = list(range(2, last))
    plan = [(0, 0), (1, 0), (2, 0), (3, 0), (0, 1), (1, 1)] + [(0, s) for s in far]
    plan += [(2, 1)] + [(1, s) for s in far] + [(3, 1)]
    plan += [(1, last)] + [(2, s) for s in far] + [(0, last), (2, last)] + [(3, s) for s in far] + [(3, last)]
    return plan


def gather_plan(bits):
    last = bits - 1
    far = list(range(last - 1, 1, -1))
    plan = [(1, last), (0, last)] + [(1, s) for s in far]
    plan += [(2, last)] + [(2, s) for s in far] + [(3, last), (1, 1)] + [(3, s) for s in far]
    plan += [(1, 0)] + [(0, s) for s in far] + [(2, 1), (2, 0), (0, 1), (0, 0), (3, 1), (3, 0)]
    return plan


def per_device(queries, cache, offset, out_weight, residual, term_exp, code_exp, gain):
    me = lax.axis_index("tp")
    parts = lax.axis_size("tp")
    bits = parts.bit_length() - 1
    block, width = residual.shape
    blocks = code_exp.shape[1]
    group = width // blocks
    cols = width // CHUNKS

    def flip(x, b):
        return lax.ppermute(x, "tp", [(i, i ^ (1 << b)) for i in range(parts)])

    order_a = list(range(bits))
    order_b = [0] + list(range(2, bits)) + [1]
    kinds = [order_a, order_b]
    uses = [1] + [0] * (CHUNKS - 1)

    state = partials(offset, queries, cache, term_exp, out_weight, uses, kinds)

    def held_back(x, others):
        return lax.optimization_barrier((x,) + tuple(others))[0] if others else x

    def merge(keep, came, last=False):
        if last:
            return keep.astype(jnp.float32) + came.astype(jnp.float32), None
        half = keep.shape[0] // 2
        send = (keep[half:].astype(jnp.float32) + came[half:].astype(jnp.float32)).astype(jnp.bfloat16)
        keep = (keep[:half].astype(jnp.float32) + came[:half].astype(jnp.float32)).astype(jnp.bfloat16)
        return keep, send

    last = bits - 1
    dones = []
    for j, step in scatter_plan(bits):
        keep, send = state[j]
        with jax.named_scope(f"rs{j}{step}"):
            came = held_back(flip(send, kinds[uses[j]][step]), dones[-1:])
            state[j] = merge(keep, came, step == last)
            dones.append(state[j][0 if step == last else 1])
    sums = [state[j][0] for j in range(CHUNKS)]
    summed = jnp.concatenate(sums, axis=1)
    stream = (summed + residual.astype(jnp.float32)).astype(jnp.bfloat16)
    wide = stream.astype(jnp.float32)
    inverse = lax.rsqrt(jnp.mean(wide * wide, axis=1, keepdims=True) + 1e-05)
    exps = lax.dynamic_slice_in_dim(code_exp, me * block, block, 0)
    cap = (powers(exps) * CODE_TOP)[:, :, None]
    normed = (wide * inverse * gain[None, :]).reshape(block, blocks, group)
    mixed = jnp.clip(normed, -cap, cap).reshape(block, width).astype(jnp.bfloat16)

    held = {j: mixed[:, j * cols : (j + 1) * cols] for j in range(CHUNKS)}
    out = None
    dones = []
    for j, step in gather_plan(bits):
        kind = uses[j]
        with jax.named_scope(f"ag{j}{step}"):
            came = flip(held[j], kinds[kind][step])
            if step:
                came = held_back(came, dones[-1:])
                held[j] = jnp.concatenate([held[j], came], axis=0)
                dones.append(held[j])
            else:
                for base, source in ((0, held[j]), (parts // 2, came)):
                    out = put(source, out, j * cols, width, kinds[kind], base)
    return (out, stream)


def solution(mesh):
    in_specs = (
        P("groups", "tp"),
        P("tp", "groups", None),
        P("groups"),
        P("tp", None),
        P(("groups", "tp"), None),
        P("tp", "groups", None),
        P("groups", None),
        P(),
    )
    out_specs = (P("groups", None), P(("groups", "tp"), None))
    return jax.shard_map(
        per_device, mesh=mesh, in_specs=in_specs, out_specs=out_specs, check_vma=False
    )
```

time: 199 us -> 162 us (0.81); the launches traced: 195 us -> 160 us
  waiting for transfers between devices: 103 us -> 68 us
  other arithmetic: 20 us -> 6.21 us
  starting transfers between devices: 32.1 us -> 45.8 us
  Pallas kernels: 24.3 us -> 37.5 us
  local copies, waits for them, and re-layouts: 13.7 us -> 0.74 us
    ppermute x32, waiting for transfers between devices: 103 us -> 68 us  [flip(): return lax.ppermute(x, 'tp', [(i, i ^ 1 << b) for i in range(parts)])]
    ppermute x32, starting transfers between devices: 32.1 us -> 45.8 us  [flip(): return lax.ppermute(x, 'tp', [(i, i ^ 1 << b) for i in range(parts)])]
    pallas_call x5 -> x9, Pallas kernels: 24.3 us -> 37.5 us  [the longest x1 20.7 us: partials(): pl.pallas_call(functools.partial(partial_kernel, key_block=key_block, hea...]
    unnamed x34 -> x18, local copies, waits for them, and re-layouts: 11.4 us -> 0.04 us
    select_n x12 -> x0, other arithmetic: 5.53 us -> none  [from_relative(): shaped = jnp.where(me >> b & 1 == 1, jnp.flip(shaped, axis), shaped)]
    convert_element_type x12, other arithmetic: 6.73 us -> 2.83 us  [the longest x5 2.2 us: merge(): (keep[:half].astype(jnp.float32) + came[:half].astype(jnp.float32)).astyp...]
    concatenate x13 -> x12, other arithmetic: 4.13 us -> 1.54 us  [per_device(): held[j] = jnp.concatenate([held[j], came], axis=0)]
  transfers between devices with their start and end apart: 32 -> 32, of which waited for: 19 -> 15; matrix products, arithmetic and copies ran while one was open for 8% -> 3% of each run, Pallas kernels for 5% -> 9%
where the time goes in v3:
time: 162 us; the launch traced here: 160 us
  waiting for transfers between devices  68 us (42%)
  starting transfers between devices  45.8 us (28%)
  Pallas kernels  37.5 us (23%)
  other arithmetic  6.21 us (4%)
  between operations  1.88 us (1%)
    ppermute x32, waiting for transfers between devices, flip(): return lax.ppermute(x, 'tp', [(i, i ^ 1 << b) for i in range(parts)])  68 us
    ppermute x32, starting transfers between devices, flip(): return lax.ppermute(x, 'tp', [(i, i ^ 1 << b) for i in range(parts)])  45.8 us
    pallas_call x1, Pallas kernels, partials(): pl.pallas_call(functools.partial(partial_kernel, key_block=key_block, hea...  20.7 us
    pallas_call x8, Pallas kernels, put(): pl.pallas_call(functools.partial(put_kernel, first=first, order=order, ba...  16.7 us
  transfers between devices with their start and end apart: 32, of which 15 were waited for; matrix products, arithmetic and copies ran while one was open for 3% of the time, Pallas kernels for 9%

profile of v3, /device:TPU:0, one launch (start us, length us, event | category | flops | bytes accessed | tf_op | source)
XLA Modules:
  0.0 160.1 jit_solution(1162855085319789463)
XLA Ops:
  1.3 20.7 %partials.1 = (bf16[128,4096]{1,0:T(8,128)(2,1)}, bf16[128,4096]{1,0:T(8,128)(2,1)}, bf16[128,4096]{1,0:T(8,128)(2,1)}, bf16[128,4096]{1,0:T(8,128)(2,1)}, bf16[...) custom-call(s32[1]{0:T(128)S(6)} %copy.28.start_ref, ...), custom_call_target="tpu_custom_call" | custom-call | tf_op jit(solution)/shard_map/partials/pallas_call | solution.py:159
  26.5 3.0 %collective-permute-start.1 = (bf16[64,4096]{1,0:T(8,128)(2,1)S(1)}, bf16[64,4096]{1,0:T(8,128)(2,1)S(1)}, u32[]{:S(2)}, u32[]{:S(2)}) collective-permute-start(bf16[64,4096]{1,0:T(8,128)(2,1)S(1)} %get-tuple-element.77), channel_id=1, source_target_pairs={{0,4},{1,5},{2,6},{3,7},{4,0},{5,1},{6,2},{7,3},{8,12},{9,13},{10,... | collective-permute-start | bytes 1572872 | tf_op jit(solution)/shard_map/rs01/ppermute | solution.py:272
  34.1 7.7 %collective-permute-done.1 = bf16[64,4096]{1,0:T(8,128)(2,1)S(1)} collective-permute-done((bf16[64,4096]{1,0:T(8,128)(2,1)S(1)}, bf16[64,4096]{1,0:T(8,128)(2,1)S(1)}, u32[]{:S(2)}, u32[]{:S(2)}) %collective-permute-start.1) | collective-permute-done | bytes 524320 | tf_op jit(solution)/shard_map/rs01/ppermute | solution.py:272
  41.9 2.8 %collective-permute-start.5 = (bf16[32,4096]{1,0:T(8,128)(2,1)S(1)}, bf16[32,4096]{1,0:T(8,128)(2,1)S(1)}, u32[]{:S(2)}, u32[]{:S(2)}) collective-permute-start(bf16[32,4096]{1,0:T(8,128)(2,1)S(1)} %get-tuple-element.87), channel_id=1, source_target_pairs={{0,8},{1,9},{2,10},{3,11},{4,12},{5,13},{6,14},{7,15},{8,0},{9,1},... | collective-permute-start | bytes 786440 | tf_op jit(solution)/shard_map/rs02/ppermute | solution.py:272
  46.5 9.9 %collective-permute-done.5 = bf16[32,4096]{1,0:T(8,128)(2,1)S(1)} collective-permute-done((bf16[32,4096]{1,0:T(8,128)(2,1)S(1)}, bf16[32,4096]{1,0:T(8,128)(2,1)S(1)}, u32[]{:S(2)}, u32[]{:S(2)}) %collective-permute-start.5) | collective-permute-done | bytes 262176 | tf_op jit(solution)/shard_map/rs02/ppermute | solution.py:272
  58.7 3.4 %collective-permute-start.11 = (bf16[16,4096]{1,0:T(8,128)(2,1)S(1)}, bf16[16,4096]{1,0:T(8,128)(2,1)S(1)}, u32[]{:S(2)}, u32[]{:S(2)}) collective-permute-start(bf16[16,4096]{1,0:T(8,128)(2,1)S(1)} %add_convert_fusion.20), channel_id=1, source_target_pairs={{0,8},{1,9},{2,10},{3,11},{4,12},{5,13},{6,14},{7,15},{8,0},{9,1},... | collective-permute-start | bytes 393224 | tf_op jit(solution)/shard_map/rs13/ppermute | solution.py:272
  62.1 5.0 %collective-permute-done.12 = bf16[64,4096]{1,0:T(8,128)(2,1)S(1)} collective-permute-done((bf16[64,4096]{1,0:T(8,128)(2,1)S(1)}, bf16[64,4096]{1,0:T(8,128)(2,1)S(1)}, u32[]{:S(2)}, u32[]{:S(2)}) %collective-permute-start.12) | collective-permute-done | bytes 524320 | tf_op jit(solution)/shard_map/rs31/ppermute | solution.py:272
  67.9 3.7 %collective-permute-start.13 = (bf16[16,4096]{1,0:T(8,128)(2,1)S(1)}, bf16[16,4096]{1,0:T(8,128)(2,1)S(1)}, u32[]{:S(2)}, u32[]{:S(2)}) collective-permute-start(bf16[16,4096]{1,0:T(8,128)(2,1)S(1)} %add_convert_fusion.19), channel_id=1, source_target_pairs={{0,8},{1,9},{2,10},{3,11},{4,12},{5,13},{6,14},{7,15},{8,0},{9,1},... | collective-permute-start | bytes 393224 | tf_op jit(solution)/shard_map/rs23/ppermute | solution.py:272
  71.6 3.9 %collective-permute-done.13 = bf16[16,4096]{1,0:T(8,128)(2,1)S(1)} collective-permute-done((bf16[16,4096]{1,0:T(8,128)(2,1)S(1)}, bf16[16,4096]{1,0:T(8,128)(2,1)S(1)}, u32[]{:S(2)}, u32[]{:S(2)}) %collective-permute-start.13) | collective-permute-done | bytes 131104 | tf_op jit(solution)/shard_map/rs23/ppermute | solution.py:272
  76.3 2.7 %collective-permute-start.15 = (bf16[16,4096]{1,0:T(8,128)(2,1)S(1)}, bf16[16,4096]{1,0:T(8,128)(2,1)S(1)}, u32[]{:S(2)}, u32[]{:S(2)}) collective-permute-start(bf16[16,4096]{1,0:T(8,128)(2,1)S(1)} %add_convert_fusion.16), channel_id=1, source_target_pairs={{0,8},{1,9},{2,10},{3,11},{4,12},{5,13},{6,14},{7,15},{8,0},{9,1},... | collective-permute-start | bytes 393224 | tf_op jit(solution)/shard_map/rs33/ppermute | solution.py:272
  79.7 3.4 %collective-permute-done.15 = bf16[16,4096]{1,0:T(8,128)(2,1)S(1)} collective-permute-done((bf16[16,4096]{1,0:T(8,128)(2,1)S(1)}, bf16[16,4096]{1,0:T(8,128)(2,1)S(1)}, u32[]{:S(2)}, u32[]{:S(2)}) %collective-permute-start.15) | collective-permute-done | bytes 131104 | tf_op jit(solution)/shard_map/rs33/ppermute | solution.py:272
  88.7 6.3 %collective-permute-done.18 = bf16[16,4096]{1,0:T(8,128)(2,1)S(1)} collective-permute-done((bf16[16,4096]{1,0:T(8,128)(2,1)S(1)}, bf16[16,4096]{1,0:T(8,128)(2,1)S(1)}, u32[]{:S(2)}, u32[]{:S(2)}) %collective-permute-start.18) | collective-permute-done | bytes 131104 | tf_op jit(solution)/shard_map/ag13/ppermute | solution.py:272
  95.8 6.5 %collective-permute-done.19 = bf16[32,4096]{1,0:T(8,128)(2,1)S(1)} collective-permute-done((bf16[32,4096]{1,0:T(8,128)(2,1)S(1)}, bf16[32,4096]{1,0:T(8,128)(2,1)S(1)}, u32[]{:S(2)}, u32[]{:S(2)}) %collective-permute-start.19) | collective-permute-done | bytes 262176 | tf_op jit(solution)/shard_map/ag12/ppermute | solution.py:272
  102.4 6.9 %collective-permute-start.16 = (bf16[16,4096]{1,0:T(8,128)(2,1)S(1)}, bf16[16,4096]{1,0:T(8,128)(2,1)S(1)}, u32[]{:S(2)}, u32[]{:S(2)}) collective-permute-start(bf16[16,4096]{1,0:T(8,128)(2,1)S(1)} %get-tuple-element.93), channel_id=1, source_target_pairs={{0,8},{1,9},{2,10},{3,11},{4,12},{5,13},{6,14},{7,15},{8,0},{9,1},... | collective-permute-start | bytes 393224 | tf_op jit(solution)/shard_map/ag33/ppermute | solution.py:272
  111.4 4.0 %collective-permute-done.21 = bf16[32,4096]{1,0:T(8,128)(2,1)S(1)} collective-permute-done((bf16[32,4096]{1,0:T(8,128)(2,1)S(1)}, bf16[32,4096]{1,0:T(8,128)(2,1)S(1)}, u32[]{:S(2)}, u32[]{:S(2)}) %collective-permute-start.21) | collective-permute-done | bytes 262176 | tf_op jit(solution)/shard_map/ag22/ppermute | solution.py:272
  117.8 5.6 %collective-permute-done.23 = bf16[64,4096]{1,0:T(8,128)(2,1)S(1)} collective-permute-done((bf16[64,4096]{1,0:T(8,128)(2,1)S(1)}, bf16[64,4096]{1,0:T(8,128)(2,1)S(1)}, u32[]{:S(2)}, u32[]{:S(2)}) %collective-permute-start.23) | collective-permute-done | bytes 524320 | tf_op jit(solution)/shard_map/ag11/ppermute | solution.py:272
  126.1 3.3 %collective-permute-start.24 = (bf16[64,4096]{1,0:T(8,128)(2,1)S(1)}, bf16[64,4096]{1,0:T(8,128)(2,1)S(1)}, u32[]{:S(2)}, u32[]{:S(2)}) collective-permute-start(bf16[64,4096]{1,0:T(8,128)(2,1)S(1)} %pad_maximum_fusion.6), channel_id=1, source_target_pairs={{0,2},{1,3},{2,0},{3,1},{4,6},{5,7},{6,4},{7,5},{8,10},{9,11},{10,... | collective-permute-start | bytes 1572872 | tf_op jit(solution)/shard_map/ag31/ppermute | solution.py:272
  129.8 4.5 %collective-permute-done.26 = bf16[64,4096]{1,0:T(8,128)(2,1)S(1)} collective-permute-done((bf16[64,4096]{1,0:T(8,128)(2,1)S(1)}, bf16[64,4096]{1,0:T(8,128)(2,1)S(1)}, u32[]{:S(2)}, u32[]{:S(2)}) %collective-permute-start.26) | collective-permute-done | bytes 524320 | tf_op jit(solution)/shard_map/ag01/ppermute | solution.py:272
  134.5 7.5 %collective-permute-done.24 = bf16[64,4096]{1,0:T(8,128)(2,1)S(1)} collective-permute-done((bf16[64,4096]{1,0:T(8,128)(2,1)S(1)}, bf16[64,4096]{1,0:T(8,128)(2,1)S(1)}, u32[]{:S(2)}, u32[]{:S(2)}) %collective-permute-start.24) | collective-permute-done | bytes 524320 | tf_op jit(solution)/shard_map/ag31/ppermute | solution.py:272
  145.2 2.1 %put.9.refs_0_ = bf16[256,16384]{1,0:T(8,128)(2,1)} custom-call(bf16[128,4096]{1,0:T(8,128)(2,1)} %collective-permute-done.31.source_ref, bf16[256,16384]{1,0:T(8,128)(2,1)} %put.8.refs_0_), custom_call_target="tpu_custom_call", output_to_operand_aliasing={{}: (1, {})} | custom-call | bytes 2097152 | tf_op jit(solution)/shard_map/ag10/put/pallas_call | solution.py:228
  147.3 2.1 %put.10.refs_0_ = bf16[256,16384]{1,0:T(8,128)(2,1)} custom-call(bf16[128,4096]{1,0:T(8,128)(2,1)} %copy-done.1, bf16[256,16384]{1,0:T(8,128)(2,1)} %put.9.refs_0_), custom_call_target="tpu_custom_call", output_to_operand_aliasing={{}: (1, {})} | custom-call | bytes 2097152 | tf_op jit(solution)/shard_map/ag20/put/pallas_call | solution.py:228
  149.4 2.1 %put.11.refs_0_ = bf16[256,16384]{1,0:T(8,128)(2,1)} custom-call(bf16[128,4096]{1,0:T(8,128)(2,1)} %collective-permute-done.30.source_ref, bf16[256,16384]{1,0:T(8,128)(2,1)} %put.10.refs_0_), custom_call_target="tpu_custom_call", output_to_operand_aliasing={{}: (1, {})} | custom-call | bytes 2097152 | tf_op jit(solution)/shard_map/ag20/put/pallas_call | solution.py:228
  153.6 2.1 %put.13.refs_0_ = bf16[256,16384]{1,0:T(8,128)(2,1)} custom-call(bf16[128,4096]{1,0:T(8,128)(2,1)} %collective-permute-done.29.source_ref, bf16[256,16384]{1,0:T(8,128)(2,1)} %put.12.refs_0_), custom_call_target="tpu_custom_call", output_to_operand_aliasing={{}: (1, {})} | custom-call | bytes 2097152 | tf_op jit(solution)/shard_map/ag00/put/pallas_call | solution.py:228
  155.7 2.1 %put.14.refs_0_ = bf16[256,16384]{1,0:T(8,128)(2,1)} custom-call(bf16[128,4096]{1,0:T(8,128)(2,1)} %pad_maximum_fusion.3.source_ref, bf16[256,16384]{1,0:T(8,128)(2,1)} %put.13.refs_0_), custom_call_target="tpu_custom_call", output_to_operand_aliasing={{}: (1, {})} | custom-call | bytes 2097152 | tf_op jit(solution)/shard_map/ag30/put/pallas_call | solution.py:228
  (102 shorter events, 36.8 us)
Async XLA Ops:
  23.1 9.2 %collective-permute-start.2 = (bf16[128,4096]{1,0:T(8,128)(2,1)}, bf16[128,4096]{1,0:T(8,128)(2,1)S(1)}, u32[]{:S(2)}, u32[]{:S(2)}) collective-permute-start(bf16[128,4096]{1,0:T(8,128)(2,1)} %get-tuple-element.39), channel_id=1, source_target_pairs={{0,1},{1,0},{2,3},{3,2},{4,5},{5,4},{6,7},{7,6},{8,9},{9,8},{10,11... | collective-permute-start | bytes 3145736 | tf_op jit(solution)/shard_map/rs30/ppermute | solution.py:272
  26.5 15.2 %collective-permute-start.1 = (bf16[64,4096]{1,0:T(8,128)(2,1)S(1)}, bf16[64,4096]{1,0:T(8,128)(2,1)S(1)}, u32[]{:S(2)}, u32[]{:S(2)}) collective-permute-start(bf16[64,4096]{1,0:T(8,128)(2,1)S(1)} %get-tuple-element.77), channel_id=1, source_target_pairs={{0,4},{1,5},{2,6},{3,7},{4,0},{5,1},{6,2},{7,3},{8,12},{9,13},{10,... | collective-permute-start | bytes 1572872 | tf_op jit(solution)/shard_map/rs01/ppermute | solution.py:272
  29.8 14.9 %collective-permute-start.6 = (bf16[64,4096]{1,0:T(8,128)(2,1)S(1)}, bf16[64,4096]{1,0:T(8,128)(2,1)S(1)}, u32[]{:S(2)}, u32[]{:S(2)}) collective-permute-start(bf16[64,4096]{1,0:T(8,128)(2,1)S(1)} %get-tuple-element.79), channel_id=1, source_target_pairs={{0,2},{1,3},{2,0},{3,1},{4,6},{5,7},{6,4},{7,5},{8,10},{9,11},{10,... | collective-permute-start | bytes 1572872 | tf_op jit(solution)/shard_map/rs11/ppermute | solution.py:272
  31.7 26.2 %collective-permute-start.8 = (bf16[64,4096]{1,0:T(8,128)(2,1)S(1)}, bf16[64,4096]{1,0:T(8,128)(2,1)S(1)}, u32[]{:S(2)}, u32[]{:S(2)}) collective-permute-start(bf16[64,4096]{1,0:T(8,128)(2,1)S(1)} %get-tuple-element.75), channel_id=1, source_target_pairs={{0,2},{1,3},{2,0},{3,1},{4,6},{5,7},{6,4},{7,5},{8,10},{9,11},{10,... | collective-permute-start | bytes 1572872 | tf_op jit(solution)/shard_map/rs21/ppermute | solution.py:272
  32.5 34.7 %collective-permute-start.12 = (bf16[64,4096]{1,0:T(8,128)(2,1)S(1)}, bf16[64,4096]{1,0:T(8,128)(2,1)S(1)}, u32[]{:S(2)}, u32[]{:S(2)}) collective-permute-start(bf16[64,4096]{1,0:T(8,128)(2,1)S(1)} %get-tuple-element.80), channel_id=1, source_target_pairs={{0,2},{1,3},{2,0},{3,1},{4,6},{5,7},{6,4},{7,5},{8,10},{9,11},{10,... | collective-permute-start | bytes 1572872 | tf_op jit(solution)/shard_map/rs31/ppermute | solution.py:272
  41.9 14.5 %collective-permute-start.5 = (bf16[32,4096]{1,0:T(8,128)(2,1)S(1)}, bf16[32,4096]{1,0:T(8,128)(2,1)S(1)}, u32[]{:S(2)}, u32[]{:S(2)}) collective-permute-start(bf16[32,4096]{1,0:T(8,128)(2,1)S(1)} %get-tuple-element.87), channel_id=1, source_target_pairs={{0,8},{1,9},{2,10},{3,11},{4,12},{5,13},{6,14},{7,15},{8,0},{9,1},... | collective-permute-start | bytes 786440 | tf_op jit(solution)/shard_map/rs02/ppermute | solution.py:272
  44.8 13.8 %collective-permute-start.10 = (bf16[32,4096]{1,0:T(8,128)(2,1)S(1)}, bf16[32,4096]{1,0:T(8,128)(2,1)S(1)}, u32[]{:S(2)}, u32[]{:S(2)}) collective-permute-start(bf16[32,4096]{1,0:T(8,128)(2,1)S(1)} %get-tuple-element.88), channel_id=1, source_target_pairs={{0,4},{1,5},{2,6},{3,7},{4,0},{5,1},{6,2},{7,3},{8,12},{9,13},{10,... | collective-permute-start | bytes 786440 | tf_op jit(solution)/shard_map/rs12/ppermute | solution.py:272
  56.5 15.1 %collective-permute-start.7 = (bf16[16,4096]{1,0:T(8,128)(2,1)S(1)}, bf16[16,4096]{1,0:T(8,128)(2,1)S(1)}, u32[]{:S(2)}, u32[]{:S(2)}) collective-permute-start(bf16[16,4096]{1,0:T(8,128)(2,1)S(1)} %add_convert_fusion.22), channel_id=1, source_target_pairs={{0,2},{1,3},{2,0},{3,1},{4,6},{5,7},{6,4},{7,5},{8,10},{9,11},{10,... | collective-permute-start | bytes 393224 | tf_op jit(solution)/shard_map/rs03/ppermute | solution.py:272
  58.0 9.8 %collective-permute-start.9 = (bf16[32,4096]{1,0:T(8,128)(2,1)S(1)}, bf16[32,4096]{1,0:T(8,128)(2,1)S(1)}, u32[]{:S(2)}, u32[]{:S(2)}) collective-permute-start(bf16[32,4096]{1,0:T(8,128)(2,1)S(1)} %get-tuple-element.83), channel_id=1, source_target_pairs={{0,4},{1,5},{2,6},{3,7},{4,0},{5,1},{6,2},{7,3},{8,12},{9,13},{10,... | collective-permute-start | bytes 786440 | tf_op jit(solution)/shard_map/rs22/ppermute | solution.py:272
  58.7 9.1 %collective-permute-start.11 = (bf16[16,4096]{1,0:T(8,128)(2,1)S(1)}, bf16[16,4096]{1,0:T(8,128)(2,1)S(1)}, u32[]{:S(2)}, u32[]{:S(2)}) collective-permute-start(bf16[16,4096]{1,0:T(8,128)(2,1)S(1)} %add_convert_fusion.20), channel_id=1, source_target_pairs={{0,8},{1,9},{2,10},{3,11},{4,12},{5,13},{6,14},{7,15},{8,0},{9,1},... | collective-permute-start | bytes 393224 | tf_op jit(solution)/shard_map/rs13/ppermute | solution.py:272
  84.9 10.2 %collective-permute-start.18 = (bf16[16,4096]{1,0:T(8,128)(2,1)S(1)}, bf16[16,4096]{1,0:T(8,128)(2,1)S(1)}, u32[]{:S(2)}, u32[]{:S(2)}) collective-permute-start(bf16[16,4096]{1,0:T(8,128)(2,1)S(1)} %get-tuple-element.91), channel_id=1, source_target_pairs={{0,8},{1,9},{2,10},{3,11},{4,12},{5,13},{6,14},{7,15},{8,0},{9,1},... | collective-permute-start | bytes 393224 | tf_op jit(solution)/shard_map/ag13/ppermute | solution.py:272
  86.7 9.0 %collective-permute-start.20 = (bf16[16,4096]{1,0:T(8,128)(2,1)S(1)}, bf16[16,4096]{1,0:T(8,128)(2,1)S(1)}, u32[]{:S(2)}, u32[]{:S(2)}) collective-permute-start(bf16[16,4096]{1,0:T(8,128)(2,1)S(1)} %get-tuple-element.90), channel_id=1, source_target_pairs={{0,2},{1,3},{2,0},{3,1},{4,6},{5,7},{6,4},{7,5},{8,10},{9,11},{10,... | collective-permute-start | bytes 393224 | tf_op jit(solution)/shard_map/ag03/ppermute | solution.py:272
  87.2 15.1 %collective-permute-start.17 = (bf16[16,4096]{1,0:T(8,128)(2,1)S(1)}, bf16[16,4096]{1,0:T(8,128)(2,1)S(1)}, u32[]{:S(2)}, u32[]{:S(2)}) collective-permute-start(bf16[16,4096]{1,0:T(8,128)(2,1)S(1)} %get-tuple-element.92), channel_id=1, source_target_pairs={{0,8},{1,9},{2,10},{3,11},{4,12},{5,13},{6,14},{7,15},{8,0},{9,1},... | collective-permute-start | bytes 393224 | tf_op jit(solution)/shard_map/ag23/ppermute | solution.py:272
  102.3 13.1 %collective-permute-start.21 = (bf16[32,4096]{1,0:T(8,128)(2,1)S(1)}, bf16[32,4096]{1,0:T(8,128)(2,1)S(1)}, u32[]{:S(2)}, u32[]{:S(2)}) collective-permute-start(bf16[32,4096]{1,0:T(8,128)(2,1)S(1)} %pad_maximum_fusion.10), channel_id=1, source_target_pairs={{0,4},{1,5},{2,6},{3,7},{4,0},{5,1},{6,2},{7,3},{8,12},{9,13},{10,... | collective-permute-start | bytes 786440 | tf_op jit(solution)/shard_map/ag22/ppermute | solution.py:272
  102.4 13.5 %collective-permute-start.16 = (bf16[16,4096]{1,0:T(8,128)(2,1)S(1)}, bf16[16,4096]{1,0:T(8,128)(2,1)S(1)}, u32[]{:S(2)}, u32[]{:S(2)}) collective-permute-start(bf16[16,4096]{1,0:T(8,128)(2,1)S(1)} %get-tuple-element.93), channel_id=1, source_target_pairs={{0,8},{1,9},{2,10},{3,11},{4,12},{5,13},{6,14},{7,15},{8,0},{9,1},... | collective-permute-start | bytes 393224 | tf_op jit(solution)/shard_map/ag33/ppermute | solution.py:272
  109.3 14.8 %collective-permute-start.25 = (bf16[32,4096]{1,0:T(8,128)(2,1)S(1)}, bf16[32,4096]{1,0:T(8,128)(2,1)S(1)}, u32[]{:S(2)}, u32[]{:S(2)}) collective-permute-start(bf16[32,4096]{1,0:T(8,128)(2,1)S(1)} %pad_maximum_fusion.9), channel_id=1, source_target_pairs={{0,8},{1,9},{2,10},{3,11},{4,12},{5,13},{6,14},{7,15},{8,0},{9,1},... | collective-permute-start | bytes 786440 | tf_op jit(solution)/shard_map/ag02/ppermute | solution.py:272
  109.4 14.0 %collective-permute-start.23 = (bf16[64,4096]{1,0:T(8,128)(2,1)S(1)}, bf16[64,4096]{1,0:T(8,128)(2,1)S(1)}, u32[]{:S(2)}, u32[]{:S(2)}) collective-permute-start(bf16[64,4096]{1,0:T(8,128)(2,1)S(1)} %pad_maximum_fusion.4), channel_id=1, source_target_pairs={{0,2},{1,3},{2,0},{3,1},{4,6},{5,7},{6,4},{7,5},{8,10},{9,11},{10,... | collective-permute-start | bytes 1572872 | tf_op jit(solution)/shard_map/ag11/ppermute | solution.py:272
  115.4 14.0 %collective-permute-start.27 = (bf16[64,4096]{1,0:T(8,128)(2,1)S(1)}, bf16[64,4096]{1,0:T(8,128)(2,1)S(1)}, u32[]{:S(2)}, u32[]{:S(2)}) collective-permute-start(bf16[64,4096]{1,0:T(8,128)(2,1)S(1)} %pad_maximum_fusion.5), channel_id=1, source_target_pairs={{0,2},{1,3},{2,0},{3,1},{4,6},{5,7},{6,4},{7,5},{8,10},{9,11},{10,... | collective-permute-start | bytes 1572872 | tf_op jit(solution)/shard_map/ag21/ppermute | solution.py:272
  124.2 10.2 %collective-permute-start.26 = (bf16[64,4096]{1,0:T(8,128)(2,1)S(1)}, bf16[64,4096]{1,0:T(8,128)(2,1)S(1)}, u32[]{:S(2)}, u32[]{:S(2)}) collective-permute-start(bf16[64,4096]{1,0:T(8,128)(2,1)S(1)} %pad_maximum_fusion.7), channel_id=1, source_target_pairs={{0,4},{1,5},{2,6},{3,7},{4,0},{5,1},{6,2},{7,3},{8,12},{9,13},{10,... | collective-permute-start | bytes 1572872 | tf_op jit(solution)/shard_map/ag01/ppermute | solution.py:272
  126.1 19.1 %collective-permute-start.31 = (bf16[128,4096]{1,0:T(8,128)(2,1)S(1)}, bf16[128,4096]{1,0:T(8,128)(2,1)}, u32[]{:S(2)}, u32[]{:S(2)}) collective-permute-start(bf16[128,4096]{1,0:T(8,128)(2,1)S(1)} %pad_maximum_fusion.source_ref), channel_id=1, source_target_pairs={{0,1},{1,0},{2,3},{3,2},{4,5},{5,4},{6,7},{7,6},{8,9},{9,8},{10,11... | collective-permute-start | bytes 3145736 | tf_op jit(solution)/shard_map/ag10/ppermute | solution.py:272
  126.1 15.9 %collective-permute-start.24 = (bf16[64,4096]{1,0:T(8,128)(2,1)S(1)}, bf16[64,4096]{1,0:T(8,128)(2,1)S(1)}, u32[]{:S(2)}, u32[]{:S(2)}) collective-permute-start(bf16[64,4096]{1,0:T(8,128)(2,1)S(1)} %pad_maximum_fusion.6), channel_id=1, source_target_pairs={{0,2},{1,3},{2,0},{3,1},{4,6},{5,7},{6,4},{7,5},{8,10},{9,11},{10,... | collective-permute-start | bytes 1572872 | tf_op jit(solution)/shard_map/ag31/ppermute | solution.py:272
  129.5 19.9 %collective-permute-start.30 = (bf16[128,4096]{1,0:T(8,128)(2,1)S(1)}, bf16[128,4096]{1,0:T(8,128)(2,1)}, u32[]{:S(2)}, u32[]{:S(2)}) collective-permute-start(bf16[128,4096]{1,0:T(8,128)(2,1)S(1)} %pad_maximum_fusion.1.source_ref), channel_id=1, source_target_pairs={{0,1},{1,0},{2,3},{3,2},{4,5},{5,4},{6,7},{7,6},{8,9},{9,8},{10,11... | collective-permute-start | bytes 3145736 | tf_op jit(solution)/shard_map/ag20/ppermute | solution.py:272
  134.4 19.2 %collective-permute-start.29 = (bf16[128,4096]{1,0:T(8,128)(2,1)S(1)}, bf16[128,4096]{1,0:T(8,128)(2,1)}, u32[]{:S(2)}, u32[]{:S(2)}) collective-permute-start(bf16[128,4096]{1,0:T(8,128)(2,1)S(1)} %pad_maximum_fusion.2.source_ref), channel_id=1, source_target_pairs={{0,1},{1,0},{2,3},{3,2},{4,5},{5,4},{6,7},{7,6},{8,9},{9,8},{10,11... | collective-permute-start | bytes 3145736 | tf_op jit(solution)/shard_map/ag00/ppermute | solution.py:272
  143.1 14.7 %collective-permute-start.28 = (bf16[128,4096]{1,0:T(8,128)(2,1)}, bf16[128,4096]{1,0:T(8,128)(2,1)}, u32[]{:S(2)}, u32[]{:S(2)}) collective-permute-start(bf16[128,4096]{1,0:T(8,128)(2,1)} %pad_maximum_fusion.3.source_ref), channel_id=1, source_target_pairs={{0,1},{1,0},{2,3},{3,2},{4,5},{5,4},{6,7},{7,6},{8,9},{9,8},{10,11... | collective-permute-start | bytes 3145736 | tf_op jit(solution)/shard_map/ag30/ppermute | solution.py:272
  (17 other events, 127.7 us)

commit v4 on v3

--- a/solution.py
+++ b/solution.py
@@ -7,10 +7,11 @@
 from jax.experimental.pallas import tpu as pltpu
 from jax.sharding import PartitionSpec as P
 
-CHUNKS = 4
+WIDTHS = (4, 5, 4, 3)
+CHUNKS = len(WIDTHS)
+GATHER = (3, 2, 1)
 KEY_BLOCK = 2048
 TILE = 1024
-PUT_COST = 4
 CODE_TOP = 448.0
 LOG2E = 1.4426950408889634
 
@@ -25,7 +26,7 @@
 
 
 def partial_kernel(
-    start_ref, q_ref, kv_ref, exp_ref, weight_ref, *refs, key_block, heads, head, kinds, orders
+    start_ref, q_ref, kv_ref, exp_ref, weight_ref, *refs, key_block, heads, head, kinds, orders, edges
 ):
     n_chunks = len(kinds)
     outs = [(refs[2 * j], refs[2 * j + 1]) for j in range(n_chunks)]
@@ -106,39 +107,34 @@
                     to = pl.ds(pl.multiple_of(place_of(i ^ me, orders[o]) * block, block), block)
                     attn_ref[o, to, h * head : (h + 1) * head] = out[i * block : (i + 1) * block]
 
-        per_chunk = n_tiles // n_chunks
-        slots = stage_ref.shape[0]
-        waiting = {}
-        for t in range(n_tiles):
-            j, within = t // per_chunk, t % per_chunk
-            slot = t % slots
-            weight_copy(t).wait()
-            for copy in waiting.pop(slot, ()):
-                copy.wait()
+        writes = []
+        for j in range(n_chunks):
+            tiles = range(edges[j] // tile, edges[j + 1] // tile)
+            for t in tiles:
+                weight_copy(t).wait()
             limit = limit_ref[kinds[j]]
-            got = jnp.dot(attn_ref[kinds[j]], held_ref[t], preferred_element_type=jnp.float32)
-            for b in range(per):
-                cut = slice(b * group, (b + 1) * group)
-                bound = jnp.broadcast_to(limit[:, t * per + b : t * per + b + 1], (rows, group))
-                part = jnp.minimum(jnp.maximum(got[:, cut], -bound), bound)
-                stage_ref[slot, :, cut] = part.astype(jnp.bfloat16)
-            copies = []
+            rel = attn_ref[kinds[j]]
+            for t in tiles:
+                got = jnp.dot(rel, held_ref[t], preferred_element_type=jnp.float32)
+                for b in range(per):
+                    cut = slice(b * group, (b + 1) * group)
+                    to = slice(t * tile + b * group, t * tile + (b + 1) * group)
+                    bound = jnp.broadcast_to(limit[:, t * per + b : t * per + b + 1], (rows, group))
+                    part = jnp.minimum(jnp.maximum(got[:, cut], -bound), bound)
+                    stage_ref[:, to] = part.astype(jnp.bfloat16)
             for side in range(2):
-                copies.append(
-                    pltpu.make_async_copy(
-                        stage_ref.at[slot, pl.ds(side * half, half), :],
-                        outs[j][side].at[:, pl.ds(within * tile, tile)],
-                        out_sems.at[slot, side],
-                    )
+                write = pltpu.make_async_copy(
+                    stage_ref.at[pl.ds(side * half, half), pl.ds(edges[j], edges[j + 1] - edges[j])],
+                    outs[j][side],
+                    out_sems.at[j, side],
                 )
-                copies[-1].start()
-            waiting[slot] = copies
-        for copies in waiting.values():
-            for copy in copies:
-                copy.wait()
-
-
-def partials(start, queries, cache, term_exp, out_weight, kinds, orders):
+                write.start()
+                writes.append(write)
+        for write in writes:
+            write.wait()
+
+
+def partials(start, queries, cache, term_exp, out_weight, kinds, orders, edges):
     rows, span = queries.shape
     context, head = cache.shape[1], cache.shape[2] // 2
     heads = span // head
@@ -147,7 +143,7 @@
     width = out_weight.shape[1]
     n_tiles = width // TILE
     key_block = min(KEY_BLOCK, context)
-    half, cols = rows // 2, width // len(kinds)
+    half = rows // 2
 
     def cache_block(step, start_ref):
         return (0, jnp.minimum(step, (start_ref[0] + rows - 1) // key_block), 0)
@@ -157,7 +153,8 @@
 
     anywhere = pl.BlockSpec(memory_space=pl.ANY)
     got = pl.pallas_call(
-        functools.partial(partial_kernel, key_block=key_block, heads=heads, head=head, kinds=kinds, orders=orders),
+        functools.partial(partial_kernel, key_block=key_block, heads=heads, head=head, kinds=kinds, orders=orders, edges=edges
+        ),
         grid_spec=pltpu.PrefetchScalarGridSpec(
             num_scalar_prefetch=1,
             grid=(context // key_block,),
@@ -174,12 +171,15 @@
                 pltpu.VMEM((n_orders, rows, blocks), jnp.float32),
                 pltpu.VMEM((n_orders, rows, span), jnp.bfloat16),
                 pltpu.VMEM((n_tiles, span, TILE), jnp.bfloat16),
-                pltpu.VMEM((4, rows, TILE), jnp.bfloat16),
+                pltpu.VMEM((rows, width), jnp.bfloat16),
                 pltpu.SemaphoreType.DMA((n_tiles,)),
-                pltpu.SemaphoreType.DMA((4, 2)),
+                pltpu.SemaphoreType.DMA((len(kinds), 2)),
             ],
         ),
-        out_shape=[jax.ShapeDtypeStruct((half, cols), jnp.bfloat16)] * (2 * len(kinds)),
+        out_shape=[
+            jax.ShapeDtypeStruct((half, edges[i // 2 + 1] - edges[i // 2]), jnp.bfloat16)
+            for i in range(2 * len(kinds))
+        ],
         compiler_params=pltpu.CompilerParams(vmem_limit_bytes=58 << 20),
         name="partials",
     )(start, queries, cache, term_exp, out_weight)
@@ -191,26 +191,19 @@
     return sum(((index >> b) & 1) << (top - k) for k, b in enumerate(order))
 
 
-def device_of(place, order):
-    top = len(order) - 1
-    return sum(((place >> (top - k)) & 1) << b for k, b in enumerate(order))
-
-
-def put_kernel(source_ref, *refs, first, order, base):
-    out_ref, stage_ref, in_sems, out_sems = refs[-4:]
+def put_kernel(*refs, places):
+    n = len(places)
+    out_ref, stages = refs[-3 - n], refs[-2 - n : -2]
+    in_sems, out_sems = refs[-2:]
     me = lax.axis_index("tp")
-    half, cols = source_ref.shape
-    block = 2 * half >> len(order)
     reads, writes = [], []
-    for i in range(half // block):
-        here = pl.ds(i * block, block)
-        to = pl.multiple_of((me ^ device_of(base + i, order)) * block, block)
-        reads.append(pltpu.make_async_copy(source_ref.at[here, :], stage_ref.at[here, :], in_sems.at[i]))
-        writes.append(
-            pltpu.make_async_copy(
-                stage_ref.at[here, :], out_ref.at[pl.ds(to, block), pl.ds(first, cols)], out_sems.at[i]
-            )
-        )
+    for i, (at, side, y, core, first) in enumerate(places):
+        source = refs[at] if side is None else refs[at].at[side]
+        cols = source.shape[-1]
+        y = side if y is None else ((me >> 1) & 1) ^ y
+        there = out_ref.at[:, y, (me & 1) ^ core, :, pl.ds(first, cols)]
+        reads.append(pltpu.make_async_copy(source, stages[i], in_sems.at[i]))
+        writes.append(pltpu.make_async_copy(stages[i], there, out_sems.at[i]))
     for read in reads:
         read.start()
     for read, write in zip(reads, writes):
@@ -220,23 +213,31 @@
         write.wait()
 
 
-def put(source, out, first, width, order, base):
-    half, cols = source.shape
-    n = 2 ** len(order) // 2
+def put(pieces, out, far, block, width):
+    sources, places = [], []
+    for array, y, core, first in pieces:
+        for side in (None,) if y is not None else range(2):
+            places.append((len(sources), side, y, core, first))
+        sources.append(array)
+    n = len(places)
+    sizes = [sources[place[0]].shape[-1] for place in places]
     anywhere = pl.BlockSpec(memory_space=pl.ANY)
-    given = (source,) + (() if out is None else (out,))
+    given = sources + ([] if out is None else [out])
     return pl.pallas_call(
-        functools.partial(put_kernel, first=first, order=order, base=base),
+        functools.partial(put_kernel, places=places),
         in_specs=[anywhere] * len(given),
         out_specs=anywhere,
-        scratch_shapes=[
-            pltpu.VMEM((half, cols), source.dtype),
+        scratch_shapes=[pltpu.VMEM((far, block, cols), sources[0].dtype) for cols in sizes]
+        + [
             pltpu.SemaphoreType.DMA((n,)),
             pltpu.SemaphoreType.DMA((n,)),
         ],
-        out_shape=jax.ShapeDtypeStruct((2 * half, width), source.dtype),
-        input_output_aliases={} if out is None else {1: 0},
-        cost_estimate=pl.CostEstimate(flops=0, bytes_accessed=PUT_COST * half * cols, transcendentals=0),
+        out_shape=jax.ShapeDtypeStruct((far, 2, 2, block, width), sources[0].dtype),
+        input_output_aliases={} if out is None else {len(sources): 0},
+        compiler_params=pltpu.CompilerParams(vmem_limit_bytes=40 << 20),
+        cost_estimate=pl.CostEstimate(
+            flops=0, bytes_accessed=4 * far * block * sum(sizes), transcendentals=0
+        ),
         name="put",
     )(*given)
 
@@ -253,9 +254,10 @@
 def gather_plan(bits):
     last = bits - 1
     far = list(range(last - 1, 1, -1))
-    plan = [(1, last), (0, last)] + [(1, s) for s in far]
-    plan += [(2, last)] + [(2, s) for s in far] + [(3, last), (1, 1)] + [(3, s) for s in far]
-    plan += [(1, 0)] + [(0, s) for s in far] + [(2, 1), (2, 0), (0, 1), (0, 0), (3, 1), (3, 0)]
+    one, two, three = GATHER
+    plan = [(one, last), (0, last)] + [(one, s) for s in far]
+    plan += [(two, last)] + [(two, s) for s in far] + [(one, 1), (three, last)] + [(three, s) for s in far]
+    plan += [(0, s) for s in far] + [(two, 1), (0, 1), (three, 1)]
     return plan
 
 
@@ -266,7 +268,8 @@
     block, width = residual.shape
     blocks = code_exp.shape[1]
     group = width // blocks
-    cols = width // CHUNKS
+    unit = width // sum(WIDTHS)
+    edges = [unit * sum(WIDTHS[:j]) for j in range(CHUNKS + 1)]
 
     def flip(x, b):
         return lax.ppermute(x, "tp", [(i, i ^ (1 << b)) for i in range(parts)])
@@ -276,7 +279,7 @@
     kinds = [order_a, order_b]
     uses = [1] + [0] * (CHUNKS - 1)
 
-    state = partials(offset, queries, cache, term_exp, out_weight, uses, kinds)
+    state = partials(offset, queries, cache, term_exp, out_weight, uses, kinds, edges)
 
     def held_back(x, others):
         return lax.optimization_barrier((x,) + tuple(others))[0] if others else x
@@ -307,21 +310,38 @@
     normed = (wide * inverse * gain[None, :]).reshape(block, blocks, group)
     mixed = jnp.clip(normed, -cap, cap).reshape(block, width).astype(jnp.bfloat16)
 
-    held = {j: mixed[:, j * cols : (j + 1) * cols] for j in range(CHUNKS)}
-    out = None
+    ones = (1,) * (bits - 1)
+    held = {j: mixed[:, edges[j] : edges[j + 1]].reshape(ones + (block, -1)) for j in range(CHUNKS)}
+    far = parts // 4
+
+    def join(x, came, b):
+        upper = (me >> b) & 1 == 1
+        axis = 0 if b == 1 else bits - b
+        return jnp.concatenate([jnp.where(upper, came, x), jnp.where(upper, x, came)], axis=axis)
+
     dones = []
+    pieces = []
+    late = []
     for j, step in gather_plan(bits):
-        kind = uses[j]
+        order = kinds[uses[j]]
         with jax.named_scope(f"ag{j}{step}"):
-            came = flip(held[j], kinds[kind][step])
-            if step:
-                came = held_back(came, dones[-1:])
-                held[j] = jnp.concatenate([held[j], came], axis=0)
+            came = held_back(flip(held[j], order[step]), dones[-1:])
+            if step > 1 or order[step] != 1:
+                held[j] = join(held[j], came, order[step])
                 dones.append(held[j])
             else:
-                for base, source in ((0, held[j]), (parts // 2, came)):
-                    out = put(source, out, j * cols, width, kinds[kind], base)
-    return (out, stream)
+                dones.append(came)
+            if step == 1 and order[step] == 1:
+                for y, x in enumerate((held[j], came)):
+                    x = x.reshape(far, block, -1)
+                    keep = late if y and j == GATHER[-1] else pieces
+                    keep += [(x, y, 0, edges[j]), (flip(x, order[0]), y, 1, edges[j])]
+            elif step == 1:
+                x = held[j].reshape(2, far, block, -1)
+                pieces += [(x, None, 0, edges[j]), (flip(x, order[0]), None, 1, edges[j])]
+    out = put(pieces, None, far, block, width)
+    out = put(late, out, far, block, width)
+    return (out.reshape(parts * block, width), stream)
 
 
 def solution(mesh):

time: 162 us -> 151 us (0.932)
  Pallas kernels: 37.5 us -> 28.5 us
    pallas_call x8 -> x2, Pallas kernels: 16.7 us -> 6.1 us  [put(): pl.pallas_call(functools.partial(put_kernel, places=places), in_specs=[an...]
    ppermute x32 -> x35, waiting for transfers between devices: 68 us -> 67.5 us  [flip(): return lax.ppermute(x, 'tp', [(i, i ^ 1 << b) for i in range(parts)])]
    ppermute x32 -> x35, starting transfers between devices: 45.8 us -> 45.5 us  [flip(): return lax.ppermute(x, 'tp', [(i, i ^ 1 << b) for i in range(parts)])]
  transfers between devices with their start and end apart: 32 -> 35, of which waited for: 15 -> 19; matrix products, arithmetic and copies ran while one was open for 3% -> 4% of each run, Pallas kernels for 9% -> 3%
where the time goes in v4:
time: 151 us
  waiting for transfers between devices  67.5 us (45%)
  starting transfers between devices  45.5 us (30%)
  Pallas kernels  28.5 us (19%)
  other arithmetic  6.64 us (4%)
  between operations  1.8 us (1%)
    ppermute x35, waiting for transfers between devices, flip(): return lax.ppermute(x, 'tp', [(i, i ^ 1 << b) for i in range(parts)])  67.5 us
    ppermute x35, starting transfers between devices, flip(): return lax.ppermute(x, 'tp', [(i, i ^ 1 << b) for i in range(parts)])  45.5 us
    pallas_call x1, Pallas kernels, partials(): pl.pallas_call(functools.partial(partial_kernel, key_block=key_block, hea...  22.4 us
    pallas_call x2, Pallas kernels, put(): pl.pallas_call(functools.partial(put_kernel, places=places), in_specs=[an...  6.1 us
  transfers between devices with their start and end apart: 35, of which 19 were waited for; matrix products, arithmetic and copies ran while one was open for 4% of the time, Pallas kernels for 3%

profile of v4, /device:TPU:0, one launch (start us, length us, event | category | flops | bytes accessed | tf_op | source)
XLA Modules:
  0.0 150.7 jit_solution(3317329082711886219)
XLA Ops:
  1.3 22.4 %partials.1 = (bf16[128,4096]{1,0:T(8,128)(2,1)}, bf16[128,4096]{1,0:T(8,128)(2,1)}, bf16[128,5120]{1,0:T(8,128)(2,1)}, bf16[128,5120]{1,0:T(8,128)(2,1)}, bf16[...) custom-call(s32[1]{0:T(128)S(6)} %copy.16.start_ref, ...), custom_call_target="tpu_custom_call" | custom-call | tf_op jit(solution)/shard_map/partials/pallas_call | solution.py:155
  24.8 1.9 %collective-permute-done = bf16[128,4096]{1,0:T(8,128)(2,1)S(1)} collective-permute-done((bf16[128,4096]{1,0:T(8,128)(2,1)}, bf16[128,4096]{1,0:T(8,128)(2,1)S(1)}, u32[]{:S(2)}, u32[]{:S(2)}) %collective-permute-start) | collective-permute-done | bytes 1048608 | tf_op jit(solution)/shard_map/rs00/ppermute | solution.py:275
  28.2 3.0 %collective-permute-start.1 = (bf16[64,4096]{1,0:T(8,128)(2,1)S(1)}, bf16[64,4096]{1,0:T(8,128)(2,1)S(1)}, u32[]{:S(2)}, u32[]{:S(2)}) collective-permute-start(bf16[64,4096]{1,0:T(8,128)(2,1)S(1)} %get-tuple-element.79), channel_id=1, source_target_pairs={{0,4},{1,5},{2,6},{3,7},{4,0},{5,1},{6,2},{7,3},{8,12},{9,13},{10,... | collective-permute-start | bytes 1572872 | tf_op jit(solution)/shard_map/rs01/ppermute | solution.py:275
  36.9 6.5 %collective-permute-done.1 = bf16[64,4096]{1,0:T(8,128)(2,1)S(1)} collective-permute-done((bf16[64,4096]{1,0:T(8,128)(2,1)S(1)}, bf16[64,4096]{1,0:T(8,128)(2,1)S(1)}, u32[]{:S(2)}, u32[]{:S(2)}) %collective-permute-start.1) | collective-permute-done | bytes 524320 | tf_op jit(solution)/shard_map/rs01/ppermute | solution.py:275
  43.6 2.8 %collective-permute-start.5 = (bf16[32,4096]{1,0:T(8,128)(2,1)S(1)}, bf16[32,4096]{1,0:T(8,128)(2,1)S(1)}, u32[]{:S(2)}, u32[]{:S(2)}) collective-permute-start(bf16[32,4096]{1,0:T(8,128)(2,1)S(1)} %get-tuple-element.89), channel_id=1, source_target_pairs={{0,8},{1,9},{2,10},{3,11},{4,12},{5,13},{6,14},{7,15},{8,0},{9,1},... | collective-permute-start | bytes 786440 | tf_op jit(solution)/shard_map/rs02/ppermute | solution.py:275
  46.4 2.9 %collective-permute-done.6 = bf16[64,5120]{1,0:T(8,128)(2,1)S(1)} collective-permute-done((bf16[64,5120]{1,0:T(8,128)(2,1)S(1)}, bf16[64,5120]{1,0:T(8,128)(2,1)S(1)}, u32[]{:S(2)}, u32[]{:S(2)}) %collective-permute-start.6) | collective-permute-done | bytes 655392 | tf_op jit(solution)/shard_map/rs11/ppermute | solution.py:275
  50.8 7.3 %collective-permute-done.5 = bf16[32,4096]{1,0:T(8,128)(2,1)S(1)} collective-permute-done((bf16[32,4096]{1,0:T(8,128)(2,1)S(1)}, bf16[32,4096]{1,0:T(8,128)(2,1)S(1)}, u32[]{:S(2)}, u32[]{:S(2)}) %collective-permute-start.5) | collective-permute-done | bytes 262176 | tf_op jit(solution)/shard_map/rs02/ppermute | solution.py:275
  62.3 3.2 %collective-permute-start.11 = (bf16[16,5120]{1,0:T(8,128)(2,1)S(1)}, bf16[16,5120]{1,0:T(8,128)(2,1)S(1)}, u32[]{:S(2)}, u32[]{:S(2)}) collective-permute-start(bf16[16,5120]{1,0:T(8,128)(2,1)S(1)} %add_convert_fusion.16), channel_id=1, source_target_pairs={{0,8},{1,9},{2,10},{3,11},{4,12},{5,13},{6,14},{7,15},{8,0},{9,1},... | collective-permute-start | bytes 491528 | tf_op jit(solution)/shard_map/rs13/ppermute | solution.py:275
  65.5 3.4 %collective-permute-done.12 = bf16[64,3072]{1,0:T(8,128)(2,1)S(1)} collective-permute-done((bf16[64,3072]{1,0:T(8,128)(2,1)S(1)}, bf16[64,3072]{1,0:T(8,128)(2,1)S(1)}, u32[]{:S(2)}, u32[]{:S(2)}) %collective-permute-start.12) | collective-permute-done | bytes 393248 | tf_op jit(solution)/shard_map/rs31/ppermute | solution.py:275
  71.7 2.6 %collective-permute-start.13 = (bf16[16,4096]{1,0:T(8,128)(2,1)S(1)}, bf16[16,4096]{1,0:T(8,128)(2,1)S(1)}, u32[]{:S(2)}, u32[]{:S(2)}) collective-permute-start(bf16[16,4096]{1,0:T(8,128)(2,1)S(1)} %add_convert_fusion.19), channel_id=1, source_target_pairs={{0,8},{1,9},{2,10},{3,11},{4,12},{5,13},{6,14},{7,15},{8,0},{9,1},... | collective-permute-start | bytes 393224 | tf_op jit(solution)/shard_map/rs23/ppermute | solution.py:275
  74.4 4.2 %collective-permute-done.13 = bf16[16,4096]{1,0:T(8,128)(2,1)S(1)} collective-permute-done((bf16[16,4096]{1,0:T(8,128)(2,1)S(1)}, bf16[16,4096]{1,0:T(8,128)(2,1)S(1)}, u32[]{:S(2)}, u32[]{:S(2)}) %collective-permute-start.13) | collective-permute-done | bytes 131104 | tf_op jit(solution)/shard_map/rs23/ppermute | solution.py:275
  81.1 3.1 %collective-permute-done.15 = bf16[16,3072]{1,0:T(8,128)(2,1)S(1)} collective-permute-done((bf16[16,3072]{1,0:T(8,128)(2,1)S(1)}, bf16[16,3072]{1,0:T(8,128)(2,1)S(1)}, u32[]{:S(2)}, u32[]{:S(2)}) %collective-permute-start.15) | collective-permute-done | bytes 98336 | tf_op jit(solution)/shard_map/rs33/ppermute | solution.py:275
  90.3 3.6 %collective-permute-done.17 = bf16[1,1,1,16,3072]{4,3,2,1,0:T(8,128)(2,1)S(1)} collective-permute-done((bf16[1,1,1,16,3072]{4,3,2,1,0:T(8,128)(2,1)S(1)}, bf16[1,1,1,16,3072]{4,3,2,1,0:T(8,128)(2,1)S(1)}, u32[]{:S(2)}, u32[]{:S(2)}) %collective-permute-start.17) | collective-permute-done | bytes 98336 | tf_op jit(solution)/shard_map/ag33/ppermute | solution.py:275
  95.1 5.6 %collective-permute-done.18 = bf16[1,2,1,16,3072]{4,3,2,1,0:T(8,128)(2,1)S(1)} collective-permute-done((bf16[1,2,1,16,3072]{4,3,2,1,0:T(8,128)(2,1)S(1)}, bf16[1,2,1,16,3072]{4,3,2,1,0:T(8,128)(2,1)S(1)}, u32[]{:S(2)}, u32[]{:S(2)}) %collective-permute-start.18) | collective-permute-done | bytes 196640 | tf_op jit(solution)/shard_map/ag32/ppermute | solution.py:275
  102.7 2.3 %collective-permute-start.16 = (bf16[1,1,1,16,5120]{4,3,2,1,0:T(8,128)(2,1)S(1)}, bf16[1,1,1,16,5120]{4,3,2,1,0:T(8,128)(2,1)S(1)}, u32[]{:S(2)}, u32[]{:S(2)}) collective-permute-start(bf16[1,1,1,16,5120]{4,3,2,1,0:T(8,128)(2,1)S(1)} %slice_bitcast_fusion), channel_id=1, source_target_pairs={{0,8},{1,9},{2,10},{3,11},{4,12},{5,13},{6,14},{7,15},{8,0},{9,1},... | collective-permute-start | bytes 491528 | tf_op jit(solution)/shard_map/ag13/ppermute | solution.py:275
  106.1 3.1 %collective-permute-done.22 = bf16[1,2,1,16,4096]{4,3,2,1,0:T(8,128)(2,1)S(1)} collective-permute-done((bf16[1,2,1,16,4096]{4,3,2,1,0:T(8,128)(2,1)S(1)}, bf16[1,2,1,16,4096]{4,3,2,1,0:T(8,128)(2,1)S(1)}, u32[]{:S(2)}, u32[]{:S(2)}) %collective-permute-start.22) | collective-permute-done | bytes 262176 | tf_op jit(solution)/shard_map/ag22/ppermute | solution.py:275
  109.2 3.6 %collective-permute-done.20 = bf16[1,2,2,16,3072]{4,3,2,1,0:T(8,128)(2,1)S(1)} collective-permute-done((bf16[1,2,2,16,3072]{4,3,2,1,0:T(8,128)(2,1)S(1)}, bf16[1,2,2,16,3072]{4,3,2,1,0:T(8,128)(2,1)S(1)}, u32[]{:S(2)}, u32[]{:S(2)}) %collective-permute-start.20) | collective-permute-done | bytes 393248 | tf_op jit(solution)/shard_map/ag31/ppermute | solution.py:275
  113.0 4.8 %collective-permute-start.25 = (bf16[2,1,1,16,4096]{4,3,2,1,0:T(8,128)(2,1)S(1)}, bf16[2,1,1,16,4096]{4,3,2,1,0:T(8,128)(2,1)S(1)}, u32[]{:S(2)}, u32[]{:S(2)}) collective-permute-start(bf16[2,1,1,16,4096]{4,3,2,1,0:T(8,128)(2,1)S(1)} %pad_maximum_fusion.6), channel_id=1, source_target_pairs={{0,8},{1,9},{2,10},{3,11},{4,12},{5,13},{6,14},{7,15},{8,0},{9,1},... | collective-permute-start | bytes 786440 | tf_op jit(solution)/shard_map/ag02/ppermute | solution.py:275
  117.7 7.0 %collective-permute-done.23 = bf16[1,2,1,16,5120]{4,3,2,1,0:T(8,128)(2,1)S(1)} collective-permute-done((bf16[1,2,1,16,5120]{4,3,2,1,0:T(8,128)(2,1)S(1)}, bf16[1,2,1,16,5120]{4,3,2,1,0:T(8,128)(2,1)S(1)}, u32[]{:S(2)}, u32[]{:S(2)}) %collective-permute-start.23) | collective-permute-done | bytes 327712 | tf_op jit(solution)/shard_map/ag12/ppermute | solution.py:275
  125.0 4.5 %collective-permute-start.26 = (bf16[2,2,1,16,4096]{4,3,2,1,0:T(8,128)(2,1)S(1)}, bf16[2,2,1,16,4096]{4,3,2,1,0:T(8,128)(2,1)S(1)}, u32[]{:S(2)}, u32[]{:S(2)}) collective-permute-start(bf16[2,2,1,16,4096]{4,3,2,1,0:T(8,128)(2,1)S(1)} %pad_maximum_fusion.3), channel_id=1, source_target_pairs={{0,4},{1,5},{2,6},{3,7},{4,0},{5,1},{6,2},{7,3},{8,12},{9,13},{10,... | collective-permute-start | bytes 1572872 | tf_op jit(solution)/shard_map/ag01/ppermute | solution.py:275
  129.5 7.2 %collective-permute-done.26 = bf16[2,2,1,16,4096]{4,3,2,1,0:T(8,128)(2,1)S(1)} collective-permute-done((bf16[2,2,1,16,4096]{4,3,2,1,0:T(8,128)(2,1)S(1)}, bf16[2,2,1,16,4096]{4,3,2,1,0:T(8,128)(2,1)S(1)}, u32[]{:S(2)}, u32[]{:S(2)}) %collective-permute-start.26) | collective-permute-done | bytes 524320 | tf_op jit(solution)/shard_map/ag01/ppermute | solution.py:275
  137.9 3.0 %collective-permute-done.24 = bf16[1,2,2,16,5120]{4,3,2,1,0:T(8,128)(2,1)S(1)} collective-permute-done((bf16[1,2,2,16,5120]{4,3,2,1,0:T(8,128)(2,1)S(1)}, bf16[1,2,2,16,5120]{4,3,2,1,0:T(8,128)(2,1)S(1)}, u32[]{:S(2)}, u32[]{:S(2)}) %collective-permute-start.24) | collective-permute-done | bytes 655392 | tf_op jit(solution)/shard_map/ag11/ppermute | solution.py:275
  141.5 2.8 %collective-permute-done.30.refs_3_ = bf16[4,16,3072]{2,1,0:T(8,128)(2,1)S(1)} collective-permute-done((bf16[4,16,3072]{2,1,0:T(8,128)(2,1)S(1)}, bf16[4,16,3072]{2,1,0:T(8,128)(2,1)S(1)}, u32[]{:S(2)}, u32[]{:S(2)}) %collective-permute-start.30) | collective-permute-done | bytes 393248 | tf_op jit(solution)/shard_map/ag31/ppermute | solution.py:275
  144.4 4.6 %put.2.refs_2_ = bf16[4,2,2,16,16384]{4,3,2,1,0:T(8,128)(2,1)} custom-call(bf16[4,16,3072]{2,1,0:T(8,128)(2,1)S(1)} %bitcast.45, bf16[4,16,3072]{2,1,0:T(8,128)(2,1)S(1)} %collective-permute-done.29.refs_1_, bf16[4,16,3072]{2,1,0:T(8,128)(2,1)S(1)} %bitcast.51, bf16[4,16,3072]{2,1,0:T(8,128)(2,1)S(1)} %collective-permute-done.30.refs_3_, ...), custom_call_target="tpu_custom_call" | custom-call | bytes 14155776 | tf_op jit(solution)/shard_map/put/pallas_call | solution.py:226
  (104 shorter events, 33.4 us)
Async XLA Ops:
  24.2 10.1 %collective-permute-start.2 = (bf16[128,3072]{1,0:T(8,128)(2,1)}, bf16[128,3072]{1,0:T(8,128)(2,1)}, u32[]{:S(2)}, u32[]{:S(2)}) collective-permute-start(bf16[128,3072]{1,0:T(8,128)(2,1)} %get-tuple-element.39), channel_id=1, source_target_pairs={{0,1},{1,0},{2,3},{3,2},{4,5},{5,4},{6,7},{7,6},{8,9},{9,8},{10,11... | collective-permute-start | bytes 2359304 | tf_op jit(solution)/shard_map/rs30/ppermute | solution.py:275
  24.7 8.5 %collective-permute-start.3 = (bf16[128,4096]{1,0:T(8,128)(2,1)}, bf16[128,4096]{1,0:T(8,128)(2,1)S(1)}, u32[]{:S(2)}, u32[]{:S(2)}) collective-permute-start(bf16[128,4096]{1,0:T(8,128)(2,1)} %get-tuple-element.41), channel_id=1, source_target_pairs={{0,1},{1,0},{2,3},{3,2},{4,5},{5,4},{6,7},{7,6},{8,9},{9,8},{10,11... | collective-permute-start | bytes 3145736 | tf_op jit(solution)/shard_map/rs20/ppermute | solution.py:275
  28.2 15.2 %collective-permute-start.1 = (bf16[64,4096]{1,0:T(8,128)(2,1)S(1)}, bf16[64,4096]{1,0:T(8,128)(2,1)S(1)}, u32[]{:S(2)}, u32[]{:S(2)}) collective-permute-start(bf16[64,4096]{1,0:T(8,128)(2,1)S(1)} %get-tuple-element.79), channel_id=1, source_target_pairs={{0,4},{1,5},{2,6},{3,7},{4,0},{5,1},{6,2},{7,3},{8,12},{9,13},{10,... | collective-permute-start | bytes 1572872 | tf_op jit(solution)/shard_map/rs01/ppermute | solution.py:275
  31.6 17.7 %collective-permute-start.6 = (bf16[64,5120]{1,0:T(8,128)(2,1)S(1)}, bf16[64,5120]{1,0:T(8,128)(2,1)S(1)}, u32[]{:S(2)}, u32[]{:S(2)}) collective-permute-start(bf16[64,5120]{1,0:T(8,128)(2,1)S(1)} %get-tuple-element.75), channel_id=1, source_target_pairs={{0,2},{1,3},{2,0},{3,1},{4,6},{5,7},{6,4},{7,5},{8,10},{9,11},{10,... | collective-permute-start | bytes 1966088 | tf_op jit(solution)/shard_map/rs11/ppermute | solution.py:275
  33.4 27.1 %collective-permute-start.8 = (bf16[64,4096]{1,0:T(8,128)(2,1)S(1)}, bf16[64,4096]{1,0:T(8,128)(2,1)S(1)}, u32[]{:S(2)}, u32[]{:S(2)}) collective-permute-start(bf16[64,4096]{1,0:T(8,128)(2,1)S(1)} %get-tuple-element.77), channel_id=1, source_target_pairs={{0,2},{1,3},{2,0},{3,1},{4,6},{5,7},{6,4},{7,5},{8,10},{9,11},{10,... | collective-permute-start | bytes 1572872 | tf_op jit(solution)/shard_map/rs21/ppermute | solution.py:275
  35.7 33.2 %collective-permute-start.12 = (bf16[64,3072]{1,0:T(8,128)(2,1)S(1)}, bf16[64,3072]{1,0:T(8,128)(2,1)S(1)}, u32[]{:S(2)}, u32[]{:S(2)}) collective-permute-start(bf16[64,3072]{1,0:T(8,128)(2,1)S(1)} %get-tuple-element.80), channel_id=1, source_target_pairs={{0,2},{1,3},{2,0},{3,1},{4,6},{5,7},{6,4},{7,5},{8,10},{9,11},{10,... | collective-permute-start | bytes 1179656 | tf_op jit(solution)/shard_map/rs31/ppermute | solution.py:275
  43.6 14.5 %collective-permute-start.5 = (bf16[32,4096]{1,0:T(8,128)(2,1)S(1)}, bf16[32,4096]{1,0:T(8,128)(2,1)S(1)}, u32[]{:S(2)}, u32[]{:S(2)}) collective-permute-start(bf16[32,4096]{1,0:T(8,128)(2,1)S(1)} %get-tuple-element.89), channel_id=1, source_target_pairs={{0,8},{1,9},{2,10},{3,11},{4,12},{5,13},{6,14},{7,15},{8,0},{9,1},... | collective-permute-start | bytes 786440 | tf_op jit(solution)/shard_map/rs02/ppermute | solution.py:275
  49.4 12.8 %collective-permute-start.10 = (bf16[32,5120]{1,0:T(8,128)(2,1)S(1)}, bf16[32,5120]{1,0:T(8,128)(2,1)S(1)}, u32[]{:S(2)}, u32[]{:S(2)}) collective-permute-start(bf16[32,5120]{1,0:T(8,128)(2,1)S(1)} %get-tuple-element.82), channel_id=1, source_target_pairs={{0,4},{1,5},{2,6},{3,7},{4,0},{5,1},{6,2},{7,3},{8,12},{9,13},{10,... | collective-permute-start | bytes 983048 | tf_op jit(solution)/shard_map/rs12/ppermute | solution.py:275
  58.1 16.2 %collective-permute-start.7 = (bf16[16,4096]{1,0:T(8,128)(2,1)S(1)}, bf16[16,4096]{1,0:T(8,128)(2,1)S(1)}, u32[]{:S(2)}, u32[]{:S(2)}) collective-permute-start(bf16[16,4096]{1,0:T(8,128)(2,1)S(1)} %add_convert_fusion.20), channel_id=1, source_target_pairs={{0,2},{1,3},{2,0},{3,1},{4,6},{5,7},{6,4},{7,5},{8,10},{9,11},{10,... | collective-permute-start | bytes 393224 | tf_op jit(solution)/shard_map/rs03/ppermute | solution.py:275
  60.6 11.1 %collective-permute-start.9 = (bf16[32,4096]{1,0:T(8,128)(2,1)S(1)}, bf16[32,4096]{1,0:T(8,128)(2,1)S(1)}, u32[]{:S(2)}, u32[]{:S(2)}) collective-permute-start(bf16[32,4096]{1,0:T(8,128)(2,1)S(1)} %get-tuple-element.87), channel_id=1, source_target_pairs={{0,4},{1,5},{2,6},{3,7},{4,0},{5,1},{6,2},{7,3},{8,12},{9,13},{10,... | collective-permute-start | bytes 786440 | tf_op jit(solution)/shard_map/rs22/ppermute | solution.py:275
  62.3 8.3 %collective-permute-start.11 = (bf16[16,5120]{1,0:T(8,128)(2,1)S(1)}, bf16[16,5120]{1,0:T(8,128)(2,1)S(1)}, u32[]{:S(2)}, u32[]{:S(2)}) collective-permute-start(bf16[16,5120]{1,0:T(8,128)(2,1)S(1)} %add_convert_fusion.16), channel_id=1, source_target_pairs={{0,8},{1,9},{2,10},{3,11},{4,12},{5,13},{6,14},{7,15},{8,0},{9,1},... | collective-permute-start | bytes 491528 | tf_op jit(solution)/shard_map/rs13/ppermute | solution.py:275
  69.0 9.6 %collective-permute-start.14 = (bf16[32,3072]{1,0:T(8,128)(2,1)S(1)}, bf16[32,3072]{1,0:T(8,128)(2,1)S(1)}, u32[]{:S(2)}, u32[]{:S(2)}) collective-permute-start(bf16[32,3072]{1,0:T(8,128)(2,1)S(1)} %get-tuple-element.90), channel_id=1, source_target_pairs={{0,4},{1,5},{2,6},{3,7},{4,0},{5,1},{6,2},{7,3},{8,12},{9,13},{10,... | collective-permute-start | bytes 589832 | tf_op jit(solution)/shard_map/rs32/ppermute | solution.py:275
  86.0 7.8 %collective-permute-start.17 = (bf16[1,1,1,16,3072]{4,3,2,1,0:T(8,128)(2,1)S(1)}, bf16[1,1,1,16,3072]{4,3,2,1,0:T(8,128)(2,1)S(1)}, u32[]{:S(2)}, u32[]{:S(2)}) collective-permute-start(bf16[1,1,1,16,3072]{4,3,2,1,0:T(8,128)(2,1)S(1)} %slice_bitcast_fusion.3), channel_id=1, source_target_pairs={{0,8},{1,9},{2,10},{3,11},{4,12},{5,13},{6,14},{7,15},{8,0},{9,1},... | collective-permute-start | bytes 294920 | tf_op jit(solution)/shard_map/ag33/ppermute | solution.py:275
  87.7 13.1 %collective-permute-start.21 = (bf16[1,1,1,16,4096]{4,3,2,1,0:T(8,128)(2,1)S(1)}, bf16[1,1,1,16,4096]{4,3,2,1,0:T(8,128)(2,1)S(1)}, u32[]{:S(2)}, u32[]{:S(2)}) collective-permute-start(bf16[1,1,1,16,4096]{4,3,2,1,0:T(8,128)(2,1)S(1)} %get-tuple-element.106), channel_id=1, source_target_pairs={{0,8},{1,9},{2,10},{3,11},{4,12},{5,13},{6,14},{7,15},{8,0},{9,1},... | collective-permute-start | bytes 393224 | tf_op jit(solution)/shard_map/ag23/ppermute | solution.py:275
  100.9 8.2 %collective-permute-start.22 = (bf16[1,2,1,16,4096]{4,3,2,1,0:T(8,128)(2,1)S(1)}, bf16[1,2,1,16,4096]{4,3,2,1,0:T(8,128)(2,1)S(1)}, u32[]{:S(2)}, u32[]{:S(2)}) collective-permute-start(bf16[1,2,1,16,4096]{4,3,2,1,0:T(8,128)(2,1)S(1)} %pad_maximum_fusion.7), channel_id=1, source_target_pairs={{0,4},{1,5},{2,6},{3,7},{4,0},{5,1},{6,2},{7,3},{8,12},{9,13},{10,... | collective-permute-start | bytes 786440 | tf_op jit(solution)/shard_map/ag22/ppermute | solution.py:275
  102.7 10.1 %collective-permute-start.16 = (bf16[1,1,1,16,5120]{4,3,2,1,0:T(8,128)(2,1)S(1)}, bf16[1,1,1,16,5120]{4,3,2,1,0:T(8,128)(2,1)S(1)}, u32[]{:S(2)}, u32[]{:S(2)}) collective-permute-start(bf16[1,1,1,16,5120]{4,3,2,1,0:T(8,128)(2,1)S(1)} %slice_bitcast_fusion), channel_id=1, source_target_pairs={{0,8},{1,9},{2,10},{3,11},{4,12},{5,13},{6,14},{7,15},{8,0},{9,1},... | collective-permute-start | bytes 491528 | tf_op jit(solution)/shard_map/ag13/ppermute | solution.py:275
  105.0 7.8 %collective-permute-start.20 = (bf16[1,2,2,16,3072]{4,3,2,1,0:T(8,128)(2,1)S(1)}, bf16[1,2,2,16,3072]{4,3,2,1,0:T(8,128)(2,1)S(1)}, u32[]{:S(2)}, u32[]{:S(2)}) collective-permute-start(bf16[1,2,2,16,3072]{4,3,2,1,0:T(8,128)(2,1)S(1)} %pad_maximum_fusion.4), channel_id=1, source_target_pairs={{0,2},{1,3},{2,0},{3,1},{4,6},{5,7},{6,4},{7,5},{8,10},{9,11},{10,... | collective-permute-start | bytes 1179656 | tf_op jit(solution)/shard_map/ag31/ppermute | solution.py:275
  112.9 11.8 %collective-permute-start.23 = (bf16[1,2,1,16,5120]{4,3,2,1,0:T(8,128)(2,1)S(1)}, bf16[1,2,1,16,5120]{4,3,2,1,0:T(8,128)(2,1)S(1)}, u32[]{:S(2)}, u32[]{:S(2)}) collective-permute-start(bf16[1,2,1,16,5120]{4,3,2,1,0:T(8,128)(2,1)S(1)} %pad_maximum_fusion.5), channel_id=1, source_target_pairs={{0,4},{1,5},{2,6},{3,7},{4,0},{5,1},{6,2},{7,3},{8,12},{9,13},{10,... | collective-permute-start | bytes 983048 | tf_op jit(solution)/shard_map/ag12/ppermute | solution.py:275
  113.0 11.9 %collective-permute-start.25 = (bf16[2,1,1,16,4096]{4,3,2,1,0:T(8,128)(2,1)S(1)}, bf16[2,1,1,16,4096]{4,3,2,1,0:T(8,128)(2,1)S(1)}, u32[]{:S(2)}, u32[]{:S(2)}) collective-permute-start(bf16[2,1,1,16,4096]{4,3,2,1,0:T(8,128)(2,1)S(1)} %pad_maximum_fusion.6), channel_id=1, source_target_pairs={{0,8},{1,9},{2,10},{3,11},{4,12},{5,13},{6,14},{7,15},{8,0},{9,1},... | collective-permute-start | bytes 786440 | tf_op jit(solution)/shard_map/ag02/ppermute | solution.py:275
  117.7 11.8 %collective-permute-start.27 = (bf16[1,2,2,16,4096]{4,3,2,1,0:T(8,128)(2,1)S(1)}, bf16[1,2,2,16,4096]{4,3,2,1,0:T(8,128)(2,1)S(1)}, u32[]{:S(2)}, u32[]{:S(2)}) collective-permute-start(bf16[1,2,2,16,4096]{4,3,2,1,0:T(8,128)(2,1)S(1)} %pad_maximum_fusion.2), channel_id=1, source_target_pairs={{0,2},{1,3},{2,0},{3,1},{4,6},{5,7},{6,4},{7,5},{8,10},{9,11},{10,... | collective-permute-start | bytes 1572872 | tf_op jit(solution)/shard_map/ag21/ppermute | solution.py:275
  125.0 11.7 %collective-permute-start.26 = (bf16[2,2,1,16,4096]{4,3,2,1,0:T(8,128)(2,1)S(1)}, bf16[2,2,1,16,4096]{4,3,2,1,0:T(8,128)(2,1)S(1)}, u32[]{:S(2)}, u32[]{:S(2)}) collective-permute-start(bf16[2,2,1,16,4096]{4,3,2,1,0:T(8,128)(2,1)S(1)} %pad_maximum_fusion.3), channel_id=1, source_target_pairs={{0,4},{1,5},{2,6},{3,7},{4,0},{5,1},{6,2},{7,3},{8,12},{9,13},{10,... | collective-permute-start | bytes 1572872 | tf_op jit(solution)/shard_map/ag01/ppermute | solution.py:275
  129.5 11.5 %collective-permute-start.24 = (bf16[1,2,2,16,5120]{4,3,2,1,0:T(8,128)(2,1)S(1)}, bf16[1,2,2,16,5120]{4,3,2,1,0:T(8,128)(2,1)S(1)}, u32[]{:S(2)}, u32[]{:S(2)}) collective-permute-start(bf16[1,2,2,16,5120]{4,3,2,1,0:T(8,128)(2,1)S(1)} %pad_maximum_fusion.1), channel_id=1, source_target_pairs={{0,2},{1,3},{2,0},{3,1},{4,6},{5,7},{6,4},{7,5},{8,10},{9,11},{10,... | collective-permute-start | bytes 1966088 | tf_op jit(solution)/shard_map/ag11/ppermute | solution.py:275
  136.8 7.6 %collective-permute-start.33 = (bf16[2,4,16,4096]{3,2,1,0:T(8,128)(2,1)S(1)}, bf16[2,4,16,4096]{3,2,1,0:T(8,128)(2,1)S(1)}, u32[]{:S(2)}, u32[]{:S(2)}) collective-permute-start(bf16[2,4,16,4096]{3,2,1,0:T(8,128)(2,1)S(1)} %bitcast.38), channel_id=1, source_target_pairs={{0,1},{1,0},{2,3},{3,2},{4,5},{5,4},{6,7},{7,6},{8,9},{9,8},{10,11... | collective-permute-start | bytes 3145736 | tf_op jit(solution)/shard_map/ag01/ppermute | solution.py:275
  141.0 8.0 %collective-permute-start.28 = (bf16[4,16,5120]{2,1,0:T(8,128)(2,1)S(1)}, bf16[4,16,5120]{2,1,0:T(8,128)(2,1)S(1)}, u32[]{:S(2)}, u32[]{:S(2)}) collective-permute-start(bf16[4,16,5120]{2,1,0:T(8,128)(2,1)S(1)} %bitcast.46), channel_id=1, source_target_pairs={{0,1},{1,0},{2,3},{3,2},{4,5},{5,4},{6,7},{7,6},{8,9},{9,8},{10,11... | collective-permute-start | bytes 1966088 | tf_op jit(solution)/shard_map/ag11/ppermute | solution.py:275
  (17 other events, 80.5 us)

commit v5 on v4

--- a/solution.py
+++ b/solution.py
@@ -7,9 +7,8 @@
 from jax.experimental.pallas import tpu as pltpu
 from jax.sharding import PartitionSpec as P
 
-WIDTHS = (4, 5, 4, 3)
-CHUNKS = len(WIDTHS)
-GATHER = (3, 2, 1)
+SCATTER = ((4, 1), (5, 0), (4, 0), (3, 0))
+GATHER = ((2, 0), (4, 0), (4, 1), (6, 0))
 KEY_BLOCK = 2048
 TILE = 1024
 CODE_TOP = 448.0
@@ -69,6 +68,7 @@
             row = lax.broadcasted_iota(jnp.int32, (rows, key_block), 0)
             col = lax.broadcasted_iota(jnp.int32, (rows, key_block), 1)
             seen = col - row <= start - step * key_block
+        all_scores = []
         for h in range(heads):
             scores = lax.dot_general(
                 q_ref[:, h * head : (h + 1) * head],
@@ -78,6 +78,8 @@
             )
             if masked:
                 scores = jnp.where(seen, scores, jnp.float32(-1e30))
+            all_scores.append(scores)
+        for h, scores in enumerate(all_scores):
             before = top_ref[h]
             top = jnp.maximum(before, jnp.max(scores, axis=1, keepdims=True))
             weights = jnp.exp2((scores - top[:, :1]) * coef).astype(jnp.bfloat16)
@@ -142,7 +144,7 @@
     blocks = term_exp.shape[2]
     width = out_weight.shape[1]
     n_tiles = width // TILE
-    key_block = min(KEY_BLOCK, context)
+    key_block = min(KEY_BLOCK * 256 // rows, context)
     half = rows // 2
 
     def cache_block(step, start_ref):
@@ -254,11 +256,15 @@
 def gather_plan(bits):
     last = bits - 1
     far = list(range(last - 1, 1, -1))
-    one, two, three = GATHER
-    plan = [(one, last), (0, last)] + [(one, s) for s in far]
-    plan += [(two, last)] + [(two, s) for s in far] + [(one, 1), (three, last)] + [(three, s) for s in far]
-    plan += [(0, s) for s in far] + [(two, 1), (0, 1), (three, 1)]
+    plan = [(0, last), (2, last)] + [(0, s) for s in far]
+    plan += [(1, last)] + [(1, s) for s in far] + [(0, 1), (3, last)] + [(3, s) for s in far]
+    plan += [(2, s) for s in far] + [(1, 1), (2, 1), (3, 1)]
     return plan
+
+
+def edges_of(chunks, width):
+    parts = sum(w for w, _ in chunks)
+    return [width * sum(w for w, _ in chunks[:j]) // parts for j in range(len(chunks) + 1)]
 
 
 def per_device(queries, cache, offset, out_weight, residual, term_exp, code_exp, gain):
@@ -268,8 +274,7 @@
     block, width = residual.shape
     blocks = code_exp.shape[1]
     group = width // blocks
-    unit = width // sum(WIDTHS)
-    edges = [unit * sum(WIDTHS[:j]) for j in range(CHUNKS + 1)]
+    edges = edges_of(SCATTER, width)
 
     def flip(x, b):
         return lax.ppermute(x, "tp", [(i, i ^ (1 << b)) for i in range(parts)])
@@ -277,7 +282,7 @@
     order_a = list(range(bits))
     order_b = [0] + list(range(2, bits)) + [1]
     kinds = [order_a, order_b]
-    uses = [1] + [0] * (CHUNKS - 1)
+    uses = [kind for _, kind in SCATTER]
 
     state = partials(offset, queries, cache, term_exp, out_weight, uses, kinds, edges)
 
@@ -300,7 +305,7 @@
             came = held_back(flip(send, kinds[uses[j]][step]), dones[-1:])
             state[j] = merge(keep, came, step == last)
             dones.append(state[j][0 if step == last else 1])
-    sums = [state[j][0] for j in range(CHUNKS)]
+    sums = [state[j][0] for j in range(len(SCATTER))]
     summed = jnp.concatenate(sums, axis=1)
     stream = (summed + residual.astype(jnp.float32)).astype(jnp.bfloat16)
     wide = stream.astype(jnp.float32)
@@ -311,7 +316,8 @@
     mixed = jnp.clip(normed, -cap, cap).reshape(block, width).astype(jnp.bfloat16)
 
     ones = (1,) * (bits - 1)
-    held = {j: mixed[:, edges[j] : edges[j + 1]].reshape(ones + (block, -1)) for j in range(CHUNKS)}
+    edges = edges_of(GATHER, width)
+    held = {j: mixed[:, edges[j] : edges[j + 1]].reshape(ones + (block, -1)) for j in range(len(GATHER))}
     far = parts // 4
 
     def join(x, came, b):
@@ -323,7 +329,7 @@
     pieces = []
     late = []
     for j, step in gather_plan(bits):
-        order = kinds[uses[j]]
+        order = kinds[GATHER[j][1]]
         with jax.named_scope(f"ag{j}{step}"):
             came = held_back(flip(held[j], order[step]), dones[-1:])
             if step > 1 or order[step] != 1:
@@ -334,7 +340,7 @@
             if step == 1 and order[step] == 1:
                 for y, x in enumerate((held[j], came)):
                     x = x.reshape(far, block, -1)
-                    keep = late if y and j == GATHER[-1] else pieces
+                    keep = late if y and j == len(GATHER) - 1 else pieces
                     keep += [(x, y, 0, edges[j]), (flip(x, order[0]), y, 1, edges[j])]
             elif step == 1:
                 x = held[j].reshape(2, far, block, -1)

time: 151 us -> 148 us (0.980)
  starting transfers between devices: 45.5 us -> 53.5 us
  waiting for transfers between devices: 67.5 us -> 61.3 us
  Pallas kernels: 28.5 us -> 22.8 us
    ppermute x35, starting transfers between devices: 45.5 us -> 53.5 us  [flip(): return lax.ppermute(x, 'tp', [(i, i ^ 1 << b) for i in range(parts)])]
    ppermute x35, waiting for transfers between devices: 67.5 us -> 61.3 us  [flip(): return lax.ppermute(x, 'tp', [(i, i ^ 1 << b) for i in range(parts)])]
    pallas_call x1, Pallas kernels: 22.4 us -> 18 us  [partials(): pl.pallas_call(functools.partial(partial_kernel, key_block=key_block, hea...]
  transfers between devices with their start and end apart: 35 -> 35, of which waited for: 19 -> 20; matrix products, arithmetic and copies ran while one was open for 4% -> 4% of each run, Pallas kernels for 3% -> 2%
where the time goes in v5:
time: 148 us; the launch traced here: 147 us
  waiting for transfers between devices  61.3 us (41%)
  starting transfers between devices  53.5 us (36%)
  Pallas kernels  22.8 us (15%)
  other arithmetic  6.63 us (4%)
  between operations  1.82 us (1%)
    ppermute x35, waiting for transfers between devices, flip(): return lax.ppermute(x, 'tp', [(i, i ^ 1 << b) for i in range(parts)])  61.3 us
    ppermute x35, starting transfers between devices, flip(): return lax.ppermute(x, 'tp', [(i, i ^ 1 << b) for i in range(parts)])  53.5 us
    pallas_call x1, Pallas kernels, partials(): pl.pallas_call(functools.partial(partial_kernel, key_block=key_block, hea...  18 us
    pallas_call x2, Pallas kernels, put(): pl.pallas_call(functools.partial(put_kernel, places=places), in_specs=[an...  4.82 us
  transfers between devices with their start and end apart: 35, of which 20 were waited for; matrix products, arithmetic and copies ran while one was open for 4% of the time, Pallas kernels for 2%

profile of v5, /device:TPU:0, one launch (start us, length us, event | category | flops | bytes accessed | tf_op | source)
XLA Modules:
  0.0 146.7 jit_solution(8191965926421651866)
XLA Ops:
  1.3 18.0 %partials.1 = (bf16[128,4096]{1,0:T(8,128)(2,1)}, bf16[128,4096]{1,0:T(8,128)(2,1)}, bf16[128,5120]{1,0:T(8,128)(2,1)}, bf16[128,5120]{1,0:T(8,128)(2,1)}, bf16[...) custom-call(s32[1]{0:T(128)S(6)} %copy.16.start_ref, ...), custom_call_target="tpu_custom_call" | custom-call | tf_op jit(solution)/shard_map/partials/pallas_call | solution.py:157
  23.8 3.0 %collective-permute-start.1 = (bf16[64,4096]{1,0:T(8,128)(2,1)S(1)}, bf16[64,4096]{1,0:T(8,128)(2,1)S(1)}, u32[]{:S(2)}, u32[]{:S(2)}) collective-permute-start(bf16[64,4096]{1,0:T(8,128)(2,1)S(1)} %get-tuple-element.79), channel_id=1, source_target_pairs={{0,4},{1,5},{2,6},{3,7},{4,0},{5,1},{6,2},{7,3},{8,12},{9,13},{10,... | collective-permute-start | bytes 1572872 | tf_op jit(solution)/shard_map/rs01/ppermute | solution.py:280
  32.5 6.5 %collective-permute-done.1 = bf16[64,4096]{1,0:T(8,128)(2,1)S(1)} collective-permute-done((bf16[64,4096]{1,0:T(8,128)(2,1)S(1)}, bf16[64,4096]{1,0:T(8,128)(2,1)S(1)}, u32[]{:S(2)}, u32[]{:S(2)}) %collective-permute-start.1) | collective-permute-done | bytes 524320 | tf_op jit(solution)/shard_map/rs01/ppermute | solution.py:280
  39.2 2.8 %collective-permute-start.5 = (bf16[32,4096]{1,0:T(8,128)(2,1)S(1)}, bf16[32,4096]{1,0:T(8,128)(2,1)S(1)}, u32[]{:S(2)}, u32[]{:S(2)}) collective-permute-start(bf16[32,4096]{1,0:T(8,128)(2,1)S(1)} %get-tuple-element.89), channel_id=1, source_target_pairs={{0,8},{1,9},{2,10},{3,11},{4,12},{5,13},{6,14},{7,15},{8,0},{9,1},... | collective-permute-start | bytes 786440 | tf_op jit(solution)/shard_map/rs02/ppermute | solution.py:280
  42.0 2.9 %collective-permute-done.6 = bf16[64,5120]{1,0:T(8,128)(2,1)S(1)} collective-permute-done((bf16[64,5120]{1,0:T(8,128)(2,1)S(1)}, bf16[64,5120]{1,0:T(8,128)(2,1)S(1)}, u32[]{:S(2)}, u32[]{:S(2)}) %collective-permute-start.6) | collective-permute-done | bytes 655392 | tf_op jit(solution)/shard_map/rs11/ppermute | solution.py:280
  46.4 7.3 %collective-permute-done.5 = bf16[32,4096]{1,0:T(8,128)(2,1)S(1)} collective-permute-done((bf16[32,4096]{1,0:T(8,128)(2,1)S(1)}, bf16[32,4096]{1,0:T(8,128)(2,1)S(1)}, u32[]{:S(2)}, u32[]{:S(2)}) %collective-permute-start.5) | collective-permute-done | bytes 262176 | tf_op jit(solution)/shard_map/rs02/ppermute | solution.py:280
  57.9 3.2 %collective-permute-start.11 = (bf16[16,5120]{1,0:T(8,128)(2,1)S(1)}, bf16[16,5120]{1,0:T(8,128)(2,1)S(1)}, u32[]{:S(2)}, u32[]{:S(2)}) collective-permute-start(bf16[16,5120]{1,0:T(8,128)(2,1)S(1)} %add_convert_fusion.16), channel_id=1, source_target_pairs={{0,8},{1,9},{2,10},{3,11},{4,12},{5,13},{6,14},{7,15},{8,0},{9,1},... | collective-permute-start | bytes 491528 | tf_op jit(solution)/shard_map/rs13/ppermute | solution.py:280
  61.1 3.4 %collective-permute-done.12 = bf16[64,3072]{1,0:T(8,128)(2,1)S(1)} collective-permute-done((bf16[64,3072]{1,0:T(8,128)(2,1)S(1)}, bf16[64,3072]{1,0:T(8,128)(2,1)S(1)}, u32[]{:S(2)}, u32[]{:S(2)}) %collective-permute-start.12) | collective-permute-done | bytes 393248 | tf_op jit(solution)/shard_map/rs31/ppermute | solution.py:280
  67.3 2.6 %collective-permute-start.13 = (bf16[16,4096]{1,0:T(8,128)(2,1)S(1)}, bf16[16,4096]{1,0:T(8,128)(2,1)S(1)}, u32[]{:S(2)}, u32[]{:S(2)}) collective-permute-start(bf16[16,4096]{1,0:T(8,128)(2,1)S(1)} %add_convert_fusion.19), channel_id=1, source_target_pairs={{0,8},{1,9},{2,10},{3,11},{4,12},{5,13},{6,14},{7,15},{8,0},{9,1},... | collective-permute-start | bytes 393224 | tf_op jit(solution)/shard_map/rs23/ppermute | solution.py:280
  70.0 4.2 %collective-permute-done.13 = bf16[16,4096]{1,0:T(8,128)(2,1)S(1)} collective-permute-done((bf16[16,4096]{1,0:T(8,128)(2,1)S(1)}, bf16[16,4096]{1,0:T(8,128)(2,1)S(1)}, u32[]{:S(2)}, u32[]{:S(2)}) %collective-permute-start.13) | collective-permute-done | bytes 131104 | tf_op jit(solution)/shard_map/rs23/ppermute | solution.py:280
  76.7 3.1 %collective-permute-done.15 = bf16[16,3072]{1,0:T(8,128)(2,1)S(1)} collective-permute-done((bf16[16,3072]{1,0:T(8,128)(2,1)S(1)}, bf16[16,3072]{1,0:T(8,128)(2,1)S(1)}, u32[]{:S(2)}, u32[]{:S(2)}) %collective-permute-start.15) | collective-permute-done | bytes 98336 | tf_op jit(solution)/shard_map/rs33/ppermute | solution.py:280
  85.9 2.7 %collective-permute-done.17 = bf16[1,1,1,16,2048]{4,3,2,1,0:T(8,128)(2,1)S(1)} collective-permute-done((bf16[1,1,1,16,2048]{4,3,2,1,0:T(8,128)(2,1)S(1)}, bf16[1,1,1,16,2048]{4,3,2,1,0:T(8,128)(2,1)S(1)}, u32[]{:S(2)}, u32[]{:S(2)}) %collective-permute-start.17) | collective-permute-done | bytes 65568 | tf_op jit(solution)/shard_map/ag03/ppermute | solution.py:280
  89.7 5.4 %collective-permute-done.18 = bf16[1,2,1,16,2048]{4,3,2,1,0:T(8,128)(2,1)S(1)} collective-permute-done((bf16[1,2,1,16,2048]{4,3,2,1,0:T(8,128)(2,1)S(1)}, bf16[1,2,1,16,2048]{4,3,2,1,0:T(8,128)(2,1)S(1)}, u32[]{:S(2)}, u32[]{:S(2)}) %collective-permute-start.18) | collective-permute-done | bytes 131104 | tf_op jit(solution)/shard_map/ag02/ppermute | solution.py:280
  97.5 2.4 %collective-permute-start.20 = (bf16[1,2,2,16,2048]{4,3,2,1,0:T(8,128)(2,1)S(1)}, bf16[1,2,2,16,2048]{4,3,2,1,0:T(8,128)(2,1)S(1)}, u32[]{:S(2)}, u32[]{:S(2)}) collective-permute-start(bf16[1,2,2,16,2048]{4,3,2,1,0:T(8,128)(2,1)S(1)} %pad_maximum_fusion.6), channel_id=1, source_target_pairs={{0,2},{1,3},{2,0},{3,1},{4,6},{5,7},{6,4},{7,5},{8,10},{9,11},{10,... | collective-permute-start | bytes 786440 | tf_op jit(solution)/shard_map/ag01/ppermute | solution.py:280
  99.8 5.0 %collective-permute-done.22 = bf16[1,2,1,16,4096]{4,3,2,1,0:T(8,128)(2,1)S(1)} collective-permute-done((bf16[1,2,1,16,4096]{4,3,2,1,0:T(8,128)(2,1)S(1)}, bf16[1,2,1,16,4096]{4,3,2,1,0:T(8,128)(2,1)S(1)}, u32[]{:S(2)}, u32[]{:S(2)}) %collective-permute-start.22) | collective-permute-done | bytes 262176 | tf_op jit(solution)/shard_map/ag12/ppermute | solution.py:280
  106.6 4.6 %collective-permute-start.25 = (bf16[2,1,1,16,4096]{4,3,2,1,0:T(8,128)(2,1)S(1)}, bf16[2,1,1,16,4096]{4,3,2,1,0:T(8,128)(2,1)S(1)}, u32[]{:S(2)}, u32[]{:S(2)}) collective-permute-start(bf16[2,1,1,16,4096]{4,3,2,1,0:T(8,128)(2,1)S(1)} %pad_maximum_fusion.5), channel_id=1, source_target_pairs={{0,8},{1,9},{2,10},{3,11},{4,12},{5,13},{6,14},{7,15},{8,0},{9,1},... | collective-permute-start | bytes 786440 | tf_op jit(solution)/shard_map/ag22/ppermute | solution.py:280
  111.2 2.7 %collective-permute-start.27 = (bf16[1,2,2,16,4096]{4,3,2,1,0:T(8,128)(2,1)S(1)}, bf16[1,2,2,16,4096]{4,3,2,1,0:T(8,128)(2,1)S(1)}, u32[]{:S(2)}, u32[]{:S(2)}) collective-permute-start(bf16[1,2,2,16,4096]{4,3,2,1,0:T(8,128)(2,1)S(1)} %pad_maximum_fusion.2), channel_id=1, source_target_pairs={{0,2},{1,3},{2,0},{3,1},{4,6},{5,7},{6,4},{7,5},{8,10},{9,11},{10,... | collective-permute-start | bytes 1572872 | tf_op jit(solution)/shard_map/ag11/ppermute | solution.py:280
  113.9 3.9 %collective-permute-done.23 = bf16[1,2,1,16,6144]{4,3,2,1,0:T(8,128)(2,1)S(1)} collective-permute-done((bf16[1,2,1,16,6144]{4,3,2,1,0:T(8,128)(2,1)S(1)}, bf16[1,2,1,16,6144]{4,3,2,1,0:T(8,128)(2,1)S(1)}, u32[]{:S(2)}, u32[]{:S(2)}) %collective-permute-start.23) | collective-permute-done | bytes 393248 | tf_op jit(solution)/shard_map/ag32/ppermute | solution.py:280
  118.1 5.8 %collective-permute-start.26 = (bf16[2,2,1,16,4096]{4,3,2,1,0:T(8,128)(2,1)S(1)}, bf16[2,2,1,16,4096]{4,3,2,1,0:T(8,128)(2,1)S(1)}, u32[]{:S(2)}, u32[]{:S(2)}) collective-permute-start(bf16[2,2,1,16,4096]{4,3,2,1,0:T(8,128)(2,1)S(1)} %pad_maximum_fusion.3), channel_id=1, source_target_pairs={{0,4},{1,5},{2,6},{3,7},{4,0},{5,1},{6,2},{7,3},{8,12},{9,13},{10,... | collective-permute-start | bytes 1572872 | tf_op jit(solution)/shard_map/ag21/ppermute | solution.py:280
  123.9 4.1 %collective-permute-start.24 = (bf16[1,2,2,16,6144]{4,3,2,1,0:T(8,128)(2,1)S(1)}, bf16[1,2,2,16,6144]{4,3,2,1,0:T(8,128)(2,1)S(1)}, u32[]{:S(2)}, u32[]{:S(2)}) collective-permute-start(bf16[1,2,2,16,6144]{4,3,2,1,0:T(8,128)(2,1)S(1)} %pad_maximum_fusion.1), channel_id=1, source_target_pairs={{0,2},{1,3},{2,0},{3,1},{4,6},{5,7},{6,4},{7,5},{8,10},{9,11},{10,... | collective-permute-start | bytes 2359304 | tf_op jit(solution)/shard_map/ag31/ppermute | solution.py:280
  128.0 3.1 %collective-permute-done.26 = bf16[2,2,1,16,4096]{4,3,2,1,0:T(8,128)(2,1)S(1)} collective-permute-done((bf16[2,2,1,16,4096]{4,3,2,1,0:T(8,128)(2,1)S(1)}, bf16[2,2,1,16,4096]{4,3,2,1,0:T(8,128)(2,1)S(1)}, u32[]{:S(2)}, u32[]{:S(2)}) %collective-permute-start.26) | collective-permute-done | bytes 524320 | tf_op jit(solution)/shard_map/ag21/ppermute | solution.py:280
  132.3 5.6 %collective-permute-done.24 = bf16[1,2,2,16,6144]{4,3,2,1,0:T(8,128)(2,1)S(1)} collective-permute-done((bf16[1,2,2,16,6144]{4,3,2,1,0:T(8,128)(2,1)S(1)}, bf16[1,2,2,16,6144]{4,3,2,1,0:T(8,128)(2,1)S(1)}, u32[]{:S(2)}, u32[]{:S(2)}) %collective-permute-start.24) | collective-permute-done | bytes 786464 | tf_op jit(solution)/shard_map/ag31/ppermute | solution.py:280
  138.5 2.4 %collective-permute-done.31.refs_5_ = bf16[4,16,4096]{2,1,0:T(8,128)(2,1)S(1)} collective-permute-done((bf16[4,16,4096]{2,1,0:T(8,128)(2,1)S(1)}, bf16[4,16,4096]{2,1,0:T(8,128)(2,1)S(1)}, u32[]{:S(2)}, u32[]{:S(2)}) %collective-permute-start.31) | collective-permute-done | bytes 524320 | tf_op jit(solution)/shard_map/ag11/ppermute | solution.py:280
  141.7 3.5 %put.2.refs_2_ = bf16[4,2,2,16,16384]{4,3,2,1,0:T(8,128)(2,1)} custom-call(bf16[4,16,2048]{2,1,0:T(8,128)(2,1)S(1)} %bitcast.45, bf16[4,16,2048]{2,1,0:T(8,128)(2,1)S(1)} %collective-permute-done.29.refs_1_, bf16[4,16,2048]{2,1,0:T(8,128)(2,1)S(1)} %bitcast.51, bf16[4,16,2048]{2,1,0:T(8,128)(2,1)S(1)} %collective-permute-done.30.refs_3_, ...), custom_call_target="tpu_custom_call" | custom-call | bytes 13631488 | tf_op jit(solution)/shard_map/put/pallas_call | solution.py:228
  (104 shorter events, 36.6 us)
Async XLA Ops:
  19.8 10.1 %collective-permute-start.2 = (bf16[128,3072]{1,0:T(8,128)(2,1)}, bf16[128,3072]{1,0:T(8,128)(2,1)}, u32[]{:S(2)}, u32[]{:S(2)}) collective-permute-start(bf16[128,3072]{1,0:T(8,128)(2,1)} %get-tuple-element.39), channel_id=1, source_target_pairs={{0,1},{1,0},{2,3},{3,2},{4,5},{5,4},{6,7},{7,6},{8,9},{9,8},{10,11... | collective-permute-start | bytes 2359304 | tf_op jit(solution)/shard_map/rs30/ppermute | solution.py:280
  20.3 8.5 %collective-permute-start.3 = (bf16[128,4096]{1,0:T(8,128)(2,1)}, bf16[128,4096]{1,0:T(8,128)(2,1)S(1)}, u32[]{:S(2)}, u32[]{:S(2)}) collective-permute-start(bf16[128,4096]{1,0:T(8,128)(2,1)} %get-tuple-element.41), channel_id=1, source_target_pairs={{0,1},{1,0},{2,3},{3,2},{4,5},{5,4},{6,7},{7,6},{8,9},{9,8},{10,11... | collective-permute-start | bytes 3145736 | tf_op jit(solution)/shard_map/rs20/ppermute | solution.py:280
  23.8 15.2 %collective-permute-start.1 = (bf16[64,4096]{1,0:T(8,128)(2,1)S(1)}, bf16[64,4096]{1,0:T(8,128)(2,1)S(1)}, u32[]{:S(2)}, u32[]{:S(2)}) collective-permute-start(bf16[64,4096]{1,0:T(8,128)(2,1)S(1)} %get-tuple-element.79), channel_id=1, source_target_pairs={{0,4},{1,5},{2,6},{3,7},{4,0},{5,1},{6,2},{7,3},{8,12},{9,13},{10,... | collective-permute-start | bytes 1572872 | tf_op jit(solution)/shard_map/rs01/ppermute | solution.py:280
  27.2 17.7 %collective-permute-start.6 = (bf16[64,5120]{1,0:T(8,128)(2,1)S(1)}, bf16[64,5120]{1,0:T(8,128)(2,1)S(1)}, u32[]{:S(2)}, u32[]{:S(2)}) collective-permute-start(bf16[64,5120]{1,0:T(8,128)(2,1)S(1)} %get-tuple-element.75), channel_id=1, source_target_pairs={{0,2},{1,3},{2,0},{3,1},{4,6},{5,7},{6,4},{7,5},{8,10},{9,11},{10,... | collective-permute-start | bytes 1966088 | tf_op jit(solution)/shard_map/rs11/ppermute | solution.py:280
  29.0 27.0 %collective-permute-start.8 = (bf16[64,4096]{1,0:T(8,128)(2,1)S(1)}, bf16[64,4096]{1,0:T(8,128)(2,1)S(1)}, u32[]{:S(2)}, u32[]{:S(2)}) collective-permute-start(bf16[64,4096]{1,0:T(8,128)(2,1)S(1)} %get-tuple-element.77), channel_id=1, source_target_pairs={{0,2},{1,3},{2,0},{3,1},{4,6},{5,7},{6,4},{7,5},{8,10},{9,11},{10,... | collective-permute-start | bytes 1572872 | tf_op jit(solution)/shard_map/rs21/ppermute | solution.py:280
  31.3 33.2 %collective-permute-start.12 = (bf16[64,3072]{1,0:T(8,128)(2,1)S(1)}, bf16[64,3072]{1,0:T(8,128)(2,1)S(1)}, u32[]{:S(2)}, u32[]{:S(2)}) collective-permute-start(bf16[64,3072]{1,0:T(8,128)(2,1)S(1)} %get-tuple-element.80), channel_id=1, source_target_pairs={{0,2},{1,3},{2,0},{3,1},{4,6},{5,7},{6,4},{7,5},{8,10},{9,11},{10,... | collective-permute-start | bytes 1179656 | tf_op jit(solution)/shard_map/rs31/ppermute | solution.py:280
  39.2 14.5 %collective-permute-start.5 = (bf16[32,4096]{1,0:T(8,128)(2,1)S(1)}, bf16[32,4096]{1,0:T(8,128)(2,1)S(1)}, u32[]{:S(2)}, u32[]{:S(2)}) collective-permute-start(bf16[32,4096]{1,0:T(8,128)(2,1)S(1)} %get-tuple-element.89), channel_id=1, source_target_pairs={{0,8},{1,9},{2,10},{3,11},{4,12},{5,13},{6,14},{7,15},{8,0},{9,1},... | collective-permute-start | bytes 786440 | tf_op jit(solution)/shard_map/rs02/ppermute | solution.py:280
  45.0 12.8 %collective-permute-start.10 = (bf16[32,5120]{1,0:T(8,128)(2,1)S(1)}, bf16[32,5120]{1,0:T(8,128)(2,1)S(1)}, u32[]{:S(2)}, u32[]{:S(2)}) collective-permute-start(bf16[32,5120]{1,0:T(8,128)(2,1)S(1)} %get-tuple-element.82), channel_id=1, source_target_pairs={{0,4},{1,5},{2,6},{3,7},{4,0},{5,1},{6,2},{7,3},{8,12},{9,13},{10,... | collective-permute-start | bytes 983048 | tf_op jit(solution)/shard_map/rs12/ppermute | solution.py:280
  53.7 16.2 %collective-permute-start.7 = (bf16[16,4096]{1,0:T(8,128)(2,1)S(1)}, bf16[16,4096]{1,0:T(8,128)(2,1)S(1)}, u32[]{:S(2)}, u32[]{:S(2)}) collective-permute-start(bf16[16,4096]{1,0:T(8,128)(2,1)S(1)} %add_convert_fusion.20), channel_id=1, source_target_pairs={{0,2},{1,3},{2,0},{3,1},{4,6},{5,7},{6,4},{7,5},{8,10},{9,11},{10,... | collective-permute-start | bytes 393224 | tf_op jit(solution)/shard_map/rs03/ppermute | solution.py:280
  56.2 11.1 %collective-permute-start.9 = (bf16[32,4096]{1,0:T(8,128)(2,1)S(1)}, bf16[32,4096]{1,0:T(8,128)(2,1)S(1)}, u32[]{:S(2)}, u32[]{:S(2)}) collective-permute-start(bf16[32,4096]{1,0:T(8,128)(2,1)S(1)} %get-tuple-element.87), channel_id=1, source_target_pairs={{0,4},{1,5},{2,6},{3,7},{4,0},{5,1},{6,2},{7,3},{8,12},{9,13},{10,... | collective-permute-start | bytes 786440 | tf_op jit(solution)/shard_map/rs22/ppermute | solution.py:280
  57.9 8.3 %collective-permute-start.11 = (bf16[16,5120]{1,0:T(8,128)(2,1)S(1)}, bf16[16,5120]{1,0:T(8,128)(2,1)S(1)}, u32[]{:S(2)}, u32[]{:S(2)}) collective-permute-start(bf16[16,5120]{1,0:T(8,128)(2,1)S(1)} %add_convert_fusion.16), channel_id=1, source_target_pairs={{0,8},{1,9},{2,10},{3,11},{4,12},{5,13},{6,14},{7,15},{8,0},{9,1},... | collective-permute-start | bytes 491528 | tf_op jit(solution)/shard_map/rs13/ppermute | solution.py:280
  64.6 9.6 %collective-permute-start.14 = (bf16[32,3072]{1,0:T(8,128)(2,1)S(1)}, bf16[32,3072]{1,0:T(8,128)(2,1)S(1)}, u32[]{:S(2)}, u32[]{:S(2)}) collective-permute-start(bf16[32,3072]{1,0:T(8,128)(2,1)S(1)} %get-tuple-element.92), channel_id=1, source_target_pairs={{0,4},{1,5},{2,6},{3,7},{4,0},{5,1},{6,2},{7,3},{8,12},{9,13},{10,... | collective-permute-start | bytes 589832 | tf_op jit(solution)/shard_map/rs32/ppermute | solution.py:280
  83.3 11.8 %collective-permute-start.21 = (bf16[1,1,1,16,4096]{4,3,2,1,0:T(8,128)(2,1)S(1)}, bf16[1,1,1,16,4096]{4,3,2,1,0:T(8,128)(2,1)S(1)}, u32[]{:S(2)}, u32[]{:S(2)}) collective-permute-start(bf16[1,1,1,16,4096]{4,3,2,1,0:T(8,128)(2,1)S(1)} %get-tuple-element.106), channel_id=1, source_target_pairs={{0,8},{1,9},{2,10},{3,11},{4,12},{5,13},{6,14},{7,15},{8,0},{9,1},... | collective-permute-start | bytes 393224 | tf_op jit(solution)/shard_map/ag13/ppermute | solution.py:280
  95.2 9.6 %collective-permute-start.22 = (bf16[1,2,1,16,4096]{4,3,2,1,0:T(8,128)(2,1)S(1)}, bf16[1,2,1,16,4096]{4,3,2,1,0:T(8,128)(2,1)S(1)}, u32[]{:S(2)}, u32[]{:S(2)}) collective-permute-start(bf16[1,2,1,16,4096]{4,3,2,1,0:T(8,128)(2,1)S(1)} %pad_maximum_fusion.7), channel_id=1, source_target_pairs={{0,4},{1,5},{2,6},{3,7},{4,0},{5,1},{6,2},{7,3},{8,12},{9,13},{10,... | collective-permute-start | bytes 786440 | tf_op jit(solution)/shard_map/ag12/ppermute | solution.py:280
  95.4 9.6 %collective-permute-start.16 = (bf16[1,1,1,16,6144]{4,3,2,1,0:T(8,128)(2,1)S(1)}, bf16[1,1,1,16,6144]{4,3,2,1,0:T(8,128)(2,1)S(1)}, u32[]{:S(2)}, u32[]{:S(2)}) collective-permute-start(bf16[1,1,1,16,6144]{4,3,2,1,0:T(8,128)(2,1)S(1)} %slice_bitcast_fusion), channel_id=1, source_target_pairs={{0,8},{1,9},{2,10},{3,11},{4,12},{5,13},{6,14},{7,15},{8,0},{9,1},... | collective-permute-start | bytes 589832 | tf_op jit(solution)/shard_map/ag33/ppermute | solution.py:280
  97.5 7.4 %collective-permute-start.20 = (bf16[1,2,2,16,2048]{4,3,2,1,0:T(8,128)(2,1)S(1)}, bf16[1,2,2,16,2048]{4,3,2,1,0:T(8,128)(2,1)S(1)}, u32[]{:S(2)}, u32[]{:S(2)}) collective-permute-start(bf16[1,2,2,16,2048]{4,3,2,1,0:T(8,128)(2,1)S(1)} %pad_maximum_fusion.6), channel_id=1, source_target_pairs={{0,2},{1,3},{2,0},{3,1},{4,6},{5,7},{6,4},{7,5},{8,10},{9,11},{10,... | collective-permute-start | bytes 786440 | tf_op jit(solution)/shard_map/ag01/ppermute | solution.py:280
  105.0 12.8 %collective-permute-start.23 = (bf16[1,2,1,16,6144]{4,3,2,1,0:T(8,128)(2,1)S(1)}, bf16[1,2,1,16,6144]{4,3,2,1,0:T(8,128)(2,1)S(1)}, u32[]{:S(2)}, u32[]{:S(2)}) collective-permute-start(bf16[1,2,1,16,6144]{4,3,2,1,0:T(8,128)(2,1)S(1)} %pad_maximum_fusion.4), channel_id=1, source_target_pairs={{0,4},{1,5},{2,6},{3,7},{4,0},{5,1},{6,2},{7,3},{8,12},{9,13},{10,... | collective-permute-start | bytes 1179656 | tf_op jit(solution)/shard_map/ag32/ppermute | solution.py:280
  106.6 11.4 %collective-permute-start.25 = (bf16[2,1,1,16,4096]{4,3,2,1,0:T(8,128)(2,1)S(1)}, bf16[2,1,1,16,4096]{4,3,2,1,0:T(8,128)(2,1)S(1)}, u32[]{:S(2)}, u32[]{:S(2)}) collective-permute-start(bf16[2,1,1,16,4096]{4,3,2,1,0:T(8,128)(2,1)S(1)} %pad_maximum_fusion.5), channel_id=1, source_target_pairs={{0,8},{1,9},{2,10},{3,11},{4,12},{5,13},{6,14},{7,15},{8,0},{9,1},... | collective-permute-start | bytes 786440 | tf_op jit(solution)/shard_map/ag22/ppermute | solution.py:280
  111.2 16.8 %collective-permute-start.27 = (bf16[1,2,2,16,4096]{4,3,2,1,0:T(8,128)(2,1)S(1)}, bf16[1,2,2,16,4096]{4,3,2,1,0:T(8,128)(2,1)S(1)}, u32[]{:S(2)}, u32[]{:S(2)}) collective-permute-start(bf16[1,2,2,16,4096]{4,3,2,1,0:T(8,128)(2,1)S(1)} %pad_maximum_fusion.2), channel_id=1, source_target_pairs={{0,2},{1,3},{2,0},{3,1},{4,6},{5,7},{6,4},{7,5},{8,10},{9,11},{10,... | collective-permute-start | bytes 1572872 | tf_op jit(solution)/shard_map/ag11/ppermute | solution.py:280
  118.1 13.0 %collective-permute-start.26 = (bf16[2,2,1,16,4096]{4,3,2,1,0:T(8,128)(2,1)S(1)}, bf16[2,2,1,16,4096]{4,3,2,1,0:T(8,128)(2,1)S(1)}, u32[]{:S(2)}, u32[]{:S(2)}) collective-permute-start(bf16[2,2,1,16,4096]{4,3,2,1,0:T(8,128)(2,1)S(1)} %pad_maximum_fusion.3), channel_id=1, source_target_pairs={{0,4},{1,5},{2,6},{3,7},{4,0},{5,1},{6,2},{7,3},{8,12},{9,13},{10,... | collective-permute-start | bytes 1572872 | tf_op jit(solution)/shard_map/ag21/ppermute | solution.py:280
  123.9 14.0 %collective-permute-start.24 = (bf16[1,2,2,16,6144]{4,3,2,1,0:T(8,128)(2,1)S(1)}, bf16[1,2,2,16,6144]{4,3,2,1,0:T(8,128)(2,1)S(1)}, u32[]{:S(2)}, u32[]{:S(2)}) collective-permute-start(bf16[1,2,2,16,6144]{4,3,2,1,0:T(8,128)(2,1)S(1)} %pad_maximum_fusion.1), channel_id=1, source_target_pairs={{0,2},{1,3},{2,0},{3,1},{4,6},{5,7},{6,4},{7,5},{8,10},{9,11},{10,... | collective-permute-start | bytes 2359304 | tf_op jit(solution)/shard_map/ag31/ppermute | solution.py:280
  131.2 10.5 %collective-permute-start.33 = (bf16[2,4,16,4096]{3,2,1,0:T(8,128)(2,1)S(1)}, bf16[2,4,16,4096]{3,2,1,0:T(8,128)(2,1)S(1)}, u32[]{:S(2)}, u32[]{:S(2)}) collective-permute-start(bf16[2,4,16,4096]{3,2,1,0:T(8,128)(2,1)S(1)} %bitcast.38), channel_id=1, source_target_pairs={{0,1},{1,0},{2,3},{3,2},{4,5},{5,4},{6,7},{7,6},{8,9},{9,8},{10,11... | collective-permute-start | bytes 3145736 | tf_op jit(solution)/shard_map/ag21/ppermute | solution.py:280
  131.9 9.8 %collective-permute-start.34 = (bf16[4,16,6144]{2,1,0:T(8,128)(2,1)S(1)}, bf16[4,16,6144]{2,1,0:T(8,128)(2,1)S(1)}, u32[]{:S(2)}, u32[]{:S(2)}) collective-permute-start(bf16[4,16,6144]{2,1,0:T(8,128)(2,1)S(1)} %bitcast.40), channel_id=1, source_target_pairs={{0,1},{1,0},{2,3},{3,2},{4,5},{5,4},{6,7},{7,6},{8,9},{9,8},{10,11... | collective-permute-start | bytes 2359304 | tf_op jit(solution)/shard_map/ag31/ppermute | solution.py:280
  137.9 7.3 %collective-permute-start.28 = (bf16[4,16,6144]{2,1,0:T(8,128)(2,1)S(1)}, bf16[4,16,6144]{2,1,0:T(8,128)(2,1)S(1)}, u32[]{:S(2)}, u32[]{:S(2)}) collective-permute-start(bf16[4,16,6144]{2,1,0:T(8,128)(2,1)S(1)} %bitcast.46), channel_id=1, source_target_pairs={{0,1},{1,0},{2,3},{3,2},{4,5},{5,4},{6,7},{7,6},{8,9},{9,8},{10,11... | collective-permute-start | bytes 2359304 | tf_op jit(solution)/shard_map/ag31/ppermute | solution.py:280
  (17 other events, 84.2 us)

commit v6 on v5

--- a/solution.py
+++ b/solution.py
@@ -311,7 +311,8 @@
     wide = stream.astype(jnp.float32)
     inverse = lax.rsqrt(jnp.mean(wide * wide, axis=1, keepdims=True) + 1e-05)
     exps = lax.dynamic_slice_in_dim(code_exp, me * block, block, 0)
-    cap = (powers(exps) * CODE_TOP)[:, :, None]
+    cap = jnp.broadcast_to((powers(exps) * CODE_TOP)[:, :, None], (block, blocks, group))
+    cap = lax.optimization_barrier(cap)
     normed = (wide * inverse * gain[None, :]).reshape(block, blocks, group)
     mixed = jnp.clip(normed, -cap, cap).reshape(block, width).astype(jnp.bfloat16)
 

time: 148 us -> 149 us (level)
  no operation moved by 1% of the time
where the time goes in v6:
time: 149 us; the launch traced here: 147 us
  waiting for transfers between devices  61 us (41%)
  starting transfers between devices  53.4 us (36%)
  Pallas kernels  22.8 us (15%)
  other arithmetic  6.42 us (4%)
  between operations  1.82 us (1%)
    ppermute x35, waiting for transfers between devices, flip(): return lax.ppermute(x, 'tp', [(i, i ^ 1 << b) for i in range(parts)])  61 us
    ppermute x35, starting transfers between devices, flip(): return lax.ppermute(x, 'tp', [(i, i ^ 1 << b) for i in range(parts)])  53.4 us
    pallas_call x1, Pallas kernels, partials(): pl.pallas_call(functools.partial(partial_kernel, key_block=key_block, hea...  18 us
    pallas_call x2, Pallas kernels, put(): pl.pallas_call(functools.partial(put_kernel, places=places), in_specs=[an...  4.82 us
  transfers between devices with their start and end apart: 35, of which 20 were waited for; matrix products, arithmetic and copies ran while one was open for 4% of the time, Pallas kernels for 2%

profile of v6, /device:TPU:0, one launch (start us, length us, event | category | flops | bytes accessed | tf_op | source)
XLA Modules:
  0.0 146.5 jit_solution(13697589400664894638)
XLA Ops:
  1.3 18.0 %partials.1 = (bf16[128,4096]{1,0:T(8,128)(2,1)}, bf16[128,4096]{1,0:T(8,128)(2,1)}, bf16[128,5120]{1,0:T(8,128)(2,1)}, bf16[128,5120]{1,0:T(8,128)(2,1)}, bf16[...) custom-call(s32[1]{0:T(128)S(6)} %copy.16.start_ref, ...), custom_call_target="tpu_custom_call" | custom-call | tf_op jit(solution)/shard_map/partials/pallas_call | solution.py:157
  23.8 3.0 %collective-permute-start.1 = (bf16[64,4096]{1,0:T(8,128)(2,1)S(1)}, bf16[64,4096]{1,0:T(8,128)(2,1)S(1)}, u32[]{:S(2)}, u32[]{:S(2)}) collective-permute-start(bf16[64,4096]{1,0:T(8,128)(2,1)S(1)} %get-tuple-element.77), channel_id=1, source_target_pairs={{0,4},{1,5},{2,6},{3,7},{4,0},{5,1},{6,2},{7,3},{8,12},{9,13},{10,... | collective-permute-start | bytes 1572872 | tf_op jit(solution)/shard_map/rs01/ppermute | solution.py:280
  32.5 6.5 %collective-permute-done.1 = bf16[64,4096]{1,0:T(8,128)(2,1)S(1)} collective-permute-done((bf16[64,4096]{1,0:T(8,128)(2,1)S(1)}, bf16[64,4096]{1,0:T(8,128)(2,1)S(1)}, u32[]{:S(2)}, u32[]{:S(2)}) %collective-permute-start.1) | collective-permute-done | bytes 524320 | tf_op jit(solution)/shard_map/rs01/ppermute | solution.py:280
  39.2 2.8 %collective-permute-start.5 = (bf16[32,4096]{1,0:T(8,128)(2,1)S(1)}, bf16[32,4096]{1,0:T(8,128)(2,1)S(1)}, u32[]{:S(2)}, u32[]{:S(2)}) collective-permute-start(bf16[32,4096]{1,0:T(8,128)(2,1)S(1)} %get-tuple-element.87), channel_id=1, source_target_pairs={{0,8},{1,9},{2,10},{3,11},{4,12},{5,13},{6,14},{7,15},{8,0},{9,1},... | collective-permute-start | bytes 786440 | tf_op jit(solution)/shard_map/rs02/ppermute | solution.py:280
  42.0 2.9 %collective-permute-done.6 = bf16[64,5120]{1,0:T(8,128)(2,1)S(1)} collective-permute-done((bf16[64,5120]{1,0:T(8,128)(2,1)S(1)}, bf16[64,5120]{1,0:T(8,128)(2,1)S(1)}, u32[]{:S(2)}, u32[]{:S(2)}) %collective-permute-start.6) | collective-permute-done | bytes 655392 | tf_op jit(solution)/shard_map/rs11/ppermute | solution.py:280
  46.4 7.3 %collective-permute-done.5 = bf16[32,4096]{1,0:T(8,128)(2,1)S(1)} collective-permute-done((bf16[32,4096]{1,0:T(8,128)(2,1)S(1)}, bf16[32,4096]{1,0:T(8,128)(2,1)S(1)}, u32[]{:S(2)}, u32[]{:S(2)}) %collective-permute-start.5) | collective-permute-done | bytes 262176 | tf_op jit(solution)/shard_map/rs02/ppermute | solution.py:280
  57.9 3.2 %collective-permute-start.11 = (bf16[16,5120]{1,0:T(8,128)(2,1)S(1)}, bf16[16,5120]{1,0:T(8,128)(2,1)S(1)}, u32[]{:S(2)}, u32[]{:S(2)}) collective-permute-start(bf16[16,5120]{1,0:T(8,128)(2,1)S(1)} %add_convert_fusion.16), channel_id=1, source_target_pairs={{0,8},{1,9},{2,10},{3,11},{4,12},{5,13},{6,14},{7,15},{8,0},{9,1},... | collective-permute-start | bytes 491528 | tf_op jit(solution)/shard_map/rs13/ppermute | solution.py:280
  61.2 3.4 %collective-permute-done.12 = bf16[64,3072]{1,0:T(8,128)(2,1)S(1)} collective-permute-done((bf16[64,3072]{1,0:T(8,128)(2,1)S(1)}, bf16[64,3072]{1,0:T(8,128)(2,1)S(1)}, u32[]{:S(2)}, u32[]{:S(2)}) %collective-permute-start.12) | collective-permute-done | bytes 393248 | tf_op jit(solution)/shard_map/rs31/ppermute | solution.py:280
  67.3 2.6 %collective-permute-start.13 = (bf16[16,4096]{1,0:T(8,128)(2,1)S(1)}, bf16[16,4096]{1,0:T(8,128)(2,1)S(1)}, u32[]{:S(2)}, u32[]{:S(2)}) collective-permute-start(bf16[16,4096]{1,0:T(8,128)(2,1)S(1)} %add_convert_fusion.19), channel_id=1, source_target_pairs={{0,8},{1,9},{2,10},{3,11},{4,12},{5,13},{6,14},{7,15},{8,0},{9,1},... | collective-permute-start | bytes 393224 | tf_op jit(solution)/shard_map/rs23/ppermute | solution.py:280
  70.1 4.2 %collective-permute-done.13 = bf16[16,4096]{1,0:T(8,128)(2,1)S(1)} collective-permute-done((bf16[16,4096]{1,0:T(8,128)(2,1)S(1)}, bf16[16,4096]{1,0:T(8,128)(2,1)S(1)}, u32[]{:S(2)}, u32[]{:S(2)}) %collective-permute-start.13) | collective-permute-done | bytes 131104 | tf_op jit(solution)/shard_map/rs23/ppermute | solution.py:280
  77.1 2.8 %collective-permute-done.15 = bf16[16,3072]{1,0:T(8,128)(2,1)S(1)} collective-permute-done((bf16[16,3072]{1,0:T(8,128)(2,1)S(1)}, bf16[16,3072]{1,0:T(8,128)(2,1)S(1)}, u32[]{:S(2)}, u32[]{:S(2)}) %collective-permute-start.15) | collective-permute-done | bytes 98336 | tf_op jit(solution)/shard_map/rs33/ppermute | solution.py:280
  85.6 2.7 %collective-permute-done.17 = bf16[1,1,1,16,2048]{4,3,2,1,0:T(8,128)(2,1)S(1)} collective-permute-done((bf16[1,1,1,16,2048]{4,3,2,1,0:T(8,128)(2,1)S(1)}, bf16[1,1,1,16,2048]{4,3,2,1,0:T(8,128)(2,1)S(1)}, u32[]{:S(2)}, u32[]{:S(2)}) %collective-permute-start.17) | collective-permute-done | bytes 65568 | tf_op jit(solution)/shard_map/ag03/ppermute | solution.py:280
  89.5 5.4 %collective-permute-done.18 = bf16[1,2,1,16,2048]{4,3,2,1,0:T(8,128)(2,1)S(1)} collective-permute-done((bf16[1,2,1,16,2048]{4,3,2,1,0:T(8,128)(2,1)S(1)}, bf16[1,2,1,16,2048]{4,3,2,1,0:T(8,128)(2,1)S(1)}, u32[]{:S(2)}, u32[]{:S(2)}) %collective-permute-start.18) | collective-permute-done | bytes 131104 | tf_op jit(solution)/shard_map/ag02/ppermute | solution.py:280
  97.2 2.4 %collective-permute-start.20 = (bf16[1,2,2,16,2048]{4,3,2,1,0:T(8,128)(2,1)S(1)}, bf16[1,2,2,16,2048]{4,3,2,1,0:T(8,128)(2,1)S(1)}, u32[]{:S(2)}, u32[]{:S(2)}) collective-permute-start(bf16[1,2,2,16,2048]{4,3,2,1,0:T(8,128)(2,1)S(1)} %pad_maximum_fusion.6), channel_id=1, source_target_pairs={{0,2},{1,3},{2,0},{3,1},{4,6},{5,7},{6,4},{7,5},{8,10},{9,11},{10,... | collective-permute-start | bytes 786440 | tf_op jit(solution)/shard_map/ag01/ppermute | solution.py:280
  99.6 5.0 %collective-permute-done.22 = bf16[1,2,1,16,4096]{4,3,2,1,0:T(8,128)(2,1)S(1)} collective-permute-done((bf16[1,2,1,16,4096]{4,3,2,1,0:T(8,128)(2,1)S(1)}, bf16[1,2,1,16,4096]{4,3,2,1,0:T(8,128)(2,1)S(1)}, u32[]{:S(2)}, u32[]{:S(2)}) %collective-permute-start.22) | collective-permute-done | bytes 262176 | tf_op jit(solution)/shard_map/ag12/ppermute | solution.py:280
  106.4 4.6 %collective-permute-start.25 = (bf16[2,1,1,16,4096]{4,3,2,1,0:T(8,128)(2,1)S(1)}, bf16[2,1,1,16,4096]{4,3,2,1,0:T(8,128)(2,1)S(1)}, u32[]{:S(2)}, u32[]{:S(2)}) collective-permute-start(bf16[2,1,1,16,4096]{4,3,2,1,0:T(8,128)(2,1)S(1)} %pad_maximum_fusion.5), channel_id=1, source_target_pairs={{0,8},{1,9},{2,10},{3,11},{4,12},{5,13},{6,14},{7,15},{8,0},{9,1},... | collective-permute-start | bytes 786440 | tf_op jit(solution)/shard_map/ag22/ppermute | solution.py:280
  111.0 2.7 %collective-permute-start.27 = (bf16[1,2,2,16,4096]{4,3,2,1,0:T(8,128)(2,1)S(1)}, bf16[1,2,2,16,4096]{4,3,2,1,0:T(8,128)(2,1)S(1)}, u32[]{:S(2)}, u32[]{:S(2)}) collective-permute-start(bf16[1,2,2,16,4096]{4,3,2,1,0:T(8,128)(2,1)S(1)} %pad_maximum_fusion.2), channel_id=1, source_target_pairs={{0,2},{1,3},{2,0},{3,1},{4,6},{5,7},{6,4},{7,5},{8,10},{9,11},{10,... | collective-permute-start | bytes 1572872 | tf_op jit(solution)/shard_map/ag11/ppermute | solution.py:280
  113.7 3.9 %collective-permute-done.23 = bf16[1,2,1,16,6144]{4,3,2,1,0:T(8,128)(2,1)S(1)} collective-permute-done((bf16[1,2,1,16,6144]{4,3,2,1,0:T(8,128)(2,1)S(1)}, bf16[1,2,1,16,6144]{4,3,2,1,0:T(8,128)(2,1)S(1)}, u32[]{:S(2)}, u32[]{:S(2)}) %collective-permute-start.23) | collective-permute-done | bytes 393248 | tf_op jit(solution)/shard_map/ag32/ppermute | solution.py:280
  117.9 5.8 %collective-permute-start.26 = (bf16[2,2,1,16,4096]{4,3,2,1,0:T(8,128)(2,1)S(1)}, bf16[2,2,1,16,4096]{4,3,2,1,0:T(8,128)(2,1)S(1)}, u32[]{:S(2)}, u32[]{:S(2)}) collective-permute-start(bf16[2,2,1,16,4096]{4,3,2,1,0:T(8,128)(2,1)S(1)} %pad_maximum_fusion.3), channel_id=1, source_target_pairs={{0,4},{1,5},{2,6},{3,7},{4,0},{5,1},{6,2},{7,3},{8,12},{9,13},{10,... | collective-permute-start | bytes 1572872 | tf_op jit(solution)/shard_map/ag21/ppermute | solution.py:280
  123.7 4.1 %collective-permute-start.24 = (bf16[1,2,2,16,6144]{4,3,2,1,0:T(8,128)(2,1)S(1)}, bf16[1,2,2,16,6144]{4,3,2,1,0:T(8,128)(2,1)S(1)}, u32[]{:S(2)}, u32[]{:S(2)}) collective-permute-start(bf16[1,2,2,16,6144]{4,3,2,1,0:T(8,128)(2,1)S(1)} %pad_maximum_fusion.1), channel_id=1, source_target_pairs={{0,2},{1,3},{2,0},{3,1},{4,6},{5,7},{6,4},{7,5},{8,10},{9,11},{10,... | collective-permute-start | bytes 2359304 | tf_op jit(solution)/shard_map/ag31/ppermute | solution.py:280
  127.7 3.1 %collective-permute-done.26 = bf16[2,2,1,16,4096]{4,3,2,1,0:T(8,128)(2,1)S(1)} collective-permute-done((bf16[2,2,1,16,4096]{4,3,2,1,0:T(8,128)(2,1)S(1)}, bf16[2,2,1,16,4096]{4,3,2,1,0:T(8,128)(2,1)S(1)}, u32[]{:S(2)}, u32[]{:S(2)}) %collective-permute-start.26) | collective-permute-done | bytes 524320 | tf_op jit(solution)/shard_map/ag21/ppermute | solution.py:280
  132.1 5.6 %collective-permute-done.24 = bf16[1,2,2,16,6144]{4,3,2,1,0:T(8,128)(2,1)S(1)} collective-permute-done((bf16[1,2,2,16,6144]{4,3,2,1,0:T(8,128)(2,1)S(1)}, bf16[1,2,2,16,6144]{4,3,2,1,0:T(8,128)(2,1)S(1)}, u32[]{:S(2)}, u32[]{:S(2)}) %collective-permute-start.24) | collective-permute-done | bytes 786464 | tf_op jit(solution)/shard_map/ag31/ppermute | solution.py:280
  138.3 2.4 %collective-permute-done.31.refs_5_ = bf16[4,16,4096]{2,1,0:T(8,128)(2,1)S(1)} collective-permute-done((bf16[4,16,4096]{2,1,0:T(8,128)(2,1)S(1)}, bf16[4,16,4096]{2,1,0:T(8,128)(2,1)S(1)}, u32[]{:S(2)}, u32[]{:S(2)}) %collective-permute-start.31) | collective-permute-done | bytes 524320 | tf_op jit(solution)/shard_map/ag11/ppermute | solution.py:280
  141.5 3.5 %put.2.refs_2_ = bf16[4,2,2,16,16384]{4,3,2,1,0:T(8,128)(2,1)} custom-call(bf16[4,16,2048]{2,1,0:T(8,128)(2,1)S(1)} %bitcast.51, bf16[4,16,2048]{2,1,0:T(8,128)(2,1)S(1)} %collective-permute-done.29.refs_1_, bf16[4,16,2048]{2,1,0:T(8,128)(2,1)S(1)} %bitcast.57, bf16[4,16,2048]{2,1,0:T(8,128)(2,1)S(1)} %collective-permute-done.30.refs_3_, ...), custom_call_target="tpu_custom_call" | custom-call | bytes 13631488 | tf_op jit(solution)/shard_map/put/pallas_call | solution.py:228
  (106 shorter events, 36.7 us)
Async XLA Ops:
  19.9 10.1 %collective-permute-start.2 = (bf16[128,3072]{1,0:T(8,128)(2,1)}, bf16[128,3072]{1,0:T(8,128)(2,1)}, u32[]{:S(2)}, u32[]{:S(2)}) collective-permute-start(bf16[128,3072]{1,0:T(8,128)(2,1)} %get-tuple-element.39), channel_id=1, source_target_pairs={{0,1},{1,0},{2,3},{3,2},{4,5},{5,4},{6,7},{7,6},{8,9},{9,8},{10,11... | collective-permute-start | bytes 2359304 | tf_op jit(solution)/shard_map/rs30/ppermute | solution.py:280
  20.3 8.5 %collective-permute-start.3 = (bf16[128,4096]{1,0:T(8,128)(2,1)}, bf16[128,4096]{1,0:T(8,128)(2,1)S(1)}, u32[]{:S(2)}, u32[]{:S(2)}) collective-permute-start(bf16[128,4096]{1,0:T(8,128)(2,1)} %get-tuple-element.41), channel_id=1, source_target_pairs={{0,1},{1,0},{2,3},{3,2},{4,5},{5,4},{6,7},{7,6},{8,9},{9,8},{10,11... | collective-permute-start | bytes 3145736 | tf_op jit(solution)/shard_map/rs20/ppermute | solution.py:280
  23.8 15.2 %collective-permute-start.1 = (bf16[64,4096]{1,0:T(8,128)(2,1)S(1)}, bf16[64,4096]{1,0:T(8,128)(2,1)S(1)}, u32[]{:S(2)}, u32[]{:S(2)}) collective-permute-start(bf16[64,4096]{1,0:T(8,128)(2,1)S(1)} %get-tuple-element.77), channel_id=1, source_target_pairs={{0,4},{1,5},{2,6},{3,7},{4,0},{5,1},{6,2},{7,3},{8,12},{9,13},{10,... | collective-permute-start | bytes 1572872 | tf_op jit(solution)/shard_map/rs01/ppermute | solution.py:280
  27.2 17.7 %collective-permute-start.6 = (bf16[64,5120]{1,0:T(8,128)(2,1)S(1)}, bf16[64,5120]{1,0:T(8,128)(2,1)S(1)}, u32[]{:S(2)}, u32[]{:S(2)}) collective-permute-start(bf16[64,5120]{1,0:T(8,128)(2,1)S(1)} %get-tuple-element.73), channel_id=1, source_target_pairs={{0,2},{1,3},{2,0},{3,1},{4,6},{5,7},{6,4},{7,5},{8,10},{9,11},{10,... | collective-permute-start | bytes 1966088 | tf_op jit(solution)/shard_map/rs11/ppermute | solution.py:280
  29.1 27.0 %collective-permute-start.8 = (bf16[64,4096]{1,0:T(8,128)(2,1)S(1)}, bf16[64,4096]{1,0:T(8,128)(2,1)S(1)}, u32[]{:S(2)}, u32[]{:S(2)}) collective-permute-start(bf16[64,4096]{1,0:T(8,128)(2,1)S(1)} %get-tuple-element.75), channel_id=1, source_target_pairs={{0,2},{1,3},{2,0},{3,1},{4,6},{5,7},{6,4},{7,5},{8,10},{9,11},{10,... | collective-permute-start | bytes 1572872 | tf_op jit(solution)/shard_map/rs21/ppermute | solution.py:280
  31.3 33.2 %collective-permute-start.12 = (bf16[64,3072]{1,0:T(8,128)(2,1)S(1)}, bf16[64,3072]{1,0:T(8,128)(2,1)S(1)}, u32[]{:S(2)}, u32[]{:S(2)}) collective-permute-start(bf16[64,3072]{1,0:T(8,128)(2,1)S(1)} %get-tuple-element.78), channel_id=1, source_target_pairs={{0,2},{1,3},{2,0},{3,1},{4,6},{5,7},{6,4},{7,5},{8,10},{9,11},{10,... | collective-permute-start | bytes 1179656 | tf_op jit(solution)/shard_map/rs31/ppermute | solution.py:280
  39.2 14.5 %collective-permute-start.5 = (bf16[32,4096]{1,0:T(8,128)(2,1)S(1)}, bf16[32,4096]{1,0:T(8,128)(2,1)S(1)}, u32[]{:S(2)}, u32[]{:S(2)}) collective-permute-start(bf16[32,4096]{1,0:T(8,128)(2,1)S(1)} %get-tuple-element.87), channel_id=1, source_target_pairs={{0,8},{1,9},{2,10},{3,11},{4,12},{5,13},{6,14},{7,15},{8,0},{9,1},... | collective-permute-start | bytes 786440 | tf_op jit(solution)/shard_map/rs02/ppermute | solution.py:280
  45.0 12.8 %collective-permute-start.10 = (bf16[32,5120]{1,0:T(8,128)(2,1)S(1)}, bf16[32,5120]{1,0:T(8,128)(2,1)S(1)}, u32[]{:S(2)}, u32[]{:S(2)}) collective-permute-start(bf16[32,5120]{1,0:T(8,128)(2,1)S(1)} %get-tuple-element.80), channel_id=1, source_target_pairs={{0,4},{1,5},{2,6},{3,7},{4,0},{5,1},{6,2},{7,3},{8,12},{9,13},{10,... | collective-permute-start | bytes 983048 | tf_op jit(solution)/shard_map/rs12/ppermute | solution.py:280
  53.8 16.2 %collective-permute-start.7 = (bf16[16,4096]{1,0:T(8,128)(2,1)S(1)}, bf16[16,4096]{1,0:T(8,128)(2,1)S(1)}, u32[]{:S(2)}, u32[]{:S(2)}) collective-permute-start(bf16[16,4096]{1,0:T(8,128)(2,1)S(1)} %add_convert_fusion.20), channel_id=1, source_target_pairs={{0,2},{1,3},{2,0},{3,1},{4,6},{5,7},{6,4},{7,5},{8,10},{9,11},{10,... | collective-permute-start | bytes 393224 | tf_op jit(solution)/shard_map/rs03/ppermute | solution.py:280
  56.2 11.1 %collective-permute-start.9 = (bf16[32,4096]{1,0:T(8,128)(2,1)S(1)}, bf16[32,4096]{1,0:T(8,128)(2,1)S(1)}, u32[]{:S(2)}, u32[]{:S(2)}) collective-permute-start(bf16[32,4096]{1,0:T(8,128)(2,1)S(1)} %get-tuple-element.85), channel_id=1, source_target_pairs={{0,4},{1,5},{2,6},{3,7},{4,0},{5,1},{6,2},{7,3},{8,12},{9,13},{10,... | collective-permute-start | bytes 786440 | tf_op jit(solution)/shard_map/rs22/ppermute | solution.py:280
  57.9 8.3 %collective-permute-start.11 = (bf16[16,5120]{1,0:T(8,128)(2,1)S(1)}, bf16[16,5120]{1,0:T(8,128)(2,1)S(1)}, u32[]{:S(2)}, u32[]{:S(2)}) collective-permute-start(bf16[16,5120]{1,0:T(8,128)(2,1)S(1)} %add_convert_fusion.16), channel_id=1, source_target_pairs={{0,8},{1,9},{2,10},{3,11},{4,12},{5,13},{6,14},{7,15},{8,0},{9,1},... | collective-permute-start | bytes 491528 | tf_op jit(solution)/shard_map/rs13/ppermute | solution.py:280
  64.6 9.6 %collective-permute-start.14 = (bf16[32,3072]{1,0:T(8,128)(2,1)S(1)}, bf16[32,3072]{1,0:T(8,128)(2,1)S(1)}, u32[]{:S(2)}, u32[]{:S(2)}) collective-permute-start(bf16[32,3072]{1,0:T(8,128)(2,1)S(1)} %get-tuple-element.90), channel_id=1, source_target_pairs={{0,4},{1,5},{2,6},{3,7},{4,0},{5,1},{6,2},{7,3},{8,12},{9,13},{10,... | collective-permute-start | bytes 589832 | tf_op jit(solution)/shard_map/rs32/ppermute | solution.py:280
  83.1 11.8 %collective-permute-start.21 = (bf16[1,1,1,16,4096]{4,3,2,1,0:T(8,128)(2,1)S(1)}, bf16[1,1,1,16,4096]{4,3,2,1,0:T(8,128)(2,1)S(1)}, u32[]{:S(2)}, u32[]{:S(2)}) collective-permute-start(bf16[1,1,1,16,4096]{4,3,2,1,0:T(8,128)(2,1)S(1)} %get-tuple-element.104), channel_id=1, source_target_pairs={{0,8},{1,9},{2,10},{3,11},{4,12},{5,13},{6,14},{7,15},{8,0},{9,1},... | collective-permute-start | bytes 393224 | tf_op jit(solution)/shard_map/ag13/ppermute | solution.py:280
  95.0 9.6 %collective-permute-start.22 = (bf16[1,2,1,16,4096]{4,3,2,1,0:T(8,128)(2,1)S(1)}, bf16[1,2,1,16,4096]{4,3,2,1,0:T(8,128)(2,1)S(1)}, u32[]{:S(2)}, u32[]{:S(2)}) collective-permute-start(bf16[1,2,1,16,4096]{4,3,2,1,0:T(8,128)(2,1)S(1)} %pad_maximum_fusion.7), channel_id=1, source_target_pairs={{0,4},{1,5},{2,6},{3,7},{4,0},{5,1},{6,2},{7,3},{8,12},{9,13},{10,... | collective-permute-start | bytes 786440 | tf_op jit(solution)/shard_map/ag12/ppermute | solution.py:280
  95.1 9.6 %collective-permute-start.16 = (bf16[1,1,1,16,6144]{4,3,2,1,0:T(8,128)(2,1)S(1)}, bf16[1,1,1,16,6144]{4,3,2,1,0:T(8,128)(2,1)S(1)}, u32[]{:S(2)}, u32[]{:S(2)}) collective-permute-start(bf16[1,1,1,16,6144]{4,3,2,1,0:T(8,128)(2,1)S(1)} %slice_bitcast_fusion), channel_id=1, source_target_pairs={{0,8},{1,9},{2,10},{3,11},{4,12},{5,13},{6,14},{7,15},{8,0},{9,1},... | collective-permute-start | bytes 589832 | tf_op jit(solution)/shard_map/ag33/ppermute | solution.py:280
  97.2 7.5 %collective-permute-start.20 = (bf16[1,2,2,16,2048]{4,3,2,1,0:T(8,128)(2,1)S(1)}, bf16[1,2,2,16,2048]{4,3,2,1,0:T(8,128)(2,1)S(1)}, u32[]{:S(2)}, u32[]{:S(2)}) collective-permute-start(bf16[1,2,2,16,2048]{4,3,2,1,0:T(8,128)(2,1)S(1)} %pad_maximum_fusion.6), channel_id=1, source_target_pairs={{0,2},{1,3},{2,0},{3,1},{4,6},{5,7},{6,4},{7,5},{8,10},{9,11},{10,... | collective-permute-start | bytes 786440 | tf_op jit(solution)/shard_map/ag01/ppermute | solution.py:280
  104.8 12.8 %collective-permute-start.23 = (bf16[1,2,1,16,6144]{4,3,2,1,0:T(8,128)(2,1)S(1)}, bf16[1,2,1,16,6144]{4,3,2,1,0:T(8,128)(2,1)S(1)}, u32[]{:S(2)}, u32[]{:S(2)}) collective-permute-start(bf16[1,2,1,16,6144]{4,3,2,1,0:T(8,128)(2,1)S(1)} %pad_maximum_fusion.4), channel_id=1, source_target_pairs={{0,4},{1,5},{2,6},{3,7},{4,0},{5,1},{6,2},{7,3},{8,12},{9,13},{10,... | collective-permute-start | bytes 1179656 | tf_op jit(solution)/shard_map/ag32/ppermute | solution.py:280
  106.4 11.4 %collective-permute-start.25 = (bf16[2,1,1,16,4096]{4,3,2,1,0:T(8,128)(2,1)S(1)}, bf16[2,1,1,16,4096]{4,3,2,1,0:T(8,128)(2,1)S(1)}, u32[]{:S(2)}, u32[]{:S(2)}) collective-permute-start(bf16[2,1,1,16,4096]{4,3,2,1,0:T(8,128)(2,1)S(1)} %pad_maximum_fusion.5), channel_id=1, source_target_pairs={{0,8},{1,9},{2,10},{3,11},{4,12},{5,13},{6,14},{7,15},{8,0},{9,1},... | collective-permute-start | bytes 786440 | tf_op jit(solution)/shard_map/ag22/ppermute | solution.py:280
  111.0 16.8 %collective-permute-start.27 = (bf16[1,2,2,16,4096]{4,3,2,1,0:T(8,128)(2,1)S(1)}, bf16[1,2,2,16,4096]{4,3,2,1,0:T(8,128)(2,1)S(1)}, u32[]{:S(2)}, u32[]{:S(2)}) collective-permute-start(bf16[1,2,2,16,4096]{4,3,2,1,0:T(8,128)(2,1)S(1)} %pad_maximum_fusion.2), channel_id=1, source_target_pairs={{0,2},{1,3},{2,0},{3,1},{4,6},{5,7},{6,4},{7,5},{8,10},{9,11},{10,... | collective-permute-start | bytes 1572872 | tf_op jit(solution)/shard_map/ag11/ppermute | solution.py:280
  117.9 13.0 %collective-permute-start.26 = (bf16[2,2,1,16,4096]{4,3,2,1,0:T(8,128)(2,1)S(1)}, bf16[2,2,1,16,4096]{4,3,2,1,0:T(8,128)(2,1)S(1)}, u32[]{:S(2)}, u32[]{:S(2)}) collective-permute-start(bf16[2,2,1,16,4096]{4,3,2,1,0:T(8,128)(2,1)S(1)} %pad_maximum_fusion.3), channel_id=1, source_target_pairs={{0,4},{1,5},{2,6},{3,7},{4,0},{5,1},{6,2},{7,3},{8,12},{9,13},{10,... | collective-permute-start | bytes 1572872 | tf_op jit(solution)/shard_map/ag21/ppermute | solution.py:280
  123.7 14.0 %collective-permute-start.24 = (bf16[1,2,2,16,6144]{4,3,2,1,0:T(8,128)(2,1)S(1)}, bf16[1,2,2,16,6144]{4,3,2,1,0:T(8,128)(2,1)S(1)}, u32[]{:S(2)}, u32[]{:S(2)}) collective-permute-start(bf16[1,2,2,16,6144]{4,3,2,1,0:T(8,128)(2,1)S(1)} %pad_maximum_fusion.1), channel_id=1, source_target_pairs={{0,2},{1,3},{2,0},{3,1},{4,6},{5,7},{6,4},{7,5},{8,10},{9,11},{10,... | collective-permute-start | bytes 2359304 | tf_op jit(solution)/shard_map/ag31/ppermute | solution.py:280
  131.0 10.5 %collective-permute-start.33 = (bf16[2,4,16,4096]{3,2,1,0:T(8,128)(2,1)S(1)}, bf16[2,4,16,4096]{3,2,1,0:T(8,128)(2,1)S(1)}, u32[]{:S(2)}, u32[]{:S(2)}) collective-permute-start(bf16[2,4,16,4096]{3,2,1,0:T(8,128)(2,1)S(1)} %bitcast.44), channel_id=1, source_target_pairs={{0,1},{1,0},{2,3},{3,2},{4,5},{5,4},{6,7},{7,6},{8,9},{9,8},{10,11... | collective-permute-start | bytes 3145736 | tf_op jit(solution)/shard_map/ag21/ppermute | solution.py:280
  131.7 9.8 %collective-permute-start.34 = (bf16[4,16,6144]{2,1,0:T(8,128)(2,1)S(1)}, bf16[4,16,6144]{2,1,0:T(8,128)(2,1)S(1)}, u32[]{:S(2)}, u32[]{:S(2)}) collective-permute-start(bf16[4,16,6144]{2,1,0:T(8,128)(2,1)S(1)} %bitcast.46), channel_id=1, source_target_pairs={{0,1},{1,0},{2,3},{3,2},{4,5},{5,4},{6,7},{7,6},{8,9},{9,8},{10,11... | collective-permute-start | bytes 2359304 | tf_op jit(solution)/shard_map/ag31/ppermute | solution.py:280
  137.7 7.3 %collective-permute-start.28 = (bf16[4,16,6144]{2,1,0:T(8,128)(2,1)S(1)}, bf16[4,16,6144]{2,1,0:T(8,128)(2,1)S(1)}, u32[]{:S(2)}, u32[]{:S(2)}) collective-permute-start(bf16[4,16,6144]{2,1,0:T(8,128)(2,1)S(1)} %bitcast.52), channel_id=1, source_target_pairs={{0,1},{1,0},{2,3},{3,2},{4,5},{5,4},{6,7},{7,6},{8,9},{9,8},{10,11... | collective-permute-start | bytes 2359304 | tf_op jit(solution)/shard_map/ag31/ppermute | solution.py:280
  (17 other events, 82.1 us)
